TPU v7x, 32 devices: a whole 2x2x4 slice. The times are simulated.
32 devices in a mesh: state: 8 (over y, x, core), obs: 4 (over z).
Axes of the slice: x: 2, y: 2, z: 4, core: 2. Of those that a mesh axis runs over, the one named last changes fastest.
Arguments:
- predictions: bfloat16 [16384, 1024], P(('state', 'obs')), may hold values from -6 to 6
- obs_index: int32 [16384], P(('state', 'obs')), may hold values from 0 to 16383, as said below
- data_values: float32 [16384], P(('state', 'obs')), may hold values from -6 to 6
- noise_var: float32 [16384], P(('state', 'obs')), may hold values from 16 to 256
- perturbations: bfloat16 [16384, 1024], P(('state', 'obs')), may hold values from -6 to 6
- unknowns: bfloat16 [65536, 1024], P(('state', 'obs')), may hold values from -6 to 6
Outputs:
- updated: bfloat16 [65536, 1024], P(('state', 'obs'))
- innovation_var: float32 [16384], P(('state', 'obs'))
Inputs may be any that keep to these rules, and one draw needn't show every extreme that they name: `obs_index`: every observation 0 to 16383 appears exactly once. Observation k belongs to device k // 512 of the joined state+obs axis. Of the 512 entries of one device, at most 32 belong to any one owner, and in every draw some device has exactly 32 entries for some owner.
All inputs are finite; a program needn't handle non-finite values.
Results may differ from a plain program's by a relative error of at most 0.007.
Values may be sent and summed in bfloat16 or wider, within the bound.
No kernel may reach another device: no remote copies, remote signals or barrier semaphores. Data moves between devices by JAX's collectives and lax.ppermute only.
A program may use at most 128 MiB of HBM per device.

v0:
```python
import jax
import jax.numpy as jnp
from jax import lax
from jax.sharding import PartitionSpec as P


def spread_of(unknowns):
    block_vals = unknowns.astype(jnp.float32)
    member_mean = jnp.mean(block_vals, axis=1, keepdims=True)
    return (block_vals - member_mean).astype(jnp.bfloat16)


def on_device(predictions, obs_index, data_values, noise_var, perturbations, unknowns):
    shards = lax.axis_size(("state", "obs"))
    row_count = predictions.shape[0]
    members = predictions.shape[1]
    capacity = 2 * row_count // shards
    owners = obs_index // row_count
    slot_ids = obs_index % row_count
    onehot = (owners[:, None] == jnp.arange(shards, dtype=jnp.int32)[None, :]).astype(jnp.int32)
    rank_rows = jnp.sum(jnp.cumsum(onehot, axis=0) * onehot, axis=1) - 1
    target = owners * capacity + rank_rows
    outgoing = jnp.zeros((shards * capacity, members), jnp.bfloat16).at[target].set(predictions)
    out_slots = jnp.full((shards * capacity,), row_count, jnp.int32).at[target].set(slot_ids)
    got_rows, got_slots = (
        lax.all_to_all(
            outgoing.reshape(shards, capacity, members),
            ("state", "obs"),
            split_axis=0,
            concat_axis=0,
            tiled=True,
        ),
        lax.all_to_all(
            out_slots.reshape(shards, capacity),
            ("state", "obs"),
            split_axis=0,
            concat_axis=0,
            tiled=True,
        ),
    )
    arranged = (
        jnp.zeros((row_count, members), jnp.bfloat16)
        .at[got_slots.reshape(-1)]
        .set(got_rows.reshape(-1, members), mode="drop")
    )
    spread = spread_of(unknowns)
    pred_vals = arranged.astype(jnp.float32)
    row_mean = jnp.mean(pred_vals, axis=1, keepdims=True)
    root_weight = jnp.sqrt(1.0 / noise_var)[:, None]
    anomalies = (root_weight * (pred_vals - row_mean)).astype(jnp.bfloat16)
    raw_innov = data_values[:, None] + perturbations.astype(jnp.float32) - pred_vals
    innovation_var = jnp.mean(raw_innov * raw_innov, axis=1)
    innovation = (root_weight * raw_innov).astype(jnp.bfloat16)
    gram_part = jnp.dot(anomalies.T, anomalies, preferred_element_type=jnp.float32)
    cross_part = jnp.dot(anomalies.T, innovation, preferred_element_type=jnp.float32)
    identity = (members - 1) * jnp.eye(members, dtype=jnp.float32)
    gram_total, cross_total = lax.psum((gram_part, cross_part), ("state", "obs"))
    factor = jnp.linalg.cholesky(gram_total + identity)
    gain_matrix = jax.scipy.linalg.cho_solve((factor, True), cross_total).astype(jnp.bfloat16)
    moved = jnp.dot(spread, gain_matrix, preferred_element_type=jnp.float32)
    updated = (unknowns.astype(jnp.float32) + moved).astype(jnp.bfloat16)
    return (updated, innovation_var)


def solution(mesh):
    return jax.shard_map(
        on_device,
        mesh=mesh,
        in_specs=(
            P(("state", "obs"), None),
            P(("state", "obs")),
            P(("state", "obs")),
            P(("state", "obs")),
            P(("state", "obs"), None),
            P(("state", "obs"), None),
        ),
        out_specs=(P(("state", "obs"), None), P(("state", "obs"))),
        check_vma=False,
    )
```

profile of v0, /device:TPU:0, one launch (start us, length us, event | category | flops | bytes accessed | tf_op | source)
XLA Modules:
  0.0 651.8 jit_solution(1755983513919163844)
XLA Ops:
  9.4 2.4 scatter_custom_fusion
  12.6 7.3 %all-to-all-start = ((s32[32,1,32]{2,1,0:T(1,128)}), s32[32,1,32]{2,1,0:T(1,128)S(1)}, u32[]{:S(2)}, u32[]{:S(2)}) async-start(s32[32,1,32]{2,1,0:T(1,128)} %all_to_all.9), calls=%async_computation | async-start | bytes 32768 | tf_op jit(solution)/shard_map/all_to_all | solution.py:33
  19.9 4.8 scatter_custom_fusion.1
  24.7 2.4 all-to-all-done
  27.0 3.5 all-to-all-start.1
  31.9 46.1 %all-to-all-done.1 = bf16[32,32,1024]{2,1,0:T(8,128)(2,1)S(1)} async-done(((bf16[32,32,1024]{2,1,0:T(8,128)(2,1)}), bf16[32,32,1024]{2,1,0:T(8,128)(2,1)S(1)}, u32[]{:S(2)}, u32[]{:S(2)}) %all-to-all-start.1) | async-done | bytes 2097184 | tf_op jit(solution)/shard_map/all_to_all | solution.py:26
  78.0 5.7 scatter_custom_fusion.2
  85.9 3.5 fusion.81
  89.4 3.6 fusion.51
  93.1 2.8 convert_reduce_fusion
  96.5 175.3 %all-reduce.4.cloned.1.call-done = (f32[1024,1024]{1,0:T(8,128)}, f32[1024,1024]{0,1:T(8,128)}) async-done(((f32[1024,1024]{1,0:T(8,128)}, f32[1024,1024]{0,1:T(8,128)}), (f32[1024,1024]{1,0:T(8,128)}, f32[1024,1024]{0,1:T(8,128)})) %all-reduce.4.cloned.1.call-update) | async-done | bytes 8388624 | tf_op jit(solution)/shard_map/psum | solution.py:57
  271.8 4.9 select_add_fusion
  276.7 5.7 copy.28
  282.4 4.5 fusion.4
  288.9 11.7 %cholesky.222 = f32[128,128]{1,0:T(8,128)S(1)} custom-call(f32[128,128]{1,0:T(8,128)S(1)} %cholesky.577), custom_call_target="Cholesky" | custom-call | tf_op jit(solution)/shard_map/jit(cholesky)/cholesky | solution.py:58
  300.6 9.8 %custom-call.66 = f32[1,128,128]{1,2,0:T(8,128)S(1)} custom-call(f32[1,128,128]{2,1,0:T(8,128)S(1)} %get-tuple-element.62), custom_call_target="InvertDiagBlocksLowerTriangular" | custom-call | tf_op jit(solution)/shard_map/jit(cholesky)/cholesky | solution.py:58
  313.5 11.7 %cholesky.243 = f32[128,128]{1,0:T(8,128)S(1)} custom-call(f32[128,128]{1,0:T(8,128)S(1)} %cholesky.581), custom_call_target="Cholesky" | custom-call | tf_op jit(solution)/shard_map/jit(cholesky)/cholesky | solution.py:58
  325.9 9.8 %custom-call.67 = f32[1,128,128]{1,2,0:T(8,128)S(1)} custom-call(f32[1,128,128]{2,1,0:T(8,128)S(1)} %get-tuple-element.60), custom_call_target="InvertDiagBlocksLowerTriangular" | custom-call | tf_op jit(solution)/shard_map/jit(cholesky)/cholesky | solution.py:58
  338.8 2.4 convolution_subtract_fusion.11
  341.2 11.7 %cholesky.466 = f32[128,128]{1,0:T(8,128)S(1)} custom-call(f32[128,128]{1,0:T(8,128)S(1)} %cholesky.586), custom_call_target="Cholesky" | custom-call | tf_op jit(solution)/shard_map/jit(cholesky)/cholesky | solution.py:58
  353.7 9.8 %custom-call.68 = f32[1,128,128]{1,2,0:T(8,128)S(1)} custom-call(f32[1,128,128]{2,1,0:T(8,128)S(1)} %get-tuple-element.58), custom_call_target="InvertDiagBlocksLowerTriangular" | custom-call | tf_op jit(solution)/shard_map/jit(cholesky)/cholesky | solution.py:58
  364.8 3.3 convolution_subtract_fusion.12
  368.1 11.7 %cholesky.485 = f32[128,128]{1,0:T(8,128)S(1)} custom-call(f32[128,128]{1,0:T(8,128)S(1)} %cholesky.591), custom_call_target="Cholesky" | custom-call | tf_op jit(solution)/shard_map/jit(cholesky)/cholesky | solution.py:58
  380.6 9.8 %custom-call.69 = f32[1,128,128]{1,2,0:T(8,128)S(1)} custom-call(f32[1,128,128]{2,1,0:T(8,128)S(1)} %get-tuple-element.56), custom_call_target="InvertDiagBlocksLowerTriangular" | custom-call | tf_op jit(solution)/shard_map/jit(cholesky)/cholesky | solution.py:58
  391.5 3.1 convolution_subtract_fusion.13
  394.7 12.2 %cholesky.504 = f32[128,128]{1,0:T(8,128)S(1)} custom-call(f32[128,128]{1,0:T(8,128)S(1)} %cholesky.596), custom_call_target="Cholesky" | custom-call | tf_op jit(solution)/shard_map/jit(cholesky)/cholesky | solution.py:58
  407.6 9.8 %custom-call.70 = f32[1,128,128]{1,2,0:T(8,128)S(1)} custom-call(f32[1,128,128]{2,1,0:T(8,128)S(1)} %get-tuple-element.54), custom_call_target="InvertDiagBlocksLowerTriangular" | custom-call | tf_op jit(solution)/shard_map/jit(cholesky)/cholesky | solution.py:58
  418.6 3.1 convolution_subtract_fusion.14
  421.7 11.7 %cholesky.524 = f32[128,128]{1,0:T(8,128)S(1)} custom-call(f32[128,128]{1,0:T(8,128)S(1)} %cholesky.601), custom_call_target="Cholesky" | custom-call | tf_op jit(solution)/shard_map/jit(cholesky)/cholesky | solution.py:58
  434.1 9.8 %custom-call.71 = f32[1,128,128]{1,2,0:T(8,128)S(1)} custom-call(f32[1,128,128]{2,1,0:T(8,128)S(1)} %get-tuple-element.52), custom_call_target="InvertDiagBlocksLowerTriangular" | custom-call | tf_op jit(solution)/shard_map/jit(cholesky)/cholesky | solution.py:58
  444.9 2.8 convolution_subtract_fusion.15
  447.8 11.7 %cholesky.544 = f32[128,128]{1,0:T(8,128)S(1)} custom-call(f32[128,128]{1,0:T(8,128)S(1)} %cholesky.606), custom_call_target="Cholesky" | custom-call | tf_op jit(solution)/shard_map/jit(cholesky)/cholesky | solution.py:58
  460.3 9.8 %custom-call.72 = f32[1,128,128]{1,2,0:T(8,128)S(1)} custom-call(f32[1,128,128]{2,1,0:T(8,128)S(1)} %get-tuple-element.50), custom_call_target="InvertDiagBlocksLowerTriangular" | custom-call | tf_op jit(solution)/shard_map/jit(cholesky)/cholesky | solution.py:58
  473.1 11.7 %cholesky.562 = f32[128,128]{1,0:T(8,128)S(1)} custom-call(f32[128,128]{1,0:T(8,128)S(1)} %convolution_subtract_fusion.16), custom_call_target="Cholesky" | custom-call | tf_op jit(solution)/shard_map/jit(cholesky)/cholesky | solution.py:58
  495.0 4.9 select_select_fusion
  499.9 23.7 %while.1 = (s32[]{:T(128)}, f32[1024,1024]{0,1:T(8,128)}, s32[8,2]{0,1:T(2,128)S(1)}, f32[8,128,128]{2,1,0:T(8,128)S(1)}, s32[]{:T(128)}) while((s32[]{:T(128)}, f32[1024,1024]{0,1:T(8,128)}, s32[8,2]{0,1:T(2,128)S(1)}, f32[8,128,128]{2,1,0:T(8,128)S(1)}, s32[]{:T(128)}) %tuple.57), condition=%wide.while_cond, body=%wide.while_body.sunk | while | flops 2 | bytes 393321 | solution.py:59
  500.6 2.2 dynamic-slice.7
  503.6 2.2 dynamic-slice.7
  506.5 2.2 dynamic-slice.7
  509.5 2.2 dynamic-slice.7
  512.5 2.2 dynamic-slice.7
  515.5 2.2 dynamic-slice.7
  518.4 2.2 dynamic-slice.7
  521.4 2.2 dynamic-slice.7
  523.7 79.0 %custom-call.73 = f32[8,128,128]{1,2,0:T(8,128)S(1)} custom-call(f32[8,128,128]{2,1,0:T(8,128)S(1)} %get-tuple-element.9), custom_call_target="InvertDiagBlocksLowerTriangular" | custom-call | tf_op jit(solution)/shard_map/jit(_cho_solve)/triangular_solve | solution.py:59
  618.7 2.5 convolution_subtract_fusion.8
  634.2 2.2 convolution_subtract_fusion.6
  638.6 6.1 fusion.1
  (170 shorter events, 68.8 us)
Async XLA Ops:
  7.2 23.4 %copy-start.7 = (f32[512]{0:T(512)S(1)}, f32[512]{0:T(512)}, u32[]{:S(2)}) copy-start(f32[512]{0:T(512)} %param.9) | copy-start | bytes 6148
  12.6 14.5 %all-to-all-start = ((s32[32,1,32]{2,1,0:T(1,128)}), s32[32,1,32]{2,1,0:T(1,128)S(1)}, u32[]{:S(2)}, u32[]{:S(2)}) async-start(s32[32,1,32]{2,1,0:T(1,128)} %all_to_all.9), calls=%async_computation | async-start | bytes 32768 | tf_op jit(solution)/shard_map/all_to_all | solution.py:33
  19.9 63.9 %copy-start.6 = (f32[512]{0:T(512)S(1)}, f32[512]{0:T(512)}, u32[]{:S(2)}) copy-start(f32[512]{0:T(512)} %param.8) | copy-start | bytes 6148
  27.0 51.0 %all-to-all-start.1 = ((bf16[32,32,1024]{2,1,0:T(8,128)(2,1)}), bf16[32,32,1024]{2,1,0:T(8,128)(2,1)S(1)}, u32[]{:S(2)}, u32[]{:S(2)}) async-start(bf16[32,32,1024]{2,1,0:T(8,128)(2,1)} %bitcast.3), calls=%async_computation.1 | async-start | bytes 4194304 | tf_op jit(solution)/shard_map/all_to_all | solution.py:26
  30.5 241.3 %all-reduce.4.cloned.1.call-start = ((), (), s32[]{:S(2)}) async-start(), calls=%async_computation.2 | async-start | bytes 16777216 | tf_op jit(solution)/shard_map/psum | solution.py:57
  85.9 3.5 copy-start.5
  286.8 2.0 copy-start.2
  336.8 2.0 copy-start
  602.7 4.4 copy-start.1
  606.4 3.6 copy-start.4
  636.4 2.2 copy-start.3
Sparse Core Ops, SparseCore 0:
  93.2 178.5 all-reduce.3
where the time goes:
time: 659 us; the launch traced here: 652 us
  other arithmetic  269 us (41%)
  waiting for transfers between devices  224 us (34%)
  matrix products  72.4 us (11%)
  local copies, waits for them, and re-layouts  55 us (8%)
  between operations  20.2 us (3%)
  starting transfers between devices  10.8 us (2%)
    psum x1, waiting for transfers between devices, on_device(): lax.psum((gram_part, cross_part), ('state', 'obs'))  175 us
    another operation x30, other arithmetic, on_device(): factor = jnp.linalg.cholesky(gram_total + identity)  168 us
    another operation x4, other arithmetic, on_device(): jax.scipy.linalg.cho_solve((factor, True), cross_total).astype(jnp.bfloat16)  83.9 us
    all_to_all x1, waiting for transfers between devices, on_device(): lax.all_to_all(outgoing.reshape(shards, capacity, members), ('state', 'ob...  46.1 us
    another operation x30, matrix products, on_device(): jax.scipy.linalg.cho_solve((factor, True), cross_total).astype(jnp.bfloat16)  33.3 us
    another operation x14, matrix products, on_device(): factor = jnp.linalg.cholesky(gram_total + identity)  25.9 us
    another operation x42, local copies, waits for them, and re-layouts  23.7 us
  transfers between devices with their start and end apart: 3, of which 3 were waited for; matrix products, arithmetic and copies ran while one was open for 1% of the time, Pallas kernels for 0%

commit v1 on v0

v1 whole, which is shorter than its diff:
```python
import functools
import jax
import jax.numpy as jnp
from jax import lax
from jax.experimental import pallas as pl
from jax.experimental.pallas import tpu as pltpu
from jax.sharding import PartitionSpec as P

AXES = ("state", "obs")
TILE = 256
TOLERANCE = 1e-4
MAX_STEPS = 4096
REFRESH = 32


def bits_of(axis):
    return [(axis, b) for b in range(lax.axis_size(axis).bit_length() - 1)]


def my_bit(dim):
    axis, b = dim
    return (lax.axis_index(axis) >> b) & 1


def swap(vals, dim):
    axis, b = dim
    return lax.ppermute(vals, axis, [(i, i ^ (1 << b)) for i in range(lax.axis_size(axis))])


def pick(vals, bit):
    half = vals.shape[0] // 2
    return lax.dynamic_slice_in_dim(vals, bit * half, half, 0)


def sum_scatter(vals, dims):
    for dim in dims:
        bit = my_bit(dim)
        vals = pick(vals, bit) + swap(pick(vals, 1 - bit), dim)
    return vals


def join(vals, dims):
    for dim in reversed(dims):
        other = swap(vals, dim)
        low = my_bit(dim) == 0
        vals = jnp.concatenate([jnp.where(low, vals, other), jnp.where(low, other, vals)])
    return vals


def orders():
    state, obs = bits_of("state"), bits_of("obs")
    return (state + obs, state[:1] + state[1:][::-1] + obs)


def tile_starts(members):
    starts, at = [], 0
    for j in range(members // TILE):
        starts.append(at)
        at += members - j * TILE
    return starts, at


def solve_kernel(tiles_ref, rhs_ref, out_ref, s1_ref, s2_ref, s3_ref, diag_ref):
    count, members = rhs_ref.shape
    shift = float(members - 1)
    starts, _ = tile_starts(members)
    blocks = members // TILE
    row = lax.broadcasted_iota(jnp.int32, (TILE, TILE), 0)
    col = lax.broadcasted_iota(jnp.int32, (TILE, TILE), 1)

    def place(vals, i, j):
        here = (pl.ds(i * TILE, TILE), pl.ds(j * TILE, TILE))
        one = vals.astype(jnp.bfloat16)
        rest = vals - one.astype(jnp.float32)
        two = rest.astype(jnp.bfloat16)
        s1_ref[here] = one
        s2_ref[here] = two
        s3_ref[here] = (rest - two.astype(jnp.float32)).astype(jnp.bfloat16)

    for j in range(blocks):
        for i in range(j, blocks):
            vals = tiles_ref[pl.ds(starts[j] + (i - j) * TILE, TILE), :]
            if i == j:
                vals = vals + jnp.where(row == col, shift, 0.0)
                diag_ref[:, pl.ds(j * TILE, TILE)] = jnp.sum(jnp.where(row == col, vals, 0.0), axis=0, keepdims=True)
                place(vals, j, j)
            else:
                place(vals, i, j)
                place(vals.T, j, i)

    def times(vals):
        one = vals.astype(jnp.bfloat16)
        rest = vals - one.astype(jnp.float32)
        two = rest.astype(jnp.bfloat16)
        three = (rest - two.astype(jnp.float32)).astype(jnp.bfloat16)
        dot = functools.partial(jnp.dot, preferred_element_type=jnp.float32)
        first = dot(jnp.concatenate([one, two, three]), s1_ref[...])
        second = dot(jnp.concatenate([one, two]), s2_ref[...])
        third = dot(one, s3_ref[...])
        small = first[2 * count :] + second[count:] + third
        return first[:count] + (first[count : 2 * count] + second[:count] + small)

    inverse = 1.0 / diag_ref[...]
    rhs = rhs_ref[...]
    bound = (TOLERANCE * shift) ** 2

    def unsolved(x, r):
        gap = jnp.sum(r * r, axis=1, keepdims=True) - bound * jnp.sum(x * x, axis=1, keepdims=True)
        return jnp.max(gap)

    def divide(a, b):
        return jnp.where(b > 0.0, a / jnp.where(b > 0.0, b, 1.0), 0.0)

    x = rhs * inverse
    r = rhs - times(x)
    z = r * inverse

    def more(carry):
        step, gap = carry[0], carry[1]
        return jnp.logical_and(step < MAX_STEPS, gap > 0.0)

    def advance(carry):
        step, _, x, r, p, rz = carry
        q = times(p)
        alpha = divide(rz, jnp.sum(p * q, axis=1, keepdims=True))
        x = x + alpha * p
        r = r - alpha * q
        r = lax.cond(step % REFRESH == REFRESH - 1, lambda x, r: rhs - times(x), lambda x, r: r, x, r)
        z = r * inverse
        rz_next = jnp.sum(r * z, axis=1, keepdims=True)
        p = z + divide(rz_next, rz) * p
        return step + 1, unsolved(x, r), x, r, p, rz_next

    init = (jnp.int32(0), unsolved(x, r), x, r, z, jnp.sum(r * z, axis=1, keepdims=True))
    out_ref[...] = lax.while_loop(more, advance, init)[2].astype(jnp.bfloat16)


def solve(tiles, rhs):
    members = rhs.shape[1]
    square = pltpu.VMEM((members, members), jnp.bfloat16)
    return pl.pallas_call(
        solve_kernel,
        out_shape=jax.ShapeDtypeStruct(rhs.shape, jnp.bfloat16),
        in_specs=[pl.BlockSpec(memory_space=pltpu.VMEM)] * 2,
        out_specs=pl.BlockSpec(memory_space=pltpu.VMEM),
        scratch_shapes=[square, square, square, pltpu.VMEM((1, members), jnp.float32)],
        compiler_params=pltpu.CompilerParams(vmem_limit_bytes=40 * 1024 * 1024),
        cost_estimate=pl.CostEstimate(flops=6 * 6 * 2 * rhs.shape[0] * members * members, bytes_accessed=6 * members * members, transcendentals=0),
        name="member_solve",
    )(tiles, rhs)


def weighted(vals, root_weight):
    member_mean = jnp.mean(vals, axis=1, keepdims=True)
    return (root_weight * (vals - member_mean)).astype(jnp.bfloat16)


def on_device(predictions, obs_index, data_values, noise_var, perturbations, unknowns):
    shards = lax.axis_size(AXES)
    rows, members = predictions.shape
    capacity = 2 * rows // shards
    me = lax.axis_index(AXES)
    first, second = orders()
    f32, bf16 = jnp.float32, jnp.bfloat16
    ids = jnp.arange(rows, dtype=jnp.int32)
    shard_ids = jnp.arange(shards, dtype=jnp.int32)
    earlier = (ids[:, None] < ids[None, :]).astype(bf16)

    owners, slots = obs_index // rows, obs_index % rows
    by_owner = (shard_ids[:, None] == owners[None, :]).astype(bf16)
    ahead = jnp.dot(by_owner, earlier, preferred_element_type=f32)
    rank = jnp.sum(ahead * by_owner.astype(f32), axis=0).astype(jnp.int32)
    place = owners * capacity + rank
    pack = (jnp.arange(shards * capacity, dtype=jnp.int32)[:, None] == place[None, :]).astype(bf16)
    outgoing = jnp.dot(pack, predictions, preferred_element_type=f32).astype(bf16)
    got = lax.all_to_all(outgoing.reshape(shards, capacity, members), AXES, split_axis=0, concat_axis=0, tiled=True)

    own = jnp.stack([obs_index.astype(f32), noise_var])[None]
    table = join(own, (bits_of("obs") + bits_of("state"))[::-1])
    index_table, noise_table = table[:, 0].astype(jnp.int32), table[:, 1]

    noise_rows = jnp.dot(by_owner.T.astype(f32), noise_table, precision=lax.Precision.HIGHEST, preferred_element_type=f32)
    noise_here = jnp.sum(jnp.where(slots[:, None] == ids[None, :], noise_rows, 0.0), axis=1, keepdims=True)
    here = weighted(predictions.astype(f32), jnp.sqrt(1.0 / noise_here))
    tiles = jnp.concatenate(
        [
            jnp.dot(here[:, j:].T, here[:, j : j + TILE], preferred_element_type=f32)
            for j in range(0, members, TILE)
        ]
    )
    half = tiles.shape[0] // 2
    gram = jnp.concatenate(
        [join(sum_scatter(tiles[:half], first), first), join(sum_scatter(tiles[half:], second), second)]
    )

    mine = index_table // rows == me
    mine_ahead = jnp.dot(mine.astype(bf16), earlier, preferred_element_type=f32).astype(jnp.int32)
    chosen = mine[:, None, :] & (mine_ahead[:, None, :] == jnp.arange(capacity, dtype=jnp.int32)[None, :, None])
    slot_of = jnp.sum(jnp.where(chosen, index_table[:, None, :] % rows + 1, 0), axis=2).reshape(1, -1) - 1
    unpack = (ids[:, None] == slot_of).astype(bf16)
    arranged = jnp.dot(unpack, got.reshape(-1, members), preferred_element_type=f32).astype(bf16)

    pred_vals = arranged.astype(f32)
    root_weight = jnp.sqrt(1.0 / noise_var)[:, None]
    anomalies = weighted(pred_vals, root_weight)
    raw_innov = data_values[:, None] + perturbations.astype(f32) - pred_vals
    innovation_var = jnp.mean(raw_innov * raw_innov, axis=1)
    innovation = (root_weight * raw_innov).astype(bf16)

    bit = my_bit(first[0])
    quarter = members // 4

    def cross_part(stream, side):
        cols = lax.dynamic_slice_in_dim(innovation, stream * 2 * quarter + side * quarter, quarter, 1)
        return jnp.dot(cols.T, anomalies, preferred_element_type=f32)

    sent = [swap(cross_part(s, 1 - bit), first[0]) for s in range(2)]
    kept = [cross_part(s, bit) for s in range(2)]
    cross = [
        sum_scatter(k + g, order[1:]) for k, g, order in zip(kept, sent, (first, second), strict=True)
    ]
    each = cross[0].shape[0]
    gain = solve(gram, jnp.concatenate(cross))
    gain_t = jnp.concatenate([join(gain[:each], first), join(gain[each:], second)])

    block_vals = unknowns.astype(f32)
    spread = (block_vals - jnp.mean(block_vals, axis=1, keepdims=True)).astype(bf16)
    moved = lax.dot_general(spread, gain_t, (((1,), (1,)), ((), ())), preferred_element_type=f32)
    return ((block_vals + moved).astype(bf16), innovation_var)


def solution(mesh):
    return jax.shard_map(
        on_device,
        mesh=mesh,
        in_specs=(
            P(AXES, None),
            P(AXES),
            P(AXES),
            P(AXES),
            P(AXES, None),
            P(AXES, None),
        ),
        out_specs=(P(AXES, None), P(AXES)),
        check_vma=False,
    )
```

time: 659 us -> 204 us (0.31); the launches traced: 652 us -> 204 us
  other arithmetic: 269 us -> 14 us
  waiting for transfers between devices: 224 us -> 81.6 us
  starting transfers between devices: 10.8 us -> 69.4 us
  local copies, waits for them, and re-layouts: 55 us -> 2.34 us
  matrix products: 72.4 us -> 24.5 us
  between operations: 20.2 us -> 1.44 us
  Pallas kernels: 0 us -> 10.6 us
    another operation x36 -> x1, other arithmetic: 253 us -> 0.69 us  [on_device(): own = jnp.stack([obs_index.astype(f32), noise_var])[None]]
    psum x1 -> x0, waiting for transfers between devices: 175 us -> none  [on_device(): lax.psum((gram_part, cross_part), ('state', 'obs'))]
    ppermute x0 -> x45, waiting for transfers between devices: none -> 81.6 us  [swap(): lax.ppermute(vals, axis, [(i, i ^ 1 << b) for i in range(lax.axis_size(ax...]
    ppermute x0 -> x45, starting transfers between devices: none -> 63 us  [swap(): lax.ppermute(vals, axis, [(i, i ^ 1 << b) for i in range(lax.axis_size(ax...]
    another operation x44 -> x0, matrix products: 59.2 us -> none  [the longest x30 33.3 us: on_device(): jax.scipy.linalg.cho_solve((factor, True), cross_total).astype(jnp.bfloat16)]
    all_to_all x2 -> x1, waiting for transfers between devices: 48.5 us -> 0.01 us  [on_device(): lax.all_to_all(outgoing.reshape(shards, capacity, members), AXES, split_a...]
    another operation x71 -> x0, local copies, waits for them, and re-layouts: 29.2 us -> none
    scatter x3 -> x0, local copies, waits for them, and re-layouts: 12.9 us -> none  [the longest x1 5.7 us: on_device(): arranged = jnp.zeros((row_count, members), jnp.bfloat16).at[got_slots.res...]
  transfers between devices with their start and end apart: 3 -> 46, of which waited for: 3 -> 33; matrix products, arithmetic and copies ran while one was open for 1% -> 15% of each run, Pallas kernels for 0% -> 0%
where the time goes in v1:
time: 204 us
  waiting for transfers between devices  81.6 us (40%)
  starting transfers between devices  69.4 us (34%)
  matrix products  24.5 us (12%)
  other arithmetic  14 us (7%)
  Pallas kernels  10.6 us (5%)
  local copies, waits for them, and re-layouts  2.34 us (1%)
    ppermute x45, waiting for transfers between devices, swap(): lax.ppermute(vals, axis, [(i, i ^ 1 << b) for i in range(lax.axis_size(ax...  81.6 us
    ppermute x45, starting transfers between devices, swap(): lax.ppermute(vals, axis, [(i, i ^ 1 << b) for i in range(lax.axis_size(ax...  63 us
    pallas_call x1, Pallas kernels, solve(): pl.pallas_call(solve_kernel, out_shape=jax.ShapeDtypeStruct(rhs.shape, jn...  10.6 us
    dot_general x1, matrix products, on_device(): lax.dot_general(spread, gain_t, (((1,), (1,)), ((), ())), preferred_eleme...  8.22 us
    dot_general x4, matrix products, cross_part(): return jnp.dot(cols.T, anomalies, preferred_element_type=f32)  6.65 us
    all_to_all x1, starting transfers between devices, on_device(): lax.all_to_all(outgoing.reshape(shards, capacity, members), AXES, split_a...  6.41 us
  transfers between devices with their start and end apart: 46, of which 33 were waited for; matrix products, arithmetic and copies ran while one was open for 15% of the time, Pallas kernels for 0%

profile of v1, /device:TPU:0, one launch (start us, length us, event | category | flops | bytes accessed | tf_op | source)
XLA Modules:
  0.0 203.9 jit_solution(4504337618898168284)
XLA Ops:
  2.1 3.1 %collective-permute-start = (f32[1,2,512]{2,0,1:T(1,128)S(1)}, f32[1,2,512]{2,0,1:T(1,128)S(1)}, u32[]{:S(2)}, u32[]{:S(2)}) collective-permute-start(f32[1,2,512]{2,0,1:T(1,128)S(1)} %broadcast_in_dim.16), channel_id=1, source_target_pairs={{0,1},{1,0},{2,3},{3,2},{4,5},{5,4},{6,7},{7,6},{8,9},{9,8},{10,11... | collective-permute-start | bytes 12296 | tf_op jit(solution)/shard_map/ppermute | solution.py:27
  6.8 3.1 %collective-permute-start.1 = (f32[2,2,512]{2,0,1:T(2,128)S(1)}, f32[2,2,512]{2,0,1:T(2,128)S(1)}, u32[]{:S(2)}, u32[]{:S(2)}) collective-permute-start(f32[2,2,512]{2,0,1:T(2,128)S(1)} %pad_maximum_fusion.24), channel_id=1, source_target_pairs={{0,2},{1,3},{2,0},{3,1},{4,6},{5,7},{6,4},{7,5},{8,10},{9,11},{10,... | collective-permute-start | bytes 24584 | tf_op jit(solution)/shard_map/ppermute | solution.py:27
  9.9 1.6 collective-permute-done.1
  11.6 3.8 %fusion.21 = bf16[1024,1024]{1,0:T(8,128)(2,1)} fusion(bf16[512,1024]{1,0:T(8,128)(2,1)} %param.6, s32[512]{0:T(512)S(1)} %convert_add_fusion.1), kind=kOutput, calls=%fused_computation.33 | convolution fusion | flops 1075314688 | bytes 3147776 | tf_op jit(solution)/shard_map/dot_general | solution.py:175
  15.4 6.4 %all-to-all-start = ((bf16[32,32,1024]{2,1,0:T(8,128)(2,1)}), bf16[32,32,1024]{2,1,0:T(8,128)(2,1)}, u32[]{:S(2)}, u32[]{:S(2)}) async-start(bf16[32,32,1024]{2,1,0:T(8,128)(2,1)} %bitcast.6), calls=%async_computation | async-start | bytes 4194304 | tf_op jit(solution)/shard_map/all_to_all | solution.py:176
  21.9 1.8 collective-permute-start.3
  23.7 12.9 %collective-permute-done.3 = f32[8,2,512]{2,0,1:T(8,128)S(1)} collective-permute-done((f32[8,2,512]{2,0,1:T(8,128)S(1)}, f32[8,2,512]{2,0,1:T(8,128)S(1)}, u32[]{:S(2)}, u32[]{:S(2)}) %collective-permute-start.3) | collective-permute-done | bytes 32800 | tf_op jit(solution)/shard_map/ppermute | solution.py:27
  36.6 1.5 collective-permute-start.4
  38.4 4.1 %collective-permute-done.4 = f32[16,2,512]{2,0,1:T(8,128)S(1)} collective-permute-done((f32[16,2,512]{2,0,1:T(8,128)S(1)}, f32[16,2,512]{2,0,1:T(8,128)S(1)}, u32[]{:S(2)}, u32[]{:S(2)}) %collective-permute-start.4) | collective-permute-done | bytes 65568 | tf_op jit(solution)/shard_map/ppermute | solution.py:27
  51.7 2.6 %collective-permute-start.16 = (f32[320,256]{1,0:T(8,128)S(1)}, f32[320,256]{1,0:T(8,128)S(1)}, u32[]{:S(2)}, u32[]{:S(2)}) collective-permute-start(f32[320,256]{1,0:T(8,128)S(1)} %constant_dynamic-slice_fusion.10), channel_id=1, source_target_pairs={{0,16},{4,20},{8,24},{12,28},{16,0},{20,4},{24,8},{28,12},{1,17},{... | collective-permute-start | bytes 983048 | tf_op jit(solution)/shard_map/ppermute | solution.py:27
  54.3 7.9 %collective-permute-done.6 = f32[320,256]{1,0:T(8,128)S(1)} collective-permute-done((f32[320,256]{1,0:T(8,128)S(1)}, f32[320,256]{1,0:T(8,128)S(1)}, u32[]{:S(2)}, u32[]{:S(2)}) %collective-permute-start.6) | collective-permute-done | bytes 327712 | tf_op jit(solution)/shard_map/ppermute | solution.py:27
  63.6 1.6 collective-permute-done.16
  65.3 1.9 collective-permute-start.17
  67.2 2.4 %collective-permute-done.7 = f32[160,256]{1,0:T(8,128)S(1)} collective-permute-done((f32[160,256]{1,0:T(8,128)S(1)}, f32[160,256]{1,0:T(8,128)S(1)}, u32[]{:S(2)}, u32[]{:S(2)}) %collective-permute-start.7) | collective-permute-done | bytes 163872 | tf_op jit(solution)/shard_map/ppermute | solution.py:27
  71.5 2.7 %collective-permute-start.18 = (f32[80,256]{1,0:T(8,128)S(1)}, f32[80,256]{1,0:T(8,128)S(1)}, u32[]{:S(2)}, u32[]{:S(2)}) collective-permute-start(f32[80,256]{1,0:T(8,128)S(1)} %constant_dynamic-slice_fusion.8), channel_id=1, source_target_pairs={{0,1},{1,0},{2,3},{3,2},{4,5},{5,4},{6,7},{7,6},{8,9},{9,8},{10,11... | collective-permute-start | bytes 245768 | tf_op jit(solution)/shard_map/ppermute | solution.py:27
  74.2 3.7 %collective-permute-start.9 = (f32[40,256]{1,0:T(8,128)S(1)}, f32[40,256]{1,0:T(8,128)S(1)}, u32[]{:S(2)}, u32[]{:S(2)}) collective-permute-start(f32[40,256]{1,0:T(8,128)S(1)} %constant_dynamic-slice_fusion.12), channel_id=1, source_target_pairs={{0,2},{1,3},{2,0},{3,1},{4,6},{5,7},{6,4},{7,5},{8,10},{9,11},{10,... | collective-permute-start | bytes 122888 | tf_op jit(solution)/shard_map/ppermute | solution.py:27
  78.0 1.6 collective-permute-start.19
  80.4 2.6 %collective-permute-start.10 = (f32[40,256]{1,0:T(8,128)S(1)}, f32[40,256]{1,0:T(8,128)S(1)}, u32[]{:S(2)}, u32[]{:S(2)}) collective-permute-start(f32[40,256]{1,0:T(8,128)S(1)} %dynamic-slice_add_fusion.16), channel_id=1, source_target_pairs={{0,2},{1,3},{2,0},{3,1},{4,6},{5,7},{6,4},{7,5},{8,10},{9,11},{10,... | collective-permute-start | bytes 122888 | tf_op jit(solution)/shard_map/ppermute | solution.py:27
  83.1 1.5 collective-permute-start.20
  85.4 2.6 %collective-permute-start.11 = (f32[80,256]{1,0:T(8,128)S(1)}, f32[80,256]{1,0:T(8,128)S(1)}, u32[]{:S(2)}, u32[]{:S(2)}) collective-permute-start(f32[80,256]{1,0:T(8,128)S(1)} %pad_maximum_fusion.16), channel_id=1, source_target_pairs={{0,1},{1,0},{2,3},{3,2},{4,5},{5,4},{6,7},{7,6},{8,9},{9,8},{10,11... | collective-permute-start | bytes 245768 | tf_op jit(solution)/shard_map/ppermute | solution.py:27
  88.1 2.4 %collective-permute-start.21 = (f32[80,256]{1,0:T(8,128)S(1)}, f32[80,256]{1,0:T(8,128)S(1)}, u32[]{:S(2)}, u32[]{:S(2)}) collective-permute-start(f32[80,256]{1,0:T(8,128)S(1)} %pad_maximum_fusion.17), channel_id=1, source_target_pairs={{0,1},{1,0},{2,3},{3,2},{4,5},{5,4},{6,7},{7,6},{8,9},{9,8},{10,11... | collective-permute-start | bytes 245768 | tf_op jit(solution)/shard_map/ppermute | solution.py:27
  93.0 1.8 collective-permute-start.22
  96.0 1.8 collective-permute-start.13
  99.6 3.6 %collective-permute-done.13 = f32[320,256]{1,0:T(8,128)S(1)} collective-permute-done((f32[320,256]{1,0:T(8,128)S(1)}, f32[320,256]{1,0:T(8,128)S(1)}, u32[]{:S(2)}, u32[]{:S(2)}) %collective-permute-start.13) | collective-permute-done | bytes 327712 | tf_op jit(solution)/shard_map/ppermute | solution.py:27
  104.1 1.9 collective-permute-done.23
  106.1 3.2 %multiply_reduce_fusion = (f32[512]{0:T(512)S(1)}, f32[512]{0:T(512)S(1)}, bf16[512,1024]{1,0:T(8,128)(2,1)S(1)}, bf16[512,1024]{1,0:T(8,128)(2,1)S(1)}) fusion(bf16[512,1024]{1,0:T(8,128)(2,1)S(1)} %copy-done.5, f32[512]{0:T(512)S(1)} %copy-done.6, f32[512]{0:T(512)S(1)} %divide_sqrt_fusion, bf16[1024,1024]{1,0:T(8,128)(2,1)} %bitcast.7, s32[1024]{0:T(1024)S(1)} %sub.90), kind=kOutput, calls=%fused_computation.24 | convolution fusion | flops 1079507968 | bytes 5255168 | tf_op jit(solution)/shard_map/dot_general | solution.py:201
  110.3 1.7 fusion.43
  113.4 2.5 %fusion.40 = f32[256,1024]{1,0:T(8,128)} fusion(bf16[512,1024]{1,0:T(8,128)(2,1)} %copy-done.2, s32[]{:T(128)S(6)} %select_n.483, bf16[512,1024]{1,0:T(8,128)(2,1)S(1)} %get-tuple-element.59, f32[512]{0:T(512)S(1)} %broadcast_multiply_fusion.2, f32[512]{0:T(512)S(1)} %divide_sqrt_fusion), kind=kOutput, calls=%fused_computation.87 | convolution fusion | flops 270532608 | bytes 2363396 | tf_op jit(solution)/shard_map/dot_general | solution.py:215
  119.3 1.8 collective-permute-start.26
  121.1 1.8 convolution_add_fusion
  123.7 10.0 %collective-permute-done.26 = f32[128,1024]{1,0:T(8,128)S(1)} collective-permute-done((f32[128,1024]{1,0:T(8,128)S(1)}, f32[128,1024]{1,0:T(8,128)S(1)}, u32[]{:S(2)}, u32[]{:S(2)}) %collective-permute-start.26) | collective-permute-done | bytes 524320 | tf_op jit(solution)/shard_map/ppermute | solution.py:27
  134.5 3.3 %collective-permute-done.31 = f32[128,1024]{1,0:T(8,128)S(1)} collective-permute-done((f32[128,1024]{1,0:T(8,128)S(1)}, f32[128,1024]{1,0:T(8,128)S(1)}, u32[]{:S(2)}, u32[]{:S(2)}) %collective-permute-start.31) | collective-permute-done | bytes 524320 | tf_op jit(solution)/shard_map/ppermute | solution.py:27
  138.0 4.8 %collective-permute-done.27 = f32[64,1024]{1,0:T(8,128)S(1)} collective-permute-done((f32[64,1024]{1,0:T(8,128)S(1)}, f32[64,1024]{1,0:T(8,128)S(1)}, u32[]{:S(2)}, u32[]{:S(2)}) %collective-permute-start.27) | collective-permute-done | bytes 262176 | tf_op jit(solution)/shard_map/ppermute | solution.py:27
  142.8 1.7 collective-permute-start.28
  145.0 1.7 collective-permute-start.33
  146.7 2.5 %collective-permute-done.28 = f32[32,1024]{1,0:T(8,128)S(1)} collective-permute-done((f32[32,1024]{1,0:T(8,128)S(1)}, f32[32,1024]{1,0:T(8,128)S(1)}, u32[]{:S(2)}, u32[]{:S(2)}) %collective-permute-start.28) | collective-permute-done | bytes 131104 | tf_op jit(solution)/shard_map/ppermute | solution.py:27
  149.2 2.2 %collective-permute-start.29 = (f32[16,1024]{1,0:T(8,128)S(1)}, f32[16,1024]{1,0:T(8,128)S(1)}, u32[]{:S(2)}, u32[]{:S(2)}) collective-permute-start(f32[16,1024]{1,0:T(8,128)S(1)} %constant_dynamic-slice_fusion.3), channel_id=1, source_target_pairs={{0,2},{1,3},{2,0},{3,1},{4,6},{5,7},{6,4},{7,5},{8,10},{9,11},{10,... | collective-permute-start | bytes 196616 | tf_op jit(solution)/shard_map/ppermute | solution.py:27
  151.5 2.1 %collective-permute-start.34 = (f32[16,1024]{1,0:T(8,128)S(1)}, f32[16,1024]{1,0:T(8,128)S(1)}, u32[]{:S(2)}, u32[]{:S(2)}) collective-permute-start(f32[16,1024]{1,0:T(8,128)S(1)} %constant_dynamic-slice_fusion.16), channel_id=1, source_target_pairs={{0,2},{1,3},{2,0},{3,1},{4,6},{5,7},{6,4},{7,5},{8,10},{9,11},{10,... | collective-permute-start | bytes 196616 | tf_op jit(solution)/shard_map/ppermute | solution.py:27
  153.6 2.2 %collective-permute-done.29 = f32[16,1024]{1,0:T(8,128)S(1)} collective-permute-done((f32[16,1024]{1,0:T(8,128)S(1)}, f32[16,1024]{1,0:T(8,128)S(1)}, u32[]{:S(2)}, u32[]{:S(2)}) %collective-permute-start.29) | collective-permute-done | bytes 65568 | tf_op jit(solution)/shard_map/ppermute | solution.py:27
  156.8 10.6 %member_solve.1 = bf16[32,1024]{1,0:T(8,128)(2,1)S(1)} custom-call(f32[2560,256]{1,0:T(8,128)S(1)} %pad_maximum_fusion.tiles_ref, f32[32,1024]{1,0:T(8,128)S(1)} %pad_maximum_fusion.13.rhs_ref), custom_call_target="tpu_custom_call" | custom-call | flops 2415919104 | bytes 6291456 | tf_op jit(solution)/shard_map/member_solve/pallas_call | solution.py:141
  167.4 2.1 %collective-permute-start.35 = (bf16[16,1024]{1,0:T(8,128)(2,1)S(1)}, bf16[16,1024]{1,0:T(8,128)(2,1)S(1)}, u32[]{:S(2)}, u32[]{:S(2)}) collective-permute-start(bf16[16,1024]{1,0:T(8,128)(2,1)S(1)} %slice.59), channel_id=1, source_target_pairs={{0,2},{1,3},{2,0},{3,1},{4,6},{5,7},{6,4},{7,5},{8,10},{9,11},{10,... | collective-permute-start | bytes 98312 | tf_op jit(solution)/shard_map/ppermute | solution.py:27
  170.1 2.1 %collective-permute-done.35 = bf16[16,1024]{1,0:T(8,128)(2,1)S(1)} collective-permute-done((bf16[16,1024]{1,0:T(8,128)(2,1)S(1)}, bf16[16,1024]{1,0:T(8,128)(2,1)S(1)}, u32[]{:S(2)}, u32[]{:S(2)}) %collective-permute-start.35) | collective-permute-done | bytes 32800 | tf_op jit(solution)/shard_map/ppermute | solution.py:27
  172.3 2.3 %collective-permute-start.40 = (bf16[16,1024]{1,0:T(8,128)(2,1)S(1)}, bf16[16,1024]{1,0:T(8,128)(2,1)S(1)}, u32[]{:S(2)}, u32[]{:S(2)}) collective-permute-start(bf16[16,1024]{1,0:T(8,128)(2,1)S(1)} %get-tuple-element.47), channel_id=1, source_target_pairs={{0,2},{1,3},{2,0},{3,1},{4,6},{5,7},{6,4},{7,5},{8,10},{9,11},{10,... | collective-permute-start | bytes 98312 | tf_op jit(solution)/shard_map/ppermute | solution.py:27
  174.6 2.0 collective-permute-start.36
  177.2 2.3 %collective-permute-start.41 = (bf16[32,1024]{1,0:T(8,128)(2,1)S(1)}, bf16[32,1024]{1,0:T(8,128)(2,1)S(1)}, u32[]{:S(2)}, u32[]{:S(2)}) collective-permute-start(bf16[32,1024]{1,0:T(8,128)(2,1)S(1)} %pad_maximum_fusion.21), channel_id=1, source_target_pairs={{0,1},{1,0},{2,3},{3,2},{4,5},{5,4},{6,7},{7,6},{8,9},{9,8},{10,11... | collective-permute-start | bytes 196616 | tf_op jit(solution)/shard_map/ppermute | solution.py:27
  182.5 3.4 %collective-permute-done.37 = bf16[64,1024]{1,0:T(8,128)(2,1)S(1)} collective-permute-done((bf16[64,1024]{1,0:T(8,128)(2,1)S(1)}, bf16[64,1024]{1,0:T(8,128)(2,1)S(1)}, u32[]{:S(2)}, u32[]{:S(2)}) %collective-permute-start.37) | collective-permute-done | bytes 131104 | tf_op jit(solution)/shard_map/ppermute | solution.py:27
  187.8 4.6 %collective-permute-done.38 = bf16[128,1024]{1,0:T(8,128)(2,1)S(1)} collective-permute-done((bf16[128,1024]{1,0:T(8,128)(2,1)S(1)}, bf16[128,1024]{1,0:T(8,128)(2,1)S(1)}, u32[]{:S(2)}, u32[]{:S(2)}) %collective-permute-start.38) | collective-permute-done | bytes 262176 | tf_op jit(solution)/shard_map/ppermute | solution.py:27
  195.7 8.2 %fusion.1 = bf16[2048,1024]{1,0:T(8,128)(2,1)} fusion(bf16[2048,1024]{1,0:T(8,128)(2,1)S(1)} %copy-done, f32[2048]{0:T(1024)S(1)} %broadcast_multiply_fusion, bf16[256,1024]{1,0:T(8,128)(2,1)S(1)} %get-tuple-element.12, bf16[256,1024]{1,0:T(8,128)(2,1)S(1)} %get-tuple-element.11, bf16[256,1024]{1,0:T(8,128)(2,1)S(1)} %get-tuple-element.10, ...), kind=kOutput, calls=%fused_computation.4 | convolution fusion | flops 4315938816 | bytes 10493952 | tf_op jit(solution)/shard_map/dot_general | solution.py:228
  (175 shorter events, 42.3 us)
Async XLA Ops:
  2.1 4.7 %collective-permute-start = (f32[1,2,512]{2,0,1:T(1,128)S(1)}, f32[1,2,512]{2,0,1:T(1,128)S(1)}, u32[]{:S(2)}, u32[]{:S(2)}) collective-permute-start(f32[1,2,512]{2,0,1:T(1,128)S(1)} %broadcast_in_dim.16), channel_id=1, source_target_pairs={{0,1},{1,0},{2,3},{3,2},{4,5},{5,4},{6,7},{7,6},{8,9},{9,8},{10,11... | collective-permute-start | bytes 12296 | tf_op jit(solution)/shard_map/ppermute | solution.py:27
  6.8 4.7 %collective-permute-start.1 = (f32[2,2,512]{2,0,1:T(2,128)S(1)}, f32[2,2,512]{2,0,1:T(2,128)S(1)}, u32[]{:S(2)}, u32[]{:S(2)}) collective-permute-start(f32[2,2,512]{2,0,1:T(2,128)S(1)} %pad_maximum_fusion.24), channel_id=1, source_target_pairs={{0,2},{1,3},{2,0},{3,1},{4,6},{5,7},{6,4},{7,5},{8,10},{9,11},{10,... | collective-permute-start | bytes 24584 | tf_op jit(solution)/shard_map/ppermute | solution.py:27
  11.6 10.3 %collective-permute-start.2 = (f32[4,2,512]{2,0,1:T(4,128)S(1)}, f32[4,2,512]{2,0,1:T(4,128)S(1)}, u32[]{:S(2)}, u32[]{:S(2)}) collective-permute-start(f32[4,2,512]{2,0,1:T(4,128)S(1)} %pad_maximum_fusion.23), channel_id=1, source_target_pairs={{0,4},{4,0},{8,12},{12,8},{16,20},{20,16},{24,28},{28,24},{1,5},{5... | collective-permute-start | bytes 49160 | tf_op jit(solution)/shard_map/ppermute | solution.py:27
  15.4 22.7 %copy-start.1 = (bf16[512,1024]{1,0:T(8,128)(2,1)S(1)}, bf16[512,1024]{1,0:T(8,128)(2,1)}, u32[]{:S(2)}) copy-start(bf16[512,1024]{1,0:T(8,128)(2,1)} %param.6) | copy-start | bytes 3145732
  15.4 90.6 %all-to-all-start = ((bf16[32,32,1024]{2,1,0:T(8,128)(2,1)}), bf16[32,32,1024]{2,1,0:T(8,128)(2,1)}, u32[]{:S(2)}, u32[]{:S(2)}) async-start(bf16[32,32,1024]{2,1,0:T(8,128)(2,1)} %bitcast.6), calls=%async_computation | async-start | bytes 4194304 | tf_op jit(solution)/shard_map/all_to_all | solution.py:176
  21.9 14.7 %collective-permute-start.3 = (f32[8,2,512]{2,0,1:T(8,128)S(1)}, f32[8,2,512]{2,0,1:T(8,128)S(1)}, u32[]{:S(2)}, u32[]{:S(2)}) collective-permute-start(f32[8,2,512]{2,0,1:T(8,128)S(1)} %pad_maximum_fusion.22), channel_id=1, source_target_pairs={{0,8},{4,12},{8,0},{12,4},{16,24},{20,28},{24,16},{28,20},{1,9},{5... | collective-permute-start | bytes 98312 | tf_op jit(solution)/shard_map/ppermute | solution.py:27
  36.6 5.9 %collective-permute-start.4 = (f32[16,2,512]{2,0,1:T(8,128)S(1)}, f32[16,2,512]{2,0,1:T(8,128)S(1)}, u32[]{:S(2)}, u32[]{:S(2)}) collective-permute-start(f32[16,2,512]{2,0,1:T(8,128)S(1)} %pad_maximum_fusion.19), channel_id=1, source_target_pairs={{0,16},{4,20},{8,24},{12,28},{16,0},{20,4},{24,8},{28,12},{1,17},{... | collective-permute-start | bytes 196616 | tf_op jit(solution)/shard_map/ppermute | solution.py:27
  46.1 2.6 %collective-permute-start.5 = (f32[640,256]{1,0:T(8,128)}, f32[640,256]{1,0:T(8,128)}, u32[]{:S(2)}, u32[]{:S(2)}) collective-permute-start(f32[640,256]{1,0:T(8,128)} %fusion.29), channel_id=1, source_target_pairs={{0,4},{4,0},{8,12},{12,8},{16,20},{20,16},{24,28},{28,24},{1,5},{5... | collective-permute-start | bytes 1966088 | tf_op jit(solution)/shard_map/ppermute | solution.py:27
  47.3 3.2 %collective-permute-start.15 = (f32[640,256]{1,0:T(8,128)}, f32[640,256]{1,0:T(8,128)}, u32[]{:S(2)}, u32[]{:S(2)}) collective-permute-start(f32[640,256]{1,0:T(8,128)} %constant_dynamic-slice_fusion.11), channel_id=1, source_target_pairs={{0,4},{4,0},{8,12},{12,8},{16,20},{20,16},{24,28},{28,24},{1,5},{5... | collective-permute-start | bytes 1966088 | tf_op jit(solution)/shard_map/ppermute | solution.py:27
  50.1 12.1 %collective-permute-start.6 = (f32[320,256]{1,0:T(8,128)S(1)}, f32[320,256]{1,0:T(8,128)S(1)}, u32[]{:S(2)}, u32[]{:S(2)}) collective-permute-start(f32[320,256]{1,0:T(8,128)S(1)} %constant_dynamic-slice_fusion.15), channel_id=1, source_target_pairs={{0,8},{4,12},{8,0},{12,4},{16,24},{20,28},{24,16},{28,20},{1,9},{5... | collective-permute-start | bytes 983048 | tf_op jit(solution)/shard_map/ppermute | solution.py:27
  51.7 13.6 %collective-permute-start.16 = (f32[320,256]{1,0:T(8,128)S(1)}, f32[320,256]{1,0:T(8,128)S(1)}, u32[]{:S(2)}, u32[]{:S(2)}) collective-permute-start(f32[320,256]{1,0:T(8,128)S(1)} %constant_dynamic-slice_fusion.10), channel_id=1, source_target_pairs={{0,16},{4,20},{8,24},{12,28},{16,0},{20,4},{24,8},{28,12},{1,17},{... | collective-permute-start | bytes 983048 | tf_op jit(solution)/shard_map/ppermute | solution.py:27
  62.3 7.3 %collective-permute-start.7 = (f32[160,256]{1,0:T(8,128)S(1)}, f32[160,256]{1,0:T(8,128)S(1)}, u32[]{:S(2)}, u32[]{:S(2)}) collective-permute-start(f32[160,256]{1,0:T(8,128)S(1)} %constant_dynamic-slice_fusion.14), channel_id=1, source_target_pairs={{0,16},{4,20},{8,24},{12,28},{16,0},{20,4},{24,8},{28,12},{1,17},{... | collective-permute-start | bytes 491528 | tf_op jit(solution)/shard_map/ppermute | solution.py:27
  65.3 6.1 %collective-permute-start.17 = (f32[160,256]{1,0:T(8,128)S(1)}, f32[160,256]{1,0:T(8,128)S(1)}, u32[]{:S(2)}, u32[]{:S(2)}) collective-permute-start(f32[160,256]{1,0:T(8,128)S(1)} %constant_dynamic-slice_fusion.9), channel_id=1, source_target_pairs={{0,8},{4,12},{8,0},{12,4},{16,24},{20,28},{24,16},{28,20},{1,9},{5... | collective-permute-start | bytes 491528 | tf_op jit(solution)/shard_map/ppermute | solution.py:27
  69.6 4.6 %collective-permute-start.8 = (f32[80,256]{1,0:T(8,128)S(1)}, f32[80,256]{1,0:T(8,128)S(1)}, u32[]{:S(2)}, u32[]{:S(2)}) collective-permute-start(f32[80,256]{1,0:T(8,128)S(1)} %constant_dynamic-slice_fusion.13), channel_id=1, source_target_pairs={{0,1},{1,0},{2,3},{3,2},{4,5},{5,4},{6,7},{7,6},{8,9},{9,8},{10,11... | collective-permute-start | bytes 245768 | tf_op jit(solution)/shard_map/ppermute | solution.py:27
  71.5 6.5 %collective-permute-start.18 = (f32[80,256]{1,0:T(8,128)S(1)}, f32[80,256]{1,0:T(8,128)S(1)}, u32[]{:S(2)}, u32[]{:S(2)}) collective-permute-start(f32[80,256]{1,0:T(8,128)S(1)} %constant_dynamic-slice_fusion.8), channel_id=1, source_target_pairs={{0,1},{1,0},{2,3},{3,2},{4,5},{5,4},{6,7},{7,6},{8,9},{9,8},{10,11... | collective-permute-start | bytes 245768 | tf_op jit(solution)/shard_map/ppermute | solution.py:27
  74.2 6.1 %collective-permute-start.9 = (f32[40,256]{1,0:T(8,128)S(1)}, f32[40,256]{1,0:T(8,128)S(1)}, u32[]{:S(2)}, u32[]{:S(2)}) collective-permute-start(f32[40,256]{1,0:T(8,128)S(1)} %constant_dynamic-slice_fusion.12), channel_id=1, source_target_pairs={{0,2},{1,3},{2,0},{3,1},{4,6},{5,7},{6,4},{7,5},{8,10},{9,11},{10,... | collective-permute-start | bytes 122888 | tf_op jit(solution)/shard_map/ppermute | solution.py:27
  78.0 5.1 %collective-permute-start.19 = (f32[40,256]{1,0:T(8,128)S(1)}, f32[40,256]{1,0:T(8,128)S(1)}, u32[]{:S(2)}, u32[]{:S(2)}) collective-permute-start(f32[40,256]{1,0:T(8,128)S(1)} %constant_dynamic-slice_fusion.7), channel_id=1, source_target_pairs={{0,2},{1,3},{2,0},{3,1},{4,6},{5,7},{6,4},{7,5},{8,10},{9,11},{10,... | collective-permute-start | bytes 122888 | tf_op jit(solution)/shard_map/ppermute | solution.py:27
  80.4 5.0 %collective-permute-start.10 = (f32[40,256]{1,0:T(8,128)S(1)}, f32[40,256]{1,0:T(8,128)S(1)}, u32[]{:S(2)}, u32[]{:S(2)}) collective-permute-start(f32[40,256]{1,0:T(8,128)S(1)} %dynamic-slice_add_fusion.16), channel_id=1, source_target_pairs={{0,2},{1,3},{2,0},{3,1},{4,6},{5,7},{6,4},{7,5},{8,10},{9,11},{10,... | collective-permute-start | bytes 122888 | tf_op jit(solution)/shard_map/ppermute | solution.py:27
  83.1 5.0 %collective-permute-start.20 = (f32[40,256]{1,0:T(8,128)S(1)}, f32[40,256]{1,0:T(8,128)S(1)}, u32[]{:S(2)}, u32[]{:S(2)}) collective-permute-start(f32[40,256]{1,0:T(8,128)S(1)} %dynamic-slice_add_fusion.15), channel_id=1, source_target_pairs={{0,2},{1,3},{2,0},{3,1},{4,6},{5,7},{6,4},{7,5},{8,10},{9,11},{10,... | collective-permute-start | bytes 122888 | tf_op jit(solution)/shard_map/ppermute | solution.py:27
  85.4 5.2 %collective-permute-start.11 = (f32[80,256]{1,0:T(8,128)S(1)}, f32[80,256]{1,0:T(8,128)S(1)}, u32[]{:S(2)}, u32[]{:S(2)}) collective-permute-start(f32[80,256]{1,0:T(8,128)S(1)} %pad_maximum_fusion.16), channel_id=1, source_target_pairs={{0,1},{1,0},{2,3},{3,2},{4,5},{5,4},{6,7},{7,6},{8,9},{9,8},{10,11... | collective-permute-start | bytes 245768 | tf_op jit(solution)/shard_map/ppermute | solution.py:27
  88.1 4.8 %collective-permute-start.21 = (f32[80,256]{1,0:T(8,128)S(1)}, f32[80,256]{1,0:T(8,128)S(1)}, u32[]{:S(2)}, u32[]{:S(2)}) collective-permute-start(f32[80,256]{1,0:T(8,128)S(1)} %pad_maximum_fusion.17), channel_id=1, source_target_pairs={{0,1},{1,0},{2,3},{3,2},{4,5},{5,4},{6,7},{7,6},{8,9},{9,8},{10,11... | collective-permute-start | bytes 245768 | tf_op jit(solution)/shard_map/ppermute | solution.py:27
  90.6 5.4 %collective-permute-start.12 = (f32[160,256]{1,0:T(8,128)S(1)}, f32[160,256]{1,0:T(8,128)S(1)}, u32[]{:S(2)}, u32[]{:S(2)}) collective-permute-start(f32[160,256]{1,0:T(8,128)S(1)} %pad_maximum_fusion.11), channel_id=1, source_target_pairs={{0,16},{4,20},{8,24},{12,28},{16,0},{20,4},{24,8},{28,12},{1,17},{... | collective-permute-start | bytes 491528 | tf_op jit(solution)/shard_map/ppermute | solution.py:27
  93.0 5.8 %collective-permute-start.22 = (f32[160,256]{1,0:T(8,128)S(1)}, f32[160,256]{1,0:T(8,128)S(1)}, u32[]{:S(2)}, u32[]{:S(2)}) collective-permute-start(f32[160,256]{1,0:T(8,128)S(1)} %pad_maximum_fusion.12), channel_id=1, source_target_pairs={{0,8},{4,12},{8,0},{12,4},{16,24},{20,28},{24,16},{28,20},{1,9},{5... | collective-permute-start | bytes 491528 | tf_op jit(solution)/shard_map/ppermute | solution.py:27
  96.0 7.1 %collective-permute-start.13 = (f32[320,256]{1,0:T(8,128)S(1)}, f32[320,256]{1,0:T(8,128)S(1)}, u32[]{:S(2)}, u32[]{:S(2)}) collective-permute-start(f32[320,256]{1,0:T(8,128)S(1)} %pad_maximum_fusion.7), channel_id=1, source_target_pairs={{0,8},{4,12},{8,0},{12,4},{16,24},{20,28},{24,16},{28,20},{1,9},{5... | collective-permute-start | bytes 983048 | tf_op jit(solution)/shard_map/ppermute | solution.py:27
  98.8 7.1 %collective-permute-start.23 = (f32[320,256]{1,0:T(8,128)S(1)}, f32[320,256]{1,0:T(8,128)S(1)}, u32[]{:S(2)}, u32[]{:S(2)}) collective-permute-start(f32[320,256]{1,0:T(8,128)S(1)} %pad_maximum_fusion.8), channel_id=1, source_target_pairs={{0,16},{4,20},{8,24},{12,28},{16,0},{20,4},{24,8},{28,12},{1,17},{... | collective-permute-start | bytes 983048 | tf_op jit(solution)/shard_map/ppermute | solution.py:27
  104.1 11.8 %collective-permute-start.14 = (f32[640,256]{1,0:T(8,128)}, f32[640,256]{1,0:T(8,128)}, u32[]{:S(2)}, u32[]{:S(2)}) collective-permute-start(f32[640,256]{1,0:T(8,128)} %pad_maximum_fusion.3), channel_id=1, source_target_pairs={{0,4},{4,0},{8,12},{12,8},{16,20},{20,16},{24,28},{28,24},{1,5},{5... | collective-permute-start | bytes 1966088 | tf_op jit(solution)/shard_map/ppermute | solution.py:27
  112.0 6.6 %collective-permute-start.25 = (f32[256,1024]{1,0:T(8,128)}, f32[256,1024]{1,0:T(8,128)S(1)}, u32[]{:S(2)}, u32[]{:S(2)}) collective-permute-start(f32[256,1024]{1,0:T(8,128)} %fusion.43), channel_id=1, source_target_pairs={{0,4},{4,0},{8,12},{12,8},{16,20},{20,16},{24,28},{28,24},{1,5},{5... | collective-permute-start | bytes 3145736 | tf_op jit(solution)/shard_map/ppermute | solution.py:27
  112.9 4.4 %collective-permute-start.24 = (f32[640,256]{1,0:T(8,128)}, f32[640,256]{1,0:T(8,128)}, u32[]{:S(2)}, u32[]{:S(2)}) collective-permute-start(f32[640,256]{1,0:T(8,128)} %pad_maximum_fusion.4), channel_id=1, source_target_pairs={{0,4},{4,0},{8,12},{12,8},{16,20},{20,16},{24,28},{28,24},{1,5},{5... | collective-permute-start | bytes 1966088 | tf_op jit(solution)/shard_map/ppermute | solution.py:27
  115.9 5.1 %collective-permute-start.30 = (f32[256,1024]{1,0:T(8,128)}, f32[256,1024]{1,0:T(8,128)}, u32[]{:S(2)}, u32[]{:S(2)}) collective-permute-start(f32[256,1024]{1,0:T(8,128)} %fusion.40), channel_id=1, source_target_pairs={{0,4},{4,0},{8,12},{12,8},{16,20},{20,16},{24,28},{28,24},{1,5},{5... | collective-permute-start | bytes 3145736 | tf_op jit(solution)/shard_map/ppermute | solution.py:27
  119.3 14.4 %collective-permute-start.26 = (f32[128,1024]{1,0:T(8,128)S(1)}, f32[128,1024]{1,0:T(8,128)S(1)}, u32[]{:S(2)}, u32[]{:S(2)}) collective-permute-start(f32[128,1024]{1,0:T(8,128)S(1)} %constant_dynamic-slice_fusion.6), channel_id=1, source_target_pairs={{0,8},{4,12},{8,0},{12,4},{16,24},{20,28},{24,16},{28,20},{1,9},{5... | collective-permute-start | bytes 1572872 | tf_op jit(solution)/shard_map/ppermute | solution.py:27
  123.0 14.8 %collective-permute-start.31 = (f32[128,1024]{1,0:T(8,128)S(1)}, f32[128,1024]{1,0:T(8,128)S(1)}, u32[]{:S(2)}, u32[]{:S(2)}) collective-permute-start(f32[128,1024]{1,0:T(8,128)S(1)} %constant_dynamic-slice_fusion.2), channel_id=1, source_target_pairs={{0,16},{4,20},{8,24},{12,28},{16,0},{20,4},{24,8},{28,12},{1,17},{... | collective-permute-start | bytes 1572872 | tf_op jit(solution)/shard_map/ppermute | solution.py:27
  133.8 9.0 %collective-permute-start.27 = (f32[64,1024]{1,0:T(8,128)S(1)}, f32[64,1024]{1,0:T(8,128)S(1)}, u32[]{:S(2)}, u32[]{:S(2)}) collective-permute-start(f32[64,1024]{1,0:T(8,128)S(1)} %constant_dynamic-slice_fusion.5), channel_id=1, source_target_pairs={{0,16},{4,20},{8,24},{12,28},{16,0},{20,4},{24,8},{28,12},{1,17},{... | collective-permute-start | bytes 786440 | tf_op jit(solution)/shard_map/ppermute | solution.py:27
  137.9 7.0 %collective-permute-start.32 = (f32[64,1024]{1,0:T(8,128)S(1)}, f32[64,1024]{1,0:T(8,128)S(1)}, u32[]{:S(2)}, u32[]{:S(2)}) collective-permute-start(f32[64,1024]{1,0:T(8,128)S(1)} %constant_dynamic-slice_fusion.1), channel_id=1, source_target_pairs={{0,8},{4,12},{8,0},{12,4},{16,24},{20,28},{24,16},{28,20},{1,9},{5... | collective-permute-start | bytes 786440 | tf_op jit(solution)/shard_map/ppermute | solution.py:27
  142.8 6.4 %collective-permute-start.28 = (f32[32,1024]{1,0:T(8,128)S(1)}, f32[32,1024]{1,0:T(8,128)S(1)}, u32[]{:S(2)}, u32[]{:S(2)}) collective-permute-start(f32[32,1024]{1,0:T(8,128)S(1)} %constant_dynamic-slice_fusion.4), channel_id=1, source_target_pairs={{0,1},{1,0},{2,3},{3,2},{4,5},{5,4},{6,7},{7,6},{8,9},{9,8},{10,11... | collective-permute-start | bytes 393224 | tf_op jit(solution)/shard_map/ppermute | solution.py:27
  145.0 6.5 %collective-permute-start.33 = (f32[32,1024]{1,0:T(8,128)S(1)}, f32[32,1024]{1,0:T(8,128)S(1)}, u32[]{:S(2)}, u32[]{:S(2)}) collective-permute-start(f32[32,1024]{1,0:T(8,128)S(1)} %constant_dynamic-slice_fusion), channel_id=1, source_target_pairs={{0,1},{1,0},{2,3},{3,2},{4,5},{5,4},{6,7},{7,6},{8,9},{9,8},{10,11... | collective-permute-start | bytes 393224 | tf_op jit(solution)/shard_map/ppermute | solution.py:27
  149.2 6.6 %collective-permute-start.29 = (f32[16,1024]{1,0:T(8,128)S(1)}, f32[16,1024]{1,0:T(8,128)S(1)}, u32[]{:S(2)}, u32[]{:S(2)}) collective-permute-start(f32[16,1024]{1,0:T(8,128)S(1)} %constant_dynamic-slice_fusion.3), channel_id=1, source_target_pairs={{0,2},{1,3},{2,0},{3,1},{4,6},{5,7},{6,4},{7,5},{8,10},{9,11},{10,... | collective-permute-start | bytes 196616 | tf_op jit(solution)/shard_map/ppermute | solution.py:27
  151.5 5.2 %collective-permute-start.34 = (f32[16,1024]{1,0:T(8,128)S(1)}, f32[16,1024]{1,0:T(8,128)S(1)}, u32[]{:S(2)}, u32[]{:S(2)}) collective-permute-start(f32[16,1024]{1,0:T(8,128)S(1)} %constant_dynamic-slice_fusion.16), channel_id=1, source_target_pairs={{0,2},{1,3},{2,0},{3,1},{4,6},{5,7},{6,4},{7,5},{8,10},{9,11},{10,... | collective-permute-start | bytes 196616 | tf_op jit(solution)/shard_map/ppermute | solution.py:27
  156.8 12.8 %copy-start = (bf16[2048,1024]{1,0:T(8,128)(2,1)S(1)}, bf16[2048,1024]{1,0:T(8,128)(2,1)}, u32[]{:S(2)}) copy-start(bf16[2048,1024]{1,0:T(8,128)(2,1)} %param.11) | copy-start | bytes 12582916
  167.4 4.9 %collective-permute-start.35 = (bf16[16,1024]{1,0:T(8,128)(2,1)S(1)}, bf16[16,1024]{1,0:T(8,128)(2,1)S(1)}, u32[]{:S(2)}, u32[]{:S(2)}) collective-permute-start(bf16[16,1024]{1,0:T(8,128)(2,1)S(1)} %slice.59), channel_id=1, source_target_pairs={{0,2},{1,3},{2,0},{3,1},{4,6},{5,7},{6,4},{7,5},{8,10},{9,11},{10,... | collective-permute-start | bytes 98312 | tf_op jit(solution)/shard_map/ppermute | solution.py:27
  172.3 4.9 %collective-permute-start.40 = (bf16[16,1024]{1,0:T(8,128)(2,1)S(1)}, bf16[16,1024]{1,0:T(8,128)(2,1)S(1)}, u32[]{:S(2)}, u32[]{:S(2)}) collective-permute-start(bf16[16,1024]{1,0:T(8,128)(2,1)S(1)} %get-tuple-element.47), channel_id=1, source_target_pairs={{0,2},{1,3},{2,0},{3,1},{4,6},{5,7},{6,4},{7,5},{8,10},{9,11},{10,... | collective-permute-start | bytes 98312 | tf_op jit(solution)/shard_map/ppermute | solution.py:27
  174.6 4.8 %collective-permute-start.36 = (bf16[32,1024]{1,0:T(8,128)(2,1)S(1)}, bf16[32,1024]{1,0:T(8,128)(2,1)S(1)}, u32[]{:S(2)}, u32[]{:S(2)}) collective-permute-start(bf16[32,1024]{1,0:T(8,128)(2,1)S(1)} %pad_maximum_fusion.20), channel_id=1, source_target_pairs={{0,1},{1,0},{2,3},{3,2},{4,5},{5,4},{6,7},{7,6},{8,9},{9,8},{10,11... | collective-permute-start | bytes 196616 | tf_op jit(solution)/shard_map/ppermute | solution.py:27
  177.2 4.5 %collective-permute-start.41 = (bf16[32,1024]{1,0:T(8,128)(2,1)S(1)}, bf16[32,1024]{1,0:T(8,128)(2,1)S(1)}, u32[]{:S(2)}, u32[]{:S(2)}) collective-permute-start(bf16[32,1024]{1,0:T(8,128)(2,1)S(1)} %pad_maximum_fusion.21), channel_id=1, source_target_pairs={{0,1},{1,0},{2,3},{3,2},{4,5},{5,4},{6,7},{7,6},{8,9},{9,8},{10,11... | collective-permute-start | bytes 196616 | tf_op jit(solution)/shard_map/ppermute | solution.py:27
  179.5 6.4 %collective-permute-start.37 = (bf16[64,1024]{1,0:T(8,128)(2,1)S(1)}, bf16[64,1024]{1,0:T(8,128)(2,1)S(1)}, u32[]{:S(2)}, u32[]{:S(2)}) collective-permute-start(bf16[64,1024]{1,0:T(8,128)(2,1)S(1)} %pad_maximum_fusion.14), channel_id=1, source_target_pairs={{0,16},{4,20},{8,24},{12,28},{16,0},{20,4},{24,8},{28,12},{1,17},{... | collective-permute-start | bytes 393224 | tf_op jit(solution)/shard_map/ppermute | solution.py:27
  181.7 5.0 %collective-permute-start.42 = (bf16[64,1024]{1,0:T(8,128)(2,1)S(1)}, bf16[64,1024]{1,0:T(8,128)(2,1)S(1)}, u32[]{:S(2)}, u32[]{:S(2)}) collective-permute-start(bf16[64,1024]{1,0:T(8,128)(2,1)S(1)} %pad_maximum_fusion.15), channel_id=1, source_target_pairs={{0,8},{4,12},{8,0},{12,4},{16,24},{20,28},{24,16},{28,20},{1,9},{5... | collective-permute-start | bytes 393224 | tf_op jit(solution)/shard_map/ppermute | solution.py:27
  186.0 6.4 %collective-permute-start.38 = (bf16[128,1024]{1,0:T(8,128)(2,1)S(1)}, bf16[128,1024]{1,0:T(8,128)(2,1)S(1)}, u32[]{:S(2)}, u32[]{:S(2)}) collective-permute-start(bf16[128,1024]{1,0:T(8,128)(2,1)S(1)} %pad_maximum_fusion.9), channel_id=1, source_target_pairs={{0,8},{4,12},{8,0},{12,4},{16,24},{20,28},{24,16},{28,20},{1,9},{5... | collective-permute-start | bytes 786440 | tf_op jit(solution)/shard_map/ppermute | solution.py:27
  186.9 6.4 %collective-permute-start.43 = (bf16[128,1024]{1,0:T(8,128)(2,1)S(1)}, bf16[128,1024]{1,0:T(8,128)(2,1)S(1)}, u32[]{:S(2)}, u32[]{:S(2)}) collective-permute-start(bf16[128,1024]{1,0:T(8,128)(2,1)S(1)} %pad_maximum_fusion.10), channel_id=1, source_target_pairs={{0,16},{4,20},{8,24},{12,28},{16,0},{20,4},{24,8},{28,12},{1,17},{... | collective-permute-start | bytes 786440 | tf_op jit(solution)/shard_map/ppermute | solution.py:27
  192.6 2.0 collective-permute-start.39
  193.5 2.0 collective-permute-start.44
  (5 other events, 26.3 us)

commit v2 on v1

--- a/solution.py
+++ b/solution.py
@@ -11,6 +11,7 @@
 TOLERANCE = 1e-4
 MAX_STEPS = 4096
 REFRESH = 32
+HOLD = 4
 
 
 def bits_of(axis):
@@ -27,29 +28,56 @@
     return lax.ppermute(vals, axis, [(i, i ^ (1 << b)) for i in range(lax.axis_size(axis))])
 
 
-def pick(vals, bit):
-    half = vals.shape[0] // 2
-    return lax.dynamic_slice_in_dim(vals, bit * half, half, 0)
-
-
-def sum_scatter(vals, dims):
-    for dim in dims:
-        bit = my_bit(dim)
-        vals = pick(vals, bit) + swap(pick(vals, 1 - bit), dim)
-    return vals
-
-
-def join(vals, dims):
-    for dim in reversed(dims):
-        other = swap(vals, dim)
-        low = my_bit(dim) == 0
-        vals = jnp.concatenate([jnp.where(low, vals, other), jnp.where(low, other, vals)])
-    return vals
-
-
-def orders():
+def halves(vals, bit):
+    half = vals.shape[1] // 2
+    return tuple(lax.dynamic_slice_in_dim(vals, b * half, half, 1) for b in (bit, 1 - bit))
+
+
+def halve(vals, dim):
+    keep, send = halves(vals, my_bit(dim))
+    return keep + swap(send, dim)
+
+
+def double(vals, dim):
+    other = swap(vals, dim)
+    low = my_bit(dim) == 0
+    return jnp.concatenate([jnp.where(low, vals, other), jnp.where(low, other, vals)], axis=1)
+
+
+def stages():
     state, obs = bits_of("state"), bits_of("obs")
-    return (state + obs, state[:1] + state[1:][::-1] + obs)
+    return state[0], (state[1:], state[1:][::-1]), obs
+
+
+def merged(parts):
+    return parts[0] if len(parts) == 1 else jnp.concatenate(parts)
+
+
+def parted(parts):
+    return parts if len(parts) == 2 else (parts[0][:1], parts[0][1:])
+
+
+def steps_of(exchange):
+    head, middle, tail = stages()
+
+    def both(dim):
+        return lambda parts: (exchange(merged(parts), dim),)
+
+    def each(dims):
+        return lambda parts: tuple(exchange(v, dim) for v, dim in zip(parted(parts), dims, strict=True))
+
+    return [both(head)] + [each(dims) for dims in zip(*middle, strict=True)] + [both(dim) for dim in tail]
+
+
+def join(vals):
+    parts = (vals,)
+    for step in reversed(steps_of(double)):
+        parts = step(parts)
+    return merged(parts)
+
+
+def after(vals, first):
+    return lax.optimization_barrier((vals, first))[0]
 
 
 def tile_starts(members):
@@ -160,7 +188,6 @@
     rows, members = predictions.shape
     capacity = 2 * rows // shards
     me = lax.axis_index(AXES)
-    first, second = orders()
     f32, bf16 = jnp.float32, jnp.bfloat16
     ids = jnp.arange(rows, dtype=jnp.int32)
     shard_ids = jnp.arange(shards, dtype=jnp.int32)
@@ -176,8 +203,9 @@
     got = lax.all_to_all(outgoing.reshape(shards, capacity, members), AXES, split_axis=0, concat_axis=0, tiled=True)
 
     own = jnp.stack([obs_index.astype(f32), noise_var])[None]
-    table = join(own, (bits_of("obs") + bits_of("state"))[::-1])
-    index_table, noise_table = table[:, 0].astype(jnp.int32), table[:, 1]
+    table = lax.all_to_all(jnp.broadcast_to(own, (shards, 2, rows)), AXES, split_axis=0, concat_axis=0, tiled=True)[None]
+    table = after(table, outgoing)
+    index_table, noise_table = table[0, :, 0].astype(jnp.int32), table[0, :, 1]
 
     noise_rows = jnp.dot(by_owner.T.astype(f32), noise_table, precision=lax.Precision.HIGHEST, preferred_element_type=f32)
     noise_here = jnp.sum(jnp.where(slots[:, None] == ids[None, :], noise_rows, 0.0), axis=1, keepdims=True)
@@ -188,10 +216,10 @@
             for j in range(0, members, TILE)
         ]
     )
-    half = tiles.shape[0] // 2
-    gram = jnp.concatenate(
-        [join(sum_scatter(tiles[:half], first), first), join(sum_scatter(tiles[half:], second), second)]
-    )
+    ahead_steps = steps_of(halve) + steps_of(double)[::-1]
+    gram = (tiles.reshape(2, -1, TILE),)
+    for step in ahead_steps[:HOLD]:
+        gram = step(gram)
 
     mine = index_table // rows == me
     mine_ahead = jnp.dot(mine.astype(bf16), earlier, preferred_element_type=f32).astype(jnp.int32)
@@ -207,21 +235,27 @@
     innovation_var = jnp.mean(raw_innov * raw_innov, axis=1)
     innovation = (root_weight * raw_innov).astype(bf16)
 
-    bit = my_bit(first[0])
+    head = stages()[0]
+    bit = my_bit(head)
     quarter = members // 4
 
-    def cross_part(stream, side):
-        cols = lax.dynamic_slice_in_dim(innovation, stream * 2 * quarter + side * quarter, quarter, 1)
-        return jnp.dot(cols.T, anomalies, preferred_element_type=f32)
-
-    sent = [swap(cross_part(s, 1 - bit), first[0]) for s in range(2)]
-    kept = [cross_part(s, bit) for s in range(2)]
-    cross = [
-        sum_scatter(k + g, order[1:]) for k, g, order in zip(kept, sent, (first, second), strict=True)
-    ]
-    each = cross[0].shape[0]
-    gain = solve(gram, jnp.concatenate(cross))
-    gain_t = jnp.concatenate([join(gain[:each], first), join(gain[each:], second)])
+    def cross_part(side):
+        cols = jnp.concatenate([lax.dynamic_slice_in_dim(innovation, (2 * s + side) * quarter, quarter, 1) for s in range(2)], axis=1)
+        return jnp.dot(cols.T, anomalies, preferred_element_type=f32).reshape(2, -1, members)
+
+    later = iter(ahead_steps[HOLD:])
+    gram = next(later)(after(gram, innovation))
+    gram, send = lax.optimization_barrier((gram, cross_part(1 - bit)))
+    cross = (cross_part(bit) + swap(send, head),)
+    gram = next(later)(gram)
+    for step in steps_of(halve)[1:]:
+        gram, cross = lax.optimization_barrier((gram, cross))
+        gram, cross = next(later)(gram), step(cross)
+    for step in later:
+        gram = step(gram)
+    tiles, cross = merged(gram).reshape(-1, TILE), merged(cross)
+    gain = solve(tiles, cross.reshape(-1, members))
+    gain_t = join(gain.reshape(2, -1, members)).reshape(members, members)
 
     block_vals = unknowns.astype(f32)
     spread = (block_vals - jnp.mean(block_vals, axis=1, keepdims=True)).astype(bf16)

time: 204 us -> 184 us (0.902)
  starting transfers between devices: 69.4 us -> 40.5 us
  waiting for transfers between devices: 81.6 us -> 98.2 us
  other arithmetic: 14 us -> 9.66 us
  matrix products: 24.5 us -> 20.6 us
    ppermute x45 -> x28, starting transfers between devices: 63 us -> 29.5 us  [swap(): lax.ppermute(vals, axis, [(i, i ^ 1 << b) for i in range(lax.axis_size(ax...]
    ppermute x45 -> x28, waiting for transfers between devices: 81.6 us -> 91.8 us  [swap(): lax.ppermute(vals, axis, [(i, i ^ 1 << b) for i in range(lax.axis_size(ax...]
    all_to_all x0 -> x1, starting transfers between devices: none -> 7.3 us  [on_device(): lax.all_to_all(jnp.broadcast_to(own, (shards, 2, rows)), AXES, split_axis...]
    all_to_all x1, waiting for transfers between devices: 0.01 us -> 3.5 us  [on_device(): lax.all_to_all(outgoing.reshape(shards, capacity, members), AXES, split_a...]
    all_to_all x0 -> x1, waiting for transfers between devices: none -> 2.84 us  [on_device(): lax.all_to_all(jnp.broadcast_to(own, (shards, 2, rows)), AXES, split_axis...]
    all_to_all x1, starting transfers between devices: 6.41 us -> 3.79 us  [on_device(): lax.all_to_all(outgoing.reshape(shards, capacity, members), AXES, split_a...]
    select_n x25 -> x13, other arithmetic: 3.75 us -> 1.26 us  [double(): jnp.where(low, vals, other)]
    dot_general x4 -> x2, matrix products: 6.65 us -> 4.27 us  [cross_part(): jnp.dot(cols.T, anomalies, preferred_element_type=f32)]
  transfers between devices with their start and end apart: 46 -> 30, of which waited for: 33 -> 24; matrix products, arithmetic and copies ran while one was open for 15% -> 8% of each run, Pallas kernels for 0% -> 0%
where the time goes in v2:
time: 184 us
  waiting for transfers between devices  98.2 us (53%)
  starting transfers between devices  40.5 us (22%)
  matrix products  20.6 us (11%)
  Pallas kernels  10.8 us (6%)
  other arithmetic  9.66 us (5%)
  local copies, waits for them, and re-layouts  2.76 us (2%)
    ppermute x28, waiting for transfers between devices, swap(): lax.ppermute(vals, axis, [(i, i ^ 1 << b) for i in range(lax.axis_size(ax...  91.8 us
    ppermute x28, starting transfers between devices, swap(): lax.ppermute(vals, axis, [(i, i ^ 1 << b) for i in range(lax.axis_size(ax...  29.5 us
    pallas_call x1, Pallas kernels, solve(): pl.pallas_call(solve_kernel, out_shape=jax.ShapeDtypeStruct(rhs.shape, jn...  10.8 us
    all_to_all x1, starting transfers between devices, on_device(): lax.all_to_all(jnp.broadcast_to(own, (shards, 2, rows)), AXES, split_axis...  7.3 us
    dot_general x1, matrix products, on_device(): lax.dot_general(spread, gain_t, (((1,), (1,)), ((), ())), preferred_eleme...  6.63 us
    dot_general x2, matrix products, cross_part(): jnp.dot(cols.T, anomalies, preferred_element_type=f32)  4.27 us
    dot_general x1, matrix products, on_device(): jnp.dot(pack, predictions, preferred_element_type=f32).astype(bf16)  3.89 us
    all_to_all x1, starting transfers between devices, on_device(): lax.all_to_all(outgoing.reshape(shards, capacity, members), AXES, split_a...  3.79 us
  transfers between devices with their start and end apart: 30, of which 24 were waited for; matrix products, arithmetic and copies ran while one was open for 8% of the time, Pallas kernels for 0%

profile of v2, /device:TPU:0, one launch (start us, length us, event | category | flops | bytes accessed | tf_op | source)
XLA Modules:
  0.0 183.9 jit_solution(8815760033751515697)
XLA Ops:
  2.8 7.3 %all-to-all-start = ((f32[32,2,512]{2,1,0:T(2,128)}), f32[32,2,512]{2,1,0:T(2,128)S(1)}, u32[]{:S(2)}, u32[]{:S(2)}) async-start(f32[32,2,512]{2,1,0:T(2,128)} %broadcast_in_dim.16), calls=%async_computation | async-start | bytes 262144 | tf_op jit(solution)/shard_map/all_to_all | solution.py:206
  10.3 1.4 convert_reduce_fusion.2
  11.8 3.9 %fusion.14 = bf16[1024,1024]{1,0:T(8,128)(2,1)} fusion(bf16[512,1024]{1,0:T(8,128)(2,1)} %param.6, s32[512]{0:T(512)S(1)} %convert_add_fusion.1), kind=kOutput, calls=%fused_computation.28 | convolution fusion | flops 1075314688 | bytes 3147776 | tf_op jit(solution)/shard_map/dot_general | solution.py:202
  15.6 2.8 %all-to-all-done = f32[32,2,512]{2,1,0:T(2,128)S(1)} async-done(((f32[32,2,512]{2,1,0:T(2,128)}), f32[32,2,512]{2,1,0:T(2,128)S(1)}, u32[]{:S(2)}, u32[]{:S(2)}) %all-to-all-start) | async-done | bytes 131104 | tf_op jit(solution)/shard_map/all_to_all | solution.py:206
  21.3 1.2 constant_dynamic-slice_fusion.15
  22.5 3.8 %all-to-all-start.1 = ((bf16[32,32,1024]{2,1,0:T(8,128)(2,1)}), bf16[32,32,1024]{2,1,0:T(8,128)(2,1)}, u32[]{:S(2)}, u32[]{:S(2)}) async-start(bf16[32,32,1024]{2,1,0:T(8,128)(2,1)} %bitcast.53), calls=%async_computation.1 | async-start | bytes 4194304 | tf_op jit(solution)/shard_map/all_to_all | solution.py:203
  26.4 1.5 dynamic-slice_add_fusion
  28.1 1.5 collective-permute-start.1
  30.4 1.6 collective-permute-start.3
  32.0 19.4 %collective-permute-done.1 = f32[1,320,256]{2,1,0:T(8,128)S(1)} collective-permute-done((f32[1,320,256]{2,1,0:T(8,128)S(1)}, f32[1,320,256]{2,1,0:T(8,128)S(1)}, u32[]{:S(2)}, u32[]{:S(2)}) %collective-permute-start.1) | collective-permute-done | bytes 327712 | tf_op jit(solution)/shard_map/ppermute | solution.py:28
  51.4 1.6 collective-permute-start.2
  53.4 5.3 %collective-permute-done.2 = f32[1,160,256]{2,1,0:T(8,128)S(1)} collective-permute-done((f32[1,160,256]{2,1,0:T(8,128)S(1)}, f32[1,160,256]{2,1,0:T(8,128)S(1)}, u32[]{:S(2)}, u32[]{:S(2)}) %collective-permute-start.2) | collective-permute-done | bytes 163872 | tf_op jit(solution)/shard_map/ppermute | solution.py:28
  58.7 1.2 collective-permute-done.4
  60.0 2.9 %collective-permute-start.5 = (f32[2,80,256]{2,1,0:T(8,128)S(1)}, f32[2,80,256]{2,1,0:T(8,128)S(1)}, u32[]{:S(2)}, u32[]{:S(2)}) collective-permute-start(f32[2,80,256]{2,1,0:T(8,128)S(1)} %fusion.38), channel_id=1, source_target_pairs={{0,1},{1,0},{2,3},{3,2},{4,5},{5,4},{6,7},{7,6},{8,9},{9,8},{10,11... | collective-permute-start | bytes 491528 | tf_op jit(solution)/shard_map/ppermute | solution.py:28
  62.9 7.0 %collective-permute-done.5 = f32[2,80,256]{2,1,0:T(8,128)S(1)} collective-permute-done((f32[2,80,256]{2,1,0:T(8,128)S(1)}, f32[2,80,256]{2,1,0:T(8,128)S(1)}, u32[]{:S(2)}, u32[]{:S(2)}) %collective-permute-start.5) | collective-permute-done | bytes 163872 | tf_op jit(solution)/shard_map/ppermute | solution.py:28
  70.0 3.5 %all-to-all-done.1 = bf16[32,32,1024]{2,1,0:T(8,128)(2,1)} async-done(((bf16[32,32,1024]{2,1,0:T(8,128)(2,1)}), bf16[32,32,1024]{2,1,0:T(8,128)(2,1)}, u32[]{:S(2)}, u32[]{:S(2)}) %all-to-all-start.1) | async-done | bytes 2097184 | tf_op jit(solution)/shard_map/all_to_all | solution.py:203
  73.5 3.2 %multiply_reduce_fusion = (f32[512]{0:T(512)S(1)}, f32[512]{0:T(512)S(1)}, bf16[512,1024]{1,0:T(8,128)(2,1)S(1)}, bf16[512,1024]{1,0:T(8,128)(2,1)S(1)}) fusion(bf16[512,1024]{1,0:T(8,128)(2,1)S(1)} %copy-done.3, f32[512]{0:T(512)S(1)} %copy-done.4, f32[512]{0:T(512)S(1)} %divide_sqrt_fusion, bf16[1024,1024]{1,0:T(8,128)(2,1)} %bitcast.5, s32[1024]{0:T(1024)S(1)} %sub.80), kind=kOutput, calls=%fused_computation.19 | convolution fusion | flops 1079507968 | bytes 5255168 | tf_op jit(solution)/shard_map/dot_general | solution.py:229
  76.8 2.3 %collective-permute-start.6 = (f32[2,40,256]{2,1,0:T(8,128)S(1)}, f32[2,40,256]{2,1,0:T(8,128)S(1)}, u32[]{:S(2)}, u32[]{:S(2)}) collective-permute-start(f32[2,40,256]{2,1,0:T(8,128)S(1)} %constant_dynamic-slice_fusion.9), channel_id=1, source_target_pairs={{0,2},{1,3},{2,0},{3,1},{4,6},{5,7},{6,4},{7,5},{8,10},{9,11},{10,... | collective-permute-start | bytes 245768 | tf_op jit(solution)/shard_map/ppermute | solution.py:28
  79.8 2.2 %fusion.24 = f32[512,1024]{1,0:T(8,128)} fusion(bf16[512,256]{1,0:T(8,128)(2,1)S(1)} %get-tuple-element.47, bf16[512,256]{1,0:T(8,128)(2,1)S(1)} %get-tuple-element.48, bf16[512,1024]{1,0:T(8,128)(2,1)S(1)} %get-tuple-element.84, f32[512]{0:T(512)S(1)} %get-tuple-element.88, f32[512]{0:T(512)S(1)} %divide_sqrt_fusion), kind=kOutput, calls=%fused_computation.51 | convolution fusion | flops 540016640 | bytes 3674112 | tf_op jit(solution)/shard_map/dot_general | solution.py:244
  82.0 1.8 collective-permute-done.6
  84.9 2.1 %fusion.28 = f32[512,1024]{1,0:T(8,128)S(1)} fusion(bf16[512,256]{1,0:T(8,128)(2,1)S(1)} %get-tuple-element.46, bf16[512,256]{1,0:T(8,128)(2,1)S(1)} %get-tuple-element.45, bf16[512,1024]{1,0:T(8,128)(2,1)} %copy-done.5, f32[512]{0:T(512)S(1)} %get-tuple-element.88, f32[512]{0:T(512)S(1)} %divide_sqrt_fusion), kind=kOutput, calls=%fused_computation.55 | convolution fusion | flops 540016640 | bytes 3674112 | tf_op jit(solution)/shard_map/dot_general | solution.py:244
  87.0 4.4 %collective-permute-done.7 = f32[2,40,256]{2,1,0:T(8,128)S(1)} collective-permute-done((f32[2,40,256]{2,1,0:T(8,128)S(1)}, f32[2,40,256]{2,1,0:T(8,128)S(1)}, u32[]{:S(2)}, u32[]{:S(2)}) %collective-permute-start.7) | collective-permute-done | bytes 81952 | tf_op jit(solution)/shard_map/ppermute | solution.py:28
  92.2 1.5 collective-permute-start.10
  93.7 1.4 collective-permute-start.11
  95.1 2.5 %collective-permute-done.9 = f32[2,80,256]{2,1,0:T(8,128)S(1)} collective-permute-done((f32[2,80,256]{2,1,0:T(8,128)S(1)}, f32[2,80,256]{2,1,0:T(8,128)S(1)}, u32[]{:S(2)}, u32[]{:S(2)}) %collective-permute-start.9) | collective-permute-done | bytes 163872 | tf_op jit(solution)/shard_map/ppermute | solution.py:28
  97.7 8.0 %collective-permute-done.10 = f32[1,128,1024]{2,1,0:T(8,128)S(1)} collective-permute-done((f32[1,128,1024]{2,1,0:T(8,128)S(1)}, f32[1,128,1024]{2,1,0:T(8,128)S(1)}, u32[]{:S(2)}, u32[]{:S(2)}) %collective-permute-start.10) | collective-permute-done | bytes 524320 | tf_op jit(solution)/shard_map/ppermute | solution.py:28
  105.8 1.5 collective-permute-done.11
  108.1 1.7 collective-permute-start.12
  110.2 1.5 collective-permute-start.15
  111.7 2.8 %collective-permute-done.13 = f32[1,160,256]{2,1,0:T(8,128)S(1)} collective-permute-done((f32[1,160,256]{2,1,0:T(8,128)S(1)}, f32[1,160,256]{2,1,0:T(8,128)S(1)}, u32[]{:S(2)}, u32[]{:S(2)}) %collective-permute-start.13) | collective-permute-done | bytes 163872 | tf_op jit(solution)/shard_map/ppermute | solution.py:28
  115.3 3.1 %collective-permute-done.14 = f32[1,64,1024]{2,1,0:T(8,128)S(1)} collective-permute-done((f32[1,64,1024]{2,1,0:T(8,128)S(1)}, f32[1,64,1024]{2,1,0:T(8,128)S(1)}, u32[]{:S(2)}, u32[]{:S(2)}) %collective-permute-start.14) | collective-permute-done | bytes 262176 | tf_op jit(solution)/shard_map/ppermute | solution.py:28
  118.6 1.5 collective-permute-start.18
  120.1 1.3 collective-permute-start.16
  121.4 1.5 collective-permute-start.17
  122.9 2.1 %collective-permute-done.18 = f32[2,32,1024]{2,1,0:T(8,128)S(1)} collective-permute-done((f32[2,32,1024]{2,1,0:T(8,128)S(1)}, f32[2,32,1024]{2,1,0:T(8,128)S(1)}, u32[]{:S(2)}, u32[]{:S(2)}) %collective-permute-start.18) | collective-permute-done | bytes 262176 | tf_op jit(solution)/shard_map/ppermute | solution.py:28
  125.1 2.3 %collective-permute-done.16 = f32[1,320,256]{2,1,0:T(8,128)S(1)} collective-permute-done((f32[1,320,256]{2,1,0:T(8,128)S(1)}, f32[1,320,256]{2,1,0:T(8,128)S(1)}, u32[]{:S(2)}, u32[]{:S(2)}) %collective-permute-start.16) | collective-permute-done | bytes 327712 | tf_op jit(solution)/shard_map/ppermute | solution.py:28
  127.4 1.0 collective-permute-done.17
  128.8 1.3 collective-permute-start.20
  130.1 8.3 %collective-permute-done.20 = f32[2,16,1024]{2,1,0:T(8,128)S(1)} collective-permute-done((f32[2,16,1024]{2,1,0:T(8,128)S(1)}, f32[2,16,1024]{2,1,0:T(8,128)S(1)}, u32[]{:S(2)}, u32[]{:S(2)}) %collective-permute-start.20) | collective-permute-done | bytes 131104 | tf_op jit(solution)/shard_map/ppermute | solution.py:28
  138.8 10.8 %member_solve.1 = bf16[32,1024]{1,0:T(8,128)(2,1)S(1)} custom-call(f32[2560,256]{1,0:T(8,128)S(1)} %bitcast.46, f32[32,1024]{1,0:T(8,128)S(1)} %bitcast.47), custom_call_target="tpu_custom_call" | custom-call | flops 2415919104 | bytes 6291456 | tf_op jit(solution)/shard_map/member_solve/pallas_call | solution.py:169
  149.7 5.7 %collective-permute-done.21 = bf16[2,16,1024]{2,1,0:T(8,128)(2,1)S(1)} collective-permute-done((bf16[2,16,1024]{2,1,0:T(8,128)(2,1)S(1)}, bf16[2,16,1024]{2,1,0:T(8,128)(2,1)S(1)}, u32[]{:S(2)}, u32[]{:S(2)}) %collective-permute-start.21) | collective-permute-done | bytes 65568 | tf_op jit(solution)/shard_map/ppermute | solution.py:28
  155.5 5.4 %collective-permute-done.22 = bf16[2,32,1024]{2,1,0:T(8,128)(2,1)S(1)} collective-permute-done((bf16[2,32,1024]{2,1,0:T(8,128)(2,1)S(1)}, bf16[2,32,1024]{2,1,0:T(8,128)(2,1)S(1)}, u32[]{:S(2)}, u32[]{:S(2)}) %collective-permute-start.22) | collective-permute-done | bytes 131104 | tf_op jit(solution)/shard_map/ppermute | solution.py:28
  161.3 1.7 collective-permute-start.23
  163.1 2.9 %collective-permute-done.25 = bf16[1,64,1024]{2,1,0:T(8,128)(2,1)S(1)} collective-permute-done((bf16[1,64,1024]{2,1,0:T(8,128)(2,1)S(1)}, bf16[1,64,1024]{2,1,0:T(8,128)(2,1)S(1)}, u32[]{:S(2)}, u32[]{:S(2)}) %collective-permute-start.25) | collective-permute-done | bytes 131104 | tf_op jit(solution)/shard_map/ppermute | solution.py:28
  166.8 2.4 %collective-permute-start.24 = (bf16[1,128,1024]{2,1,0:T(8,128)(2,1)S(1)}, bf16[1,128,1024]{2,1,0:T(8,128)(2,1)S(1)}, u32[]{:S(2)}, u32[]{:S(2)}) collective-permute-start(bf16[1,128,1024]{2,1,0:T(8,128)(2,1)S(1)} %pad_maximum_fusion.8), channel_id=1, source_target_pairs={{0,8},{4,12},{8,0},{12,4},{16,24},{20,28},{24,16},{28,20},{1,9},{5... | collective-permute-start | bytes 786440 | tf_op jit(solution)/shard_map/ppermute | solution.py:28
  169.2 3.3 %collective-permute-done.26 = bf16[1,128,1024]{2,1,0:T(8,128)(2,1)S(1)} collective-permute-done((bf16[1,128,1024]{2,1,0:T(8,128)(2,1)S(1)}, bf16[1,128,1024]{2,1,0:T(8,128)(2,1)S(1)}, u32[]{:S(2)}, u32[]{:S(2)}) %collective-permute-start.26) | collective-permute-done | bytes 262176 | tf_op jit(solution)/shard_map/ppermute | solution.py:28
  174.5 2.0 %collective-permute-done.27 = bf16[2,256,1024]{2,1,0:T(8,128)(2,1)S(1)} collective-permute-done((bf16[2,256,1024]{2,1,0:T(8,128)(2,1)S(1)}, bf16[2,256,1024]{2,1,0:T(8,128)(2,1)S(1)}, u32[]{:S(2)}, u32[]{:S(2)}) %collective-permute-start.27) | collective-permute-done | bytes 1048608 | tf_op jit(solution)/shard_map/ppermute | solution.py:28
  177.2 6.6 %fusion.1 = bf16[2048,1024]{1,0:T(8,128)(2,1)} fusion(bf16[2048,1024]{1,0:T(8,128)(2,1)S(1)} %copy-done, bf16[1024,1024]{1,0:T(8,128)(2,1)S(1)} %bitcast.54, f32[2048]{0:T(1024)S(1)} %broadcast_multiply_fusion), kind=kOutput, calls=%fused_computation.4 | convolution fusion | flops 4307550208 | bytes 10493952 | tf_op jit(solution)/shard_map/dot_general | solution.py:262
  (116 shorter events, 16.3 us)
Async XLA Ops:
  2.8 15.7 %all-to-all-start = ((f32[32,2,512]{2,1,0:T(2,128)}), f32[32,2,512]{2,1,0:T(2,128)S(1)}, u32[]{:S(2)}, u32[]{:S(2)}) async-start(f32[32,2,512]{2,1,0:T(2,128)} %broadcast_in_dim.16), calls=%async_computation | async-start | bytes 262144 | tf_op jit(solution)/shard_map/all_to_all | solution.py:206
  11.7 7.5 %copy-start.1 = (bf16[512,1024]{1,0:T(8,128)(2,1)S(1)}, bf16[512,1024]{1,0:T(8,128)(2,1)}, u32[]{:S(2)}) copy-start(bf16[512,1024]{1,0:T(8,128)(2,1)} %param.6) | copy-start | bytes 3145732
  22.5 4.0 %collective-permute-start = (f32[2,640,256]{2,1,0:T(8,128)}, f32[2,640,256]{2,1,0:T(8,128)}, u32[]{:S(2)}, u32[]{:S(2)}) collective-permute-start(f32[2,640,256]{2,1,0:T(8,128)} %constant_dynamic-slice_fusion.15), channel_id=1, source_target_pairs={{0,4},{4,0},{8,12},{12,8},{16,20},{20,16},{24,28},{28,24},{1,5},{5... | collective-permute-start | bytes 3932168 | tf_op jit(solution)/shard_map/ppermute | solution.py:28
  22.5 3.8 %copy-start.2 = (f32[512]{0:T(512)S(1)}, f32[512]{0:T(512)}, u32[]{:S(2)}) copy-start(f32[512]{0:T(512)} %param.9) | copy-start | bytes 6148
  22.5 51.0 %all-to-all-start.1 = ((bf16[32,32,1024]{2,1,0:T(8,128)(2,1)}), bf16[32,32,1024]{2,1,0:T(8,128)(2,1)}, u32[]{:S(2)}, u32[]{:S(2)}) async-start(bf16[32,32,1024]{2,1,0:T(8,128)(2,1)} %bitcast.53), calls=%async_computation.1 | async-start | bytes 4194304 | tf_op jit(solution)/shard_map/all_to_all | solution.py:203
  28.1 23.3 %collective-permute-start.1 = (f32[1,320,256]{2,1,0:T(8,128)S(1)}, f32[1,320,256]{2,1,0:T(8,128)S(1)}, u32[]{:S(2)}, u32[]{:S(2)}) collective-permute-start(f32[1,320,256]{2,1,0:T(8,128)S(1)} %constant_dynamic-slice_fusion.14), channel_id=1, source_target_pairs={{0,8},{4,12},{8,0},{12,4},{16,24},{20,28},{24,16},{28,20},{1,9},{5... | collective-permute-start | bytes 983048 | tf_op jit(solution)/shard_map/ppermute | solution.py:28
  30.4 22.6 %collective-permute-start.3 = (f32[1,320,256]{2,1,0:T(8,128)S(1)}, f32[1,320,256]{2,1,0:T(8,128)S(1)}, u32[]{:S(2)}, u32[]{:S(2)}) collective-permute-start(f32[1,320,256]{2,1,0:T(8,128)S(1)} %constant_dynamic-slice_fusion.12), channel_id=1, source_target_pairs={{0,16},{4,20},{8,24},{12,28},{16,0},{20,4},{24,8},{28,12},{1,17},{... | collective-permute-start | bytes 983048 | tf_op jit(solution)/shard_map/ppermute | solution.py:28
  51.4 22.1 %copy-start.3 = (bf16[512,1024]{1,0:T(8,128)(2,1)S(1)}, bf16[512,1024]{1,0:T(8,128)(2,1)}, u32[]{:S(2)}) copy-start(bf16[512,1024]{1,0:T(8,128)(2,1)} %param.10) | copy-start | bytes 3145732
  51.4 22.1 %copy-start.4 = (f32[512]{0:T(512)S(1)}, f32[512]{0:T(512)}, u32[]{:S(2)}) copy-start(f32[512]{0:T(512)} %param.8) | copy-start | bytes 6148
  51.4 7.3 %collective-permute-start.2 = (f32[1,160,256]{2,1,0:T(8,128)S(1)}, f32[1,160,256]{2,1,0:T(8,128)S(1)}, u32[]{:S(2)}, u32[]{:S(2)}) collective-permute-start(f32[1,160,256]{2,1,0:T(8,128)S(1)} %constant_dynamic-slice_fusion.13), channel_id=1, source_target_pairs={{0,16},{4,20},{8,24},{12,28},{16,0},{20,4},{24,8},{28,12},{1,17},{... | collective-permute-start | bytes 491528 | tf_op jit(solution)/shard_map/ppermute | solution.py:28
  53.1 6.9 %collective-permute-start.4 = (f32[1,160,256]{2,1,0:T(8,128)S(1)}, f32[1,160,256]{2,1,0:T(8,128)S(1)}, u32[]{:S(2)}, u32[]{:S(2)}) collective-permute-start(f32[1,160,256]{2,1,0:T(8,128)S(1)} %constant_dynamic-slice_fusion.11), channel_id=1, source_target_pairs={{0,8},{4,12},{8,0},{12,4},{16,24},{20,28},{24,16},{28,20},{1,9},{5... | collective-permute-start | bytes 491528 | tf_op jit(solution)/shard_map/ppermute | solution.py:28
  60.0 10.0 %collective-permute-start.5 = (f32[2,80,256]{2,1,0:T(8,128)S(1)}, f32[2,80,256]{2,1,0:T(8,128)S(1)}, u32[]{:S(2)}, u32[]{:S(2)}) collective-permute-start(f32[2,80,256]{2,1,0:T(8,128)S(1)} %fusion.38), channel_id=1, source_target_pairs={{0,1},{1,0},{2,3},{3,2},{4,5},{5,4},{6,7},{7,6},{8,9},{9,8},{10,11... | collective-permute-start | bytes 491528 | tf_op jit(solution)/shard_map/ppermute | solution.py:28
  76.7 7.1 %copy-start.5 = (bf16[512,1024]{1,0:T(8,128)(2,1)}, bf16[512,1024]{1,0:T(8,128)(2,1)S(1)}, u32[]{:S(2)}) copy-start(bf16[512,1024]{1,0:T(8,128)(2,1)S(1)} %get-tuple-element.84) | copy-start | bytes 3145732
  76.8 7.1 %collective-permute-start.6 = (f32[2,40,256]{2,1,0:T(8,128)S(1)}, f32[2,40,256]{2,1,0:T(8,128)S(1)}, u32[]{:S(2)}, u32[]{:S(2)}) collective-permute-start(f32[2,40,256]{2,1,0:T(8,128)S(1)} %constant_dynamic-slice_fusion.9), channel_id=1, source_target_pairs={{0,2},{1,3},{2,0},{3,1},{4,6},{5,7},{6,4},{7,5},{8,10},{9,11},{10,... | collective-permute-start | bytes 245768 | tf_op jit(solution)/shard_map/ppermute | solution.py:28
  83.8 7.6 %collective-permute-start.8 = (f32[2,256,1024]{2,1,0:T(8,128)}, f32[2,256,1024]{2,1,0:T(8,128)S(1)}, u32[]{:S(2)}, u32[]{:S(2)}) collective-permute-start(f32[2,256,1024]{2,1,0:T(8,128)} %bitcast.6), channel_id=1, source_target_pairs={{0,4},{4,0},{8,12},{12,8},{16,20},{20,16},{24,28},{28,24},{1,5},{5... | collective-permute-start | bytes 6291464 | tf_op jit(solution)/shard_map/ppermute | solution.py:28
  84.0 7.4 %collective-permute-start.7 = (f32[2,40,256]{2,1,0:T(8,128)S(1)}, f32[2,40,256]{2,1,0:T(8,128)S(1)}, u32[]{:S(2)}, u32[]{:S(2)}) collective-permute-start(f32[2,40,256]{2,1,0:T(8,128)S(1)} %dynamic-slice_add_fusion.11), channel_id=1, source_target_pairs={{0,2},{1,3},{2,0},{3,1},{4,6},{5,7},{6,4},{7,5},{8,10},{9,11},{10,... | collective-permute-start | bytes 245768 | tf_op jit(solution)/shard_map/ppermute | solution.py:28
  91.9 5.7 %collective-permute-start.9 = (f32[2,80,256]{2,1,0:T(8,128)S(1)}, f32[2,80,256]{2,1,0:T(8,128)S(1)}, u32[]{:S(2)}, u32[]{:S(2)}) collective-permute-start(f32[2,80,256]{2,1,0:T(8,128)S(1)} %pad_maximum_fusion.10), channel_id=1, source_target_pairs={{0,1},{1,0},{2,3},{3,2},{4,5},{5,4},{6,7},{7,6},{8,9},{9,8},{10,11... | collective-permute-start | bytes 491528 | tf_op jit(solution)/shard_map/ppermute | solution.py:28
  92.2 13.5 %collective-permute-start.10 = (f32[1,128,1024]{2,1,0:T(8,128)S(1)}, f32[1,128,1024]{2,1,0:T(8,128)S(1)}, u32[]{:S(2)}, u32[]{:S(2)}) collective-permute-start(f32[1,128,1024]{2,1,0:T(8,128)S(1)} %constant_dynamic-slice_fusion.4), channel_id=1, source_target_pairs={{0,8},{4,12},{8,0},{12,4},{16,24},{20,28},{24,16},{28,20},{1,9},{5... | collective-permute-start | bytes 1572872 | tf_op jit(solution)/shard_map/ppermute | solution.py:28
  93.7 13.6 %collective-permute-start.11 = (f32[1,128,1024]{2,1,0:T(8,128)S(1)}, f32[1,128,1024]{2,1,0:T(8,128)S(1)}, u32[]{:S(2)}, u32[]{:S(2)}) collective-permute-start(f32[1,128,1024]{2,1,0:T(8,128)S(1)} %constant_dynamic-slice_fusion.3), channel_id=1, source_target_pairs={{0,16},{4,20},{8,24},{12,28},{16,0},{20,4},{24,8},{28,12},{1,17},{... | collective-permute-start | bytes 1572872 | tf_op jit(solution)/shard_map/ppermute | solution.py:28
  107.4 7.1 %collective-permute-start.13 = (f32[1,160,256]{2,1,0:T(8,128)S(1)}, f32[1,160,256]{2,1,0:T(8,128)S(1)}, u32[]{:S(2)}, u32[]{:S(2)}) collective-permute-start(f32[1,160,256]{2,1,0:T(8,128)S(1)} %get-tuple-element.63), channel_id=1, source_target_pairs={{0,8},{4,12},{8,0},{12,4},{16,24},{20,28},{24,16},{28,20},{1,9},{5... | collective-permute-start | bytes 491528 | tf_op jit(solution)/shard_map/ppermute | solution.py:28
  108.1 7.1 %collective-permute-start.12 = (f32[1,160,256]{2,1,0:T(8,128)S(1)}, f32[1,160,256]{2,1,0:T(8,128)S(1)}, u32[]{:S(2)}, u32[]{:S(2)}) collective-permute-start(f32[1,160,256]{2,1,0:T(8,128)S(1)} %get-tuple-element.64), channel_id=1, source_target_pairs={{0,16},{4,20},{8,24},{12,28},{16,0},{20,4},{24,8},{28,12},{1,17},{... | collective-permute-start | bytes 491528 | tf_op jit(solution)/shard_map/ppermute | solution.py:28
  109.8 8.6 %collective-permute-start.14 = (f32[1,64,1024]{2,1,0:T(8,128)S(1)}, f32[1,64,1024]{2,1,0:T(8,128)S(1)}, u32[]{:S(2)}, u32[]{:S(2)}) collective-permute-start(f32[1,64,1024]{2,1,0:T(8,128)S(1)} %constant_dynamic-slice_fusion.2), channel_id=1, source_target_pairs={{0,16},{4,20},{8,24},{12,28},{16,0},{20,4},{24,8},{28,12},{1,17},{... | collective-permute-start | bytes 786440 | tf_op jit(solution)/shard_map/ppermute | solution.py:28
  110.2 8.2 %collective-permute-start.15 = (f32[1,64,1024]{2,1,0:T(8,128)S(1)}, f32[1,64,1024]{2,1,0:T(8,128)S(1)}, u32[]{:S(2)}, u32[]{:S(2)}) collective-permute-start(f32[1,64,1024]{2,1,0:T(8,128)S(1)} %constant_dynamic-slice_fusion.1), channel_id=1, source_target_pairs={{0,8},{4,12},{8,0},{12,4},{16,24},{20,28},{24,16},{28,20},{1,9},{5... | collective-permute-start | bytes 786440 | tf_op jit(solution)/shard_map/ppermute | solution.py:28
  118.6 6.4 %collective-permute-start.18 = (f32[2,32,1024]{2,1,0:T(8,128)S(1)}, f32[2,32,1024]{2,1,0:T(8,128)S(1)}, u32[]{:S(2)}, u32[]{:S(2)}) collective-permute-start(f32[2,32,1024]{2,1,0:T(8,128)S(1)} %constant_dynamic-slice_fusion), channel_id=1, source_target_pairs={{0,1},{1,0},{2,3},{3,2},{4,5},{5,4},{6,7},{7,6},{8,9},{9,8},{10,11... | collective-permute-start | bytes 786440 | tf_op jit(solution)/shard_map/ppermute | solution.py:28
  120.1 7.3 %collective-permute-start.16 = (f32[1,320,256]{2,1,0:T(8,128)S(1)}, f32[1,320,256]{2,1,0:T(8,128)S(1)}, u32[]{:S(2)}, u32[]{:S(2)}) collective-permute-start(f32[1,320,256]{2,1,0:T(8,128)S(1)} %pad_maximum_fusion.6), channel_id=1, source_target_pairs={{0,8},{4,12},{8,0},{12,4},{16,24},{20,28},{24,16},{28,20},{1,9},{5... | collective-permute-start | bytes 983048 | tf_op jit(solution)/shard_map/ppermute | solution.py:28
  121.4 7.1 %collective-permute-start.17 = (f32[1,320,256]{2,1,0:T(8,128)S(1)}, f32[1,320,256]{2,1,0:T(8,128)S(1)}, u32[]{:S(2)}, u32[]{:S(2)}) collective-permute-start(f32[1,320,256]{2,1,0:T(8,128)S(1)} %pad_maximum_fusion.7), channel_id=1, source_target_pairs={{0,16},{4,20},{8,24},{12,28},{16,0},{20,4},{24,8},{28,12},{1,17},{... | collective-permute-start | bytes 983048 | tf_op jit(solution)/shard_map/ppermute | solution.py:28
  128.7 9.8 %collective-permute-start.19 = (f32[2,640,256]{2,1,0:T(8,128)S(1)}, f32[2,640,256]{2,1,0:T(8,128)S(1)}, u32[]{:S(2)}, u32[]{:S(2)}) collective-permute-start(f32[2,640,256]{2,1,0:T(8,128)S(1)} %constant_dynamic-update-slice_fusion.2), channel_id=1, source_target_pairs={{0,4},{4,0},{8,12},{12,8},{16,20},{20,16},{24,28},{28,24},{1,5},{5... | collective-permute-start | bytes 3932168 | tf_op jit(solution)/shard_map/ppermute | solution.py:28
  128.8 9.7 %collective-permute-start.20 = (f32[2,16,1024]{2,1,0:T(8,128)S(1)}, f32[2,16,1024]{2,1,0:T(8,128)S(1)}, u32[]{:S(2)}, u32[]{:S(2)}) collective-permute-start(f32[2,16,1024]{2,1,0:T(8,128)S(1)} %constant_dynamic-slice_fusion.10), channel_id=1, source_target_pairs={{0,2},{1,3},{2,0},{3,1},{4,6},{5,7},{6,4},{7,5},{8,10},{9,11},{10,... | collective-permute-start | bytes 393224 | tf_op jit(solution)/shard_map/ppermute | solution.py:28
  149.6 5.8 %collective-permute-start.21 = (bf16[2,16,1024]{2,1,0:T(8,128)(2,1)S(1)}, bf16[2,16,1024]{2,1,0:T(8,128)(2,1)S(1)}, u32[]{:S(2)}, u32[]{:S(2)}) collective-permute-start(bf16[2,16,1024]{2,1,0:T(8,128)(2,1)S(1)} %bitcast.48), channel_id=1, source_target_pairs={{0,2},{1,3},{2,0},{3,1},{4,6},{5,7},{6,4},{7,5},{8,10},{9,11},{10,... | collective-permute-start | bytes 196616 | tf_op jit(solution)/shard_map/ppermute | solution.py:28
  155.4 5.4 %collective-permute-start.22 = (bf16[2,32,1024]{2,1,0:T(8,128)(2,1)S(1)}, bf16[2,32,1024]{2,1,0:T(8,128)(2,1)S(1)}, u32[]{:S(2)}, u32[]{:S(2)}) collective-permute-start(bf16[2,32,1024]{2,1,0:T(8,128)(2,1)S(1)} %pad_maximum_fusion.12), channel_id=1, source_target_pairs={{0,1},{1,0},{2,3},{3,2},{4,5},{5,4},{6,7},{7,6},{8,9},{9,8},{10,11... | collective-permute-start | bytes 393224 | tf_op jit(solution)/shard_map/ppermute | solution.py:28
  161.0 5.0 %collective-permute-start.25 = (bf16[1,64,1024]{2,1,0:T(8,128)(2,1)S(1)}, bf16[1,64,1024]{2,1,0:T(8,128)(2,1)S(1)}, u32[]{:S(2)}, u32[]{:S(2)}) collective-permute-start(bf16[1,64,1024]{2,1,0:T(8,128)(2,1)S(1)} %get-tuple-element.70), channel_id=1, source_target_pairs={{0,8},{4,12},{8,0},{12,4},{16,24},{20,28},{24,16},{28,20},{1,9},{5... | collective-permute-start | bytes 393224 | tf_op jit(solution)/shard_map/ppermute | solution.py:28
  161.3 5.4 %collective-permute-start.23 = (bf16[1,64,1024]{2,1,0:T(8,128)(2,1)S(1)}, bf16[1,64,1024]{2,1,0:T(8,128)(2,1)S(1)}, u32[]{:S(2)}, u32[]{:S(2)}) collective-permute-start(bf16[1,64,1024]{2,1,0:T(8,128)(2,1)S(1)} %get-tuple-element.69), channel_id=1, source_target_pairs={{0,16},{4,20},{8,24},{12,28},{16,0},{20,4},{24,8},{28,12},{1,17},{... | collective-permute-start | bytes 393224 | tf_op jit(solution)/shard_map/ppermute | solution.py:28
  166.1 6.4 %collective-permute-start.26 = (bf16[1,128,1024]{2,1,0:T(8,128)(2,1)S(1)}, bf16[1,128,1024]{2,1,0:T(8,128)(2,1)S(1)}, u32[]{:S(2)}, u32[]{:S(2)}) collective-permute-start(bf16[1,128,1024]{2,1,0:T(8,128)(2,1)S(1)} %pad_maximum_fusion.9), channel_id=1, source_target_pairs={{0,16},{4,20},{8,24},{12,28},{16,0},{20,4},{24,8},{28,12},{1,17},{... | collective-permute-start | bytes 786440 | tf_op jit(solution)/shard_map/ppermute | solution.py:28
  166.8 7.1 %copy-start = (bf16[2048,1024]{1,0:T(8,128)(2,1)S(1)}, bf16[2048,1024]{1,0:T(8,128)(2,1)}, u32[]{:S(2)}) copy-start(bf16[2048,1024]{1,0:T(8,128)(2,1)} %param.11) | copy-start | bytes 12582916
  166.8 6.8 %collective-permute-start.24 = (bf16[1,128,1024]{2,1,0:T(8,128)(2,1)S(1)}, bf16[1,128,1024]{2,1,0:T(8,128)(2,1)S(1)}, u32[]{:S(2)}, u32[]{:S(2)}) collective-permute-start(bf16[1,128,1024]{2,1,0:T(8,128)(2,1)S(1)} %pad_maximum_fusion.8), channel_id=1, source_target_pairs={{0,8},{4,12},{8,0},{12,4},{16,24},{20,28},{24,16},{28,20},{1,9},{5... | collective-permute-start | bytes 786440 | tf_op jit(solution)/shard_map/ppermute | solution.py:28
  173.8 2.7 %collective-permute-start.27 = (bf16[2,256,1024]{2,1,0:T(8,128)(2,1)S(1)}, bf16[2,256,1024]{2,1,0:T(8,128)(2,1)S(1)}, u32[]{:S(2)}, u32[]{:S(2)}) collective-permute-start(bf16[2,256,1024]{2,1,0:T(8,128)(2,1)S(1)} %maximum_maximum_fusion), channel_id=1, source_target_pairs={{0,4},{4,0},{8,12},{12,8},{16,20},{20,16},{24,28},{28,24},{1,5},{5... | collective-permute-start | bytes 3145736 | tf_op jit(solution)/shard_map/ppermute | solution.py:28

commit v3 on v2

--- a/solution.py
+++ b/solution.py
@@ -8,9 +8,10 @@
 
 AXES = ("state", "obs")
 TILE = 256
-TOLERANCE = 1e-4
+TOLERANCE = 5e-4
 MAX_STEPS = 4096
 REFRESH = 32
+FIRST_STEPS = 3
 HOLD = 4
 
 
@@ -67,13 +68,6 @@
         return lambda parts: tuple(exchange(v, dim) for v, dim in zip(parted(parts), dims, strict=True))
 
     return [both(head)] + [each(dims) for dims in zip(*middle, strict=True)] + [both(dim) for dim in tail]
-
-
-def join(vals):
-    parts = (vals,)
-    for step in reversed(steps_of(double)):
-        parts = step(parts)
-    return merged(parts)
 
 
 def after(vals, first):
@@ -88,7 +82,7 @@
     return starts, at
 
 
-def solve_kernel(tiles_ref, rhs_ref, out_ref, s1_ref, s2_ref, s3_ref, diag_ref):
+def solve_kernel(bit_ref, near_ref, far_ref, rhs_ref, out_ref, tiles_ref, s1_ref, s2_ref, s3_ref, diag_ref):
     count, members = rhs_ref.shape
     shift = float(members - 1)
     starts, _ = tile_starts(members)
@@ -105,31 +99,46 @@
         s2_ref[here] = two
         s3_ref[here] = (rest - two.astype(jnp.float32)).astype(jnp.bfloat16)
 
+    streams, half, _ = near_ref.shape
+    for s in range(streams):
+        for side, ref in ((bit_ref[0], near_ref), (1 - bit_ref[0], far_ref)):
+            tiles_ref[pl.ds(pl.multiple_of((2 * s + side) * half, 8), half), :] = ref[s]
+
     for j in range(blocks):
         for i in range(j, blocks):
             vals = tiles_ref[pl.ds(starts[j] + (i - j) * TILE, TILE), :]
             if i == j:
-                vals = vals + jnp.where(row == col, shift, 0.0)
-                diag_ref[:, pl.ds(j * TILE, TILE)] = jnp.sum(jnp.where(row == col, vals, 0.0), axis=0, keepdims=True)
-                place(vals, j, j)
+                on = jnp.where(row == col, vals, 0.0)
+                diag_ref[:, pl.ds(j * TILE, TILE)] = jnp.sum(on, axis=0, keepdims=True) + shift
+                place(vals - on, j, j)
             else:
                 place(vals, i, j)
                 place(vals.T, j, i)
 
-    def times(vals):
+    diag = diag_ref[...]
+    inverse = 1.0 / diag
+    rhs = rhs_ref[...]
+    dot = functools.partial(jnp.dot, preferred_element_type=jnp.float32)
+
+    def split(vals):
         one = vals.astype(jnp.bfloat16)
         rest = vals - one.astype(jnp.float32)
-        two = rest.astype(jnp.bfloat16)
+        return one, rest.astype(jnp.bfloat16), rest
+
+    def times(vals):
+        one, two, rest = split(vals)
         three = (rest - two.astype(jnp.float32)).astype(jnp.bfloat16)
-        dot = functools.partial(jnp.dot, preferred_element_type=jnp.float32)
         first = dot(jnp.concatenate([one, two, three]), s1_ref[...])
         second = dot(jnp.concatenate([one, two]), s2_ref[...])
         third = dot(one, s3_ref[...])
         small = first[2 * count :] + second[count:] + third
-        return first[:count] + (first[count : 2 * count] + second[:count] + small)
-
-    inverse = 1.0 / diag_ref[...]
-    rhs = rhs_ref[...]
+        return vals * diag + (first[:count] + (first[count : 2 * count] + second[:count] + small))
+
+    def nearly_times(vals):
+        one, two, _ = split(vals)
+        first = dot(jnp.concatenate([one, two]), s1_ref[...])
+        return vals * diag + (first[:count] + first[count:])
+
     bound = (TOLERANCE * shift) ** 2
 
     def unsolved(x, r):
@@ -139,43 +148,60 @@
     def divide(a, b):
         return jnp.where(b > 0.0, a / jnp.where(b > 0.0, b, 1.0), 0.0)
 
-    x = rhs * inverse
+    def step_of(product, x, r, p, rz):
+        q = product(p)
+        alpha = divide(rz, jnp.sum(p * q, axis=1, keepdims=True))
+        return x + alpha * p, r - alpha * q
+
+    def turn(r, p, rz):
+        z = r * inverse
+        rz_next = jnp.sum(r * z, axis=1, keepdims=True)
+        return z + divide(rz_next, rz) * p, rz_next
+
+    x, r = jnp.zeros_like(rhs), rhs
+    p, rz = turn(r, r, jnp.zeros((count, 1), jnp.float32))
+    for i in range(FIRST_STEPS):
+        x, r = step_of(nearly_times, x, r, p, rz)
+        if i < FIRST_STEPS - 1:
+            p, rz = turn(r, p, rz)
+
     r = rhs - times(x)
-    z = r * inverse
+    p, rz = turn(r, r, jnp.zeros((count, 1), jnp.float32))
 
     def more(carry):
-        step, gap = carry[0], carry[1]
-        return jnp.logical_and(step < MAX_STEPS, gap > 0.0)
+        return jnp.logical_and(carry[0] < MAX_STEPS, carry[1] > 0.0)
 
     def advance(carry):
         step, _, x, r, p, rz = carry
-        q = times(p)
-        alpha = divide(rz, jnp.sum(p * q, axis=1, keepdims=True))
-        x = x + alpha * p
-        r = r - alpha * q
+        x, r = step_of(times, x, r, p, rz)
         r = lax.cond(step % REFRESH == REFRESH - 1, lambda x, r: rhs - times(x), lambda x, r: r, x, r)
-        z = r * inverse
-        rz_next = jnp.sum(r * z, axis=1, keepdims=True)
-        p = z + divide(rz_next, rz) * p
-        return step + 1, unsolved(x, r), x, r, p, rz_next
-
-    init = (jnp.int32(0), unsolved(x, r), x, r, z, jnp.sum(r * z, axis=1, keepdims=True))
-    out_ref[...] = lax.while_loop(more, advance, init)[2].astype(jnp.bfloat16)
-
-
-def solve(tiles, rhs):
+        p, rz = turn(r, p, rz)
+        return step + 1, unsolved(x, r), x, r, p, rz
+
+    x = lax.while_loop(more, advance, (jnp.int32(0), unsolved(x, r), x, r, p, rz))[2]
+    out_ref[...] = x.astype(jnp.bfloat16)
+
+
+def solve(bit, near, far, rhs):
     members = rhs.shape[1]
     square = pltpu.VMEM((members, members), jnp.bfloat16)
+    vmem = pl.BlockSpec(memory_space=pltpu.VMEM)
     return pl.pallas_call(
         solve_kernel,
         out_shape=jax.ShapeDtypeStruct(rhs.shape, jnp.bfloat16),
-        in_specs=[pl.BlockSpec(memory_space=pltpu.VMEM)] * 2,
-        out_specs=pl.BlockSpec(memory_space=pltpu.VMEM),
-        scratch_shapes=[square, square, square, pltpu.VMEM((1, members), jnp.float32)],
+        in_specs=[pl.BlockSpec(memory_space=pltpu.SMEM), vmem, vmem, vmem],
+        out_specs=vmem,
+        scratch_shapes=[
+            pltpu.VMEM((tile_starts(members)[1], TILE), jnp.float32),
+            square,
+            square,
+            square,
+            pltpu.VMEM((1, members), jnp.float32),
+        ],
         compiler_params=pltpu.CompilerParams(vmem_limit_bytes=40 * 1024 * 1024),
-        cost_estimate=pl.CostEstimate(flops=6 * 6 * 2 * rhs.shape[0] * members * members, bytes_accessed=6 * members * members, transcendentals=0),
+        cost_estimate=pl.CostEstimate(flops=24 * 2 * rhs.shape[0] * members * members, bytes_accessed=6 * members * members, transcendentals=0),
         name="member_solve",
-    )(tiles, rhs)
+    )(bit, near, far, rhs)
 
 
 def weighted(vals, root_weight):
@@ -216,7 +242,7 @@
             for j in range(0, members, TILE)
         ]
     )
-    ahead_steps = steps_of(halve) + steps_of(double)[::-1]
+    ahead_steps = steps_of(halve) + steps_of(double)[:0:-1]
     gram = (tiles.reshape(2, -1, TILE),)
     for step in ahead_steps[:HOLD]:
         gram = step(gram)
@@ -237,30 +263,41 @@
 
     head = stages()[0]
     bit = my_bit(head)
-    quarter = members // 4
+    wide = members // 2
 
     def cross_part(side):
-        cols = jnp.concatenate([lax.dynamic_slice_in_dim(innovation, (2 * s + side) * quarter, quarter, 1) for s in range(2)], axis=1)
+        cols = lax.dynamic_slice_in_dim(innovation, side * wide, wide, 1)
         return jnp.dot(cols.T, anomalies, preferred_element_type=f32).reshape(2, -1, members)
 
+    block_vals = unknowns.astype(f32)
+    spread = (block_vals - jnp.mean(block_vals, axis=1, keepdims=True)).astype(bf16)
+
     later = iter(ahead_steps[HOLD:])
-    gram = next(later)(after(gram, innovation))
-    gram, send = lax.optimization_barrier((gram, cross_part(1 - bit)))
+    gram, send, spread = lax.optimization_barrier((gram, cross_part(1 - bit), spread))
     cross = (cross_part(bit) + swap(send, head),)
     gram = next(later)(gram)
     for step in steps_of(halve)[1:]:
         gram, cross = lax.optimization_barrier((gram, cross))
-        gram, cross = next(later)(gram), step(cross)
+        gram, cross = next(later, lambda parts: parts)(gram), step(cross)
     for step in later:
         gram = step(gram)
-    tiles, cross = merged(gram).reshape(-1, TILE), merged(cross)
-    gain = solve(tiles, cross.reshape(-1, members))
-    gain_t = join(gain.reshape(2, -1, members)).reshape(members, members)
-
-    block_vals = unknowns.astype(f32)
-    spread = (block_vals - jnp.mean(block_vals, axis=1, keepdims=True)).astype(bf16)
-    moved = lax.dot_general(spread, gain_t, (((1,), (1,)), ((), ())), preferred_element_type=f32)
-    return ((block_vals + moved).astype(bf16), innovation_var)
+    near, cross = lax.optimization_barrier((merged(gram), merged(cross)))
+    side = jnp.reshape(bit, (1,)).astype(jnp.int32)
+    gain = solve(side, near, swap(near, head), cross.reshape(-1, members)).reshape(2, -1, members)
+
+    gain = (gain,)
+    for step in steps_of(double)[:0:-1]:
+        gain = step(gain)
+    gain = merged(gain).reshape(wide, members)
+    other = swap(gain, head)
+
+    def side_of(gain, at):
+        moved = lax.dot_general(spread, gain, (((1,), (1,)), ((), ())), preferred_element_type=f32)
+        return (lax.dynamic_slice_in_dim(unknowns, at, wide, 1).astype(f32) + moved).astype(bf16)
+
+    updated = lax.dynamic_update_slice_in_dim(jnp.zeros_like(unknowns), side_of(gain, bit * wide), bit * wide, 1)
+    updated = lax.dynamic_update_slice_in_dim(updated, side_of(other, (1 - bit) * wide), (1 - bit) * wide, 1)
+    return (updated, innovation_var)
 
 
 def solution(mesh):

time: 184 us -> 176 us (0.957)
  waiting for transfers between devices: 98.2 us -> 87.5 us
  local copies, waits for them, and re-layouts: 2.76 us -> 7.24 us
  matrix products: 20.6 us -> 17.4 us
  Pallas kernels: 10.8 us -> 8.44 us
  starting transfers between devices: 40.5 us -> 42.7 us
    ppermute x28, waiting for transfers between devices: 91.8 us -> 82.9 us  [swap(): lax.ppermute(vals, axis, [(i, i ^ 1 << b) for i in range(lax.axis_size(ax...]
    unnamed x14 -> x19, local copies, waits for them, and re-layouts: 0.1 us -> 5.31 us
    convert_element_type x0 -> x1, other arithmetic: none -> 2.76 us  [on_device(): (block_vals - jnp.mean(block_vals, axis=1, keepdims=True)).astype(bf16)]
    pallas_call x1, Pallas kernels: 10.8 us -> 8.44 us  [solve(): pl.pallas_call(solve_kernel, out_shape=jax.ShapeDtypeStruct(rhs.shape, jn...]
    ppermute x28, starting transfers between devices: 29.5 us -> 31.7 us  [swap(): lax.ppermute(vals, axis, [(i, i ^ 1 << b) for i in range(lax.axis_size(ax...]
    reduce_sum x1, other arithmetic: 0.62 us -> 2.89 us  [on_device(): jnp.mean(block_vals, axis=1, keepdims=True)]
    dot_general x1 -> x2, matrix products: 6.63 us -> 4.83 us  [side_of(): lax.dot_general(spread, gain, (((1,), (1,)), ((), ())), preferred_element...]
  transfers between devices with their start and end apart: 30 -> 30, of which waited for: 24 -> 26; matrix products, arithmetic and copies ran while one was open for 8% -> 11% of each run, Pallas kernels for 0% -> 0%
where the time goes in v3:
time: 176 us
  waiting for transfers between devices  87.5 us (50%)
  starting transfers between devices  42.7 us (24%)
  matrix products  17.4 us (10%)
  other arithmetic  11.1 us (6%)
  Pallas kernels  8.44 us (5%)
  local copies, waits for them, and re-layouts  7.24 us (4%)
    ppermute x28, waiting for transfers between devices, swap(): lax.ppermute(vals, axis, [(i, i ^ 1 << b) for i in range(lax.axis_size(ax...  82.9 us
    ppermute x28, starting transfers between devices, swap(): lax.ppermute(vals, axis, [(i, i ^ 1 << b) for i in range(lax.axis_size(ax...  31.7 us
    pallas_call x1, Pallas kernels, solve(): pl.pallas_call(solve_kernel, out_shape=jax.ShapeDtypeStruct(rhs.shape, jn...  8.44 us
    all_to_all x1, starting transfers between devices, on_device(): lax.all_to_all(jnp.broadcast_to(own, (shards, 2, rows)), AXES, split_axis...  7.3 us
    unnamed x19, local copies, waits for them, and re-layouts  5.31 us
    dot_general x2, matrix products, side_of(): lax.dot_general(spread, gain, (((1,), (1,)), ((), ())), preferred_element...  4.83 us
    dot_general x2, matrix products, cross_part(): jnp.dot(cols.T, anomalies, preferred_element_type=f32)  4.51 us
    all_to_all x1, starting transfers between devices, on_device(): lax.all_to_all(outgoing.reshape(shards, capacity, members), AXES, split_a...  3.62 us
  transfers between devices with their start and end apart: 30, of which 26 were waited for; matrix products, arithmetic and copies ran while one was open for 11% of the time, Pallas kernels for 0%

profile of v3, /device:TPU:0, one launch (start us, length us, event | category | flops | bytes accessed | tf_op | source)
XLA Modules:
  0.0 175.6 jit_solution(13035274718233943523)
XLA Ops:
  2.8 7.3 %all-to-all-start = ((f32[32,2,512]{2,1,0:T(2,128)}), f32[32,2,512]{2,1,0:T(2,128)S(1)}, u32[]{:S(2)}, u32[]{:S(2)}) async-start(f32[32,2,512]{2,1,0:T(2,128)} %broadcast_in_dim.19), calls=%async_computation | async-start | bytes 262144 | tf_op jit(solution)/shard_map/all_to_all | solution.py:232
  10.3 2.9 %convert_reduce_fusion = f32[2048]{0:T(1024)S(1)} fusion(bf16[2048,1024]{1,0:T(8,128)(2,1)} %param.11), kind=kLoop, calls=%fused_computation.1 | loop fusion | flops 4192256 | bytes 4202496 | tf_op jit(solution)/shard_map/reduce_sum | solution.py:273
  13.2 2.6 %fusion.10 = bf16[1024,1024]{1,0:T(8,128)(2,1)} fusion(bf16[512,1024]{1,0:T(8,128)(2,1)S(1)} %copy-done.4, s32[512]{0:T(512)S(1)} %convert_add_fusion), kind=kOutput, calls=%fused_computation.26 | convolution fusion | flops 1075314688 | bytes 3147776 | tf_op jit(solution)/shard_map/dot_general | solution.py:228
  16.1 2.4 %all-to-all-done = f32[32,2,512]{2,1,0:T(2,128)S(1)} async-done(((f32[32,2,512]{2,1,0:T(2,128)}), f32[32,2,512]{2,1,0:T(2,128)S(1)}, u32[]{:S(2)}, u32[]{:S(2)}) %all-to-all-start) | async-done | bytes 131104 | tf_op jit(solution)/shard_map/all_to_all | solution.py:232
  18.5 3.6 %all-to-all-start.1 = ((bf16[32,32,1024]{2,1,0:T(8,128)(2,1)}), bf16[32,32,1024]{2,1,0:T(8,128)(2,1)S(1)}, u32[]{:S(2)}, u32[]{:S(2)}) async-start(bf16[32,32,1024]{2,1,0:T(8,128)(2,1)} %bitcast.4), calls=%async_computation.1 | async-start | bytes 4194304 | tf_op jit(solution)/shard_map/all_to_all | solution.py:229
  27.0 2.8 %fusion = bf16[2048,1024]{1,0:T(8,128)(2,1)} fusion(bf16[2048,1024]{1,0:T(8,128)(2,1)S(1)} %copy-done, f32[2048]{0:T(1024)S(1)} %broadcast_multiply_fusion), kind=kLoop, calls=%fused_computation.2 | loop fusion | flops 6291456 | bytes 8396800 | tf_op jit(solution)/shard_map/convert_element_type | solution.py:273
  30.1 1.8 %collective-permute-start.3 = (f32[1,320,256]{2,1,0:T(8,128)S(1)}, f32[1,320,256]{2,1,0:T(8,128)S(1)}, u32[]{:S(2)}, u32[]{:S(2)}) collective-permute-start(f32[1,320,256]{2,1,0:T(8,128)S(1)} %constant_dynamic-slice_fusion.8), channel_id=1, source_target_pairs={{0,16},{4,20},{8,24},{12,28},{16,0},{20,4},{24,8},{28,12},{1,17},{... | collective-permute-start | bytes 983048 | tf_op jit(solution)/shard_map/ppermute | solution.py:29
  32.9 1.5 collective-permute-start.1
  34.4 14.6 %collective-permute-done.3 = f32[1,320,256]{2,1,0:T(8,128)S(1)} collective-permute-done((f32[1,320,256]{2,1,0:T(8,128)S(1)}, f32[1,320,256]{2,1,0:T(8,128)S(1)}, u32[]{:S(2)}, u32[]{:S(2)}) %collective-permute-start.3) | collective-permute-done | bytes 327712 | tf_op jit(solution)/shard_map/ppermute | solution.py:29
  49.3 1.4 collective-permute-start.2
  50.7 5.7 %collective-permute-done.4 = f32[1,160,256]{2,1,0:T(8,128)S(1)} collective-permute-done((f32[1,160,256]{2,1,0:T(8,128)S(1)}, f32[1,160,256]{2,1,0:T(8,128)S(1)}, u32[]{:S(2)}, u32[]{:S(2)}) %collective-permute-start.4) | collective-permute-done | bytes 163872 | tf_op jit(solution)/shard_map/ppermute | solution.py:29
  56.5 1.9 %collective-permute-done.2 = f32[1,160,256]{2,1,0:T(8,128)S(1)} collective-permute-done((f32[1,160,256]{2,1,0:T(8,128)S(1)}, f32[1,160,256]{2,1,0:T(8,128)S(1)}, u32[]{:S(2)}, u32[]{:S(2)}) %collective-permute-start.2) | collective-permute-done | bytes 163872 | tf_op jit(solution)/shard_map/ppermute | solution.py:29
  58.4 1.3 collective-permute-start.5
  59.8 7.5 %collective-permute-done.5 = f32[2,80,256]{2,1,0:T(8,128)S(1)} collective-permute-done((f32[2,80,256]{2,1,0:T(8,128)S(1)}, f32[2,80,256]{2,1,0:T(8,128)S(1)}, u32[]{:S(2)}, u32[]{:S(2)}) %collective-permute-start.5) | collective-permute-done | bytes 163872 | tf_op jit(solution)/shard_map/ppermute | solution.py:29
  67.3 2.2 %all-to-all-done.1 = bf16[32,32,1024]{2,1,0:T(8,128)(2,1)S(1)} async-done(((bf16[32,32,1024]{2,1,0:T(8,128)(2,1)}), bf16[32,32,1024]{2,1,0:T(8,128)(2,1)S(1)}, u32[]{:S(2)}, u32[]{:S(2)}) %all-to-all-start.1) | async-done | bytes 2097184 | tf_op jit(solution)/shard_map/all_to_all | solution.py:229
  69.5 2.9 %multiply_reduce_fusion = (f32[512]{0:T(512)S(1)}, f32[512]{0:T(512)S(1)}, bf16[512,1024]{1,0:T(8,128)(2,1)S(1)}, bf16[512,1024]{1,0:T(8,128)(2,1)S(1)}) fusion(bf16[512,1024]{1,0:T(8,128)(2,1)} %param.10, f32[512]{0:T(512)S(1)} %copy-done.6, f32[512]{0:T(512)S(1)} %divide_sqrt_fusion, bf16[1024,1024]{1,0:T(8,128)(2,1)S(1)} %bitcast.55, s32[1024]{0:T(1024)S(1)} %sub.80), kind=kOutput, calls=%fused_computation.17 | convolution fusion | flops 1079507968 | bytes 5255168 | tf_op jit(solution)/shard_map/dot_general | solution.py:255
  72.4 2.3 %fusion.22 = f32[512,1024]{1,0:T(8,128)} fusion(bf16[512,1024]{1,0:T(8,128)(2,1)S(1)} %get-tuple-element.38, s32[]{:T(128)S(6)} %select_n.283, bf16[512,1024]{1,0:T(8,128)(2,1)S(1)} %get-tuple-element.78, f32[512]{0:T(512)S(1)} %broadcast_multiply_fusion.2, f32[512]{0:T(512)S(1)} %divide_sqrt_fusion), kind=kOutput, calls=%fused_computation.48 | convolution fusion | flops 538968064 | bytes 3674116 | tf_op jit(solution)/shard_map/dot_general | solution.py:270
  75.6 1.5 collective-permute-start.6
  77.2 2.2 %fusion.20 = f32[512,1024]{1,0:T(8,128)S(1)} fusion(bf16[512,1024]{1,0:T(8,128)(2,1)} %copy-done.7, s32[]{:T(128)S(6)} %select_n.264, bf16[512,1024]{1,0:T(8,128)(2,1)} %copy-done.8, f32[512]{0:T(512)S(1)} %broadcast_multiply_fusion.2, f32[512]{0:T(512)S(1)} %divide_sqrt_fusion), kind=kOutput, calls=%fused_computation.46 | convolution fusion | flops 538968064 | bytes 3674116 | tf_op jit(solution)/shard_map/dot_general | solution.py:270
  79.4 1.6 collective-permute-done.6
  81.6 3.3 %collective-permute-start.10 = (f32[1,128,1024]{2,1,0:T(8,128)S(1)}, f32[1,128,1024]{2,1,0:T(8,128)S(1)}, u32[]{:S(2)}, u32[]{:S(2)}) collective-permute-start(f32[1,128,1024]{2,1,0:T(8,128)S(1)} %constant_dynamic-slice_fusion.4), channel_id=1, source_target_pairs={{0,16},{4,20},{8,24},{12,28},{16,0},{20,4},{24,8},{28,12},{1,17},{... | collective-permute-start | bytes 1572872 | tf_op jit(solution)/shard_map/ppermute | solution.py:29
  86.2 4.3 %collective-permute-done.8 = f32[2,40,256]{2,1,0:T(8,128)S(1)} collective-permute-done((f32[2,40,256]{2,1,0:T(8,128)S(1)}, f32[2,40,256]{2,1,0:T(8,128)S(1)}, u32[]{:S(2)}, u32[]{:S(2)}) %collective-permute-start.8) | collective-permute-done | bytes 81952 | tf_op jit(solution)/shard_map/ppermute | solution.py:29
  90.5 3.9 %collective-permute-done.10 = f32[1,128,1024]{2,1,0:T(8,128)S(1)} collective-permute-done((f32[1,128,1024]{2,1,0:T(8,128)S(1)}, f32[1,128,1024]{2,1,0:T(8,128)S(1)}, u32[]{:S(2)}, u32[]{:S(2)}) %collective-permute-start.10) | collective-permute-done | bytes 524320 | tf_op jit(solution)/shard_map/ppermute | solution.py:29
  94.6 3.3 %collective-permute-done.9 = f32[1,128,1024]{2,1,0:T(8,128)S(1)} collective-permute-done((f32[1,128,1024]{2,1,0:T(8,128)S(1)}, f32[1,128,1024]{2,1,0:T(8,128)S(1)}, u32[]{:S(2)}, u32[]{:S(2)}) %collective-permute-start.9) | collective-permute-done | bytes 524320 | tf_op jit(solution)/shard_map/ppermute | solution.py:29
  98.0 2.8 %collective-permute-start.11 = (f32[2,80,256]{2,1,0:T(8,128)S(1)}, f32[2,80,256]{2,1,0:T(8,128)S(1)}, u32[]{:S(2)}, u32[]{:S(2)}) collective-permute-start(f32[2,80,256]{2,1,0:T(8,128)S(1)} %pad_maximum_fusion.6), channel_id=1, source_target_pairs={{0,1},{1,0},{2,3},{3,2},{4,5},{5,4},{6,7},{7,6},{8,9},{9,8},{10,11... | collective-permute-start | bytes 491528 | tf_op jit(solution)/shard_map/ppermute | solution.py:29
  101.4 1.5 collective-permute-start.12
  104.1 3.1 %collective-permute-done.13 = f32[1,64,1024]{2,1,0:T(8,128)S(1)} collective-permute-done((f32[1,64,1024]{2,1,0:T(8,128)S(1)}, f32[1,64,1024]{2,1,0:T(8,128)S(1)}, u32[]{:S(2)}, u32[]{:S(2)}) %collective-permute-start.13) | collective-permute-done | bytes 262176 | tf_op jit(solution)/shard_map/ppermute | solution.py:29
  108.3 1.5 collective-permute-start.14
  110.7 3.0 %collective-permute-done.14 = f32[1,160,256]{2,1,0:T(8,128)S(1)} collective-permute-done((f32[1,160,256]{2,1,0:T(8,128)S(1)}, f32[1,160,256]{2,1,0:T(8,128)S(1)}, u32[]{:S(2)}, u32[]{:S(2)}) %collective-permute-start.14) | collective-permute-done | bytes 163872 | tf_op jit(solution)/shard_map/ppermute | solution.py:29
  113.7 1.5 collective-permute-done.15
  115.3 3.0 %collective-permute-done.16 = f32[2,32,1024]{2,1,0:T(8,128)S(1)} collective-permute-done((f32[2,32,1024]{2,1,0:T(8,128)S(1)}, f32[2,32,1024]{2,1,0:T(8,128)S(1)}, u32[]{:S(2)}, u32[]{:S(2)}) %collective-permute-start.16) | collective-permute-done | bytes 262176 | tf_op jit(solution)/shard_map/ppermute | solution.py:29
  118.8 2.1 %collective-permute-start.17 = (f32[1,320,256]{2,1,0:T(8,128)S(1)}, f32[1,320,256]{2,1,0:T(8,128)S(1)}, u32[]{:S(2)}, u32[]{:S(2)}) collective-permute-start(f32[1,320,256]{2,1,0:T(8,128)S(1)} %pad_maximum_fusion.2), channel_id=1, source_target_pairs={{0,8},{4,12},{8,0},{12,4},{16,24},{20,28},{24,16},{28,20},{1,9},{5... | collective-permute-start | bytes 983048 | tf_op jit(solution)/shard_map/ppermute | solution.py:29
  121.3 3.5 %collective-permute-done.19 = f32[2,16,1024]{2,1,0:T(8,128)S(1)} collective-permute-done((f32[2,16,1024]{2,1,0:T(8,128)S(1)}, f32[2,16,1024]{2,1,0:T(8,128)S(1)}, u32[]{:S(2)}, u32[]{:S(2)}) %collective-permute-start.19) | collective-permute-done | bytes 131104 | tf_op jit(solution)/shard_map/ppermute | solution.py:29
  126.0 2.0 %collective-permute-done.18 = f32[1,320,256]{2,1,0:T(8,128)S(1)} collective-permute-done((f32[1,320,256]{2,1,0:T(8,128)S(1)}, f32[1,320,256]{2,1,0:T(8,128)S(1)}, u32[]{:S(2)}, u32[]{:S(2)}) %collective-permute-start.18) | collective-permute-done | bytes 327712 | tf_op jit(solution)/shard_map/ppermute | solution.py:29
  128.2 3.0 %collective-permute-done.20.far_ref = f32[2,640,256]{2,1,0:T(8,128)S(1)} collective-permute-done((f32[2,640,256]{2,1,0:T(8,128)S(1)}, f32[2,640,256]{2,1,0:T(8,128)S(1)}, u32[]{:S(2)}, u32[]{:S(2)}) %collective-permute-start.20) | collective-permute-done | bytes 1310752 | tf_op jit(solution)/shard_map/ppermute | solution.py:29
  131.2 8.4 %member_solve.1 = bf16[32,1024]{1,0:T(8,128)(2,1)S(1)} custom-call(s32[1]{0:T(128)} %bitcast.7.bit_ref, f32[2,640,256]{2,1,0:T(8,128)S(1)} %maximum_maximum_fusion.near_ref, f32[2,640,256]{2,1,0:T(8,128)S(1)} %collective-permute-done.20.far_ref, f32[32,1024]{1,0:T(8,128)S(1)} %bitcast.49), custom_call_target="tpu_custom_call" | custom-call | flops 1610612736 | bytes 6291456 | tf_op jit(solution)/shard_map/member_solve/pallas_call | solution.py:189
  139.6 2.1 %collective-permute-start.21 = (bf16[2,16,1024]{2,1,0:T(8,128)(2,1)S(1)}, bf16[2,16,1024]{2,1,0:T(8,128)(2,1)S(1)}, u32[]{:S(2)}, u32[]{:S(2)}) collective-permute-start(bf16[2,16,1024]{2,1,0:T(8,128)(2,1)S(1)} %bitcast.50), channel_id=1, source_target_pairs={{0,2},{1,3},{2,0},{3,1},{4,6},{5,7},{6,4},{7,5},{8,10},{9,11},{10,... | collective-permute-start | bytes 196616 | tf_op jit(solution)/shard_map/ppermute | solution.py:29
  141.7 3.3 %collective-permute-done.21 = bf16[2,16,1024]{2,1,0:T(8,128)(2,1)S(1)} collective-permute-done((bf16[2,16,1024]{2,1,0:T(8,128)(2,1)S(1)}, bf16[2,16,1024]{2,1,0:T(8,128)(2,1)S(1)}, u32[]{:S(2)}, u32[]{:S(2)}) %collective-permute-start.21) | collective-permute-done | bytes 65568 | tf_op jit(solution)/shard_map/ppermute | solution.py:29
  145.0 1.6 collective-permute-start.22
  146.6 4.0 %collective-permute-done.22 = bf16[2,32,1024]{2,1,0:T(8,128)(2,1)S(1)} collective-permute-done((bf16[2,32,1024]{2,1,0:T(8,128)(2,1)S(1)}, bf16[2,32,1024]{2,1,0:T(8,128)(2,1)S(1)}, u32[]{:S(2)}, u32[]{:S(2)}) %collective-permute-start.22) | collective-permute-done | bytes 131104 | tf_op jit(solution)/shard_map/ppermute | solution.py:29
  150.8 3.0 %collective-permute-start.23 = (bf16[1,64,1024]{2,1,0:T(8,128)(2,1)S(1)}, bf16[1,64,1024]{2,1,0:T(8,128)(2,1)S(1)}, u32[]{:S(2)}, u32[]{:S(2)}) collective-permute-start(bf16[1,64,1024]{2,1,0:T(8,128)(2,1)S(1)} %get-tuple-element.63), channel_id=1, source_target_pairs={{0,16},{4,20},{8,24},{12,28},{16,0},{20,4},{24,8},{28,12},{1,17},{... | collective-permute-start | bytes 393224 | tf_op jit(solution)/shard_map/ppermute | solution.py:29
  154.2 2.6 %collective-permute-done.23 = bf16[1,64,1024]{2,1,0:T(8,128)(2,1)S(1)} collective-permute-done((bf16[1,64,1024]{2,1,0:T(8,128)(2,1)S(1)}, bf16[1,64,1024]{2,1,0:T(8,128)(2,1)S(1)}, u32[]{:S(2)}, u32[]{:S(2)}) %collective-permute-start.23) | collective-permute-done | bytes 131104 | tf_op jit(solution)/shard_map/ppermute | solution.py:29
  157.3 1.8 %collective-permute-done.25 = bf16[1,64,1024]{2,1,0:T(8,128)(2,1)S(1)} collective-permute-done((bf16[1,64,1024]{2,1,0:T(8,128)(2,1)S(1)}, bf16[1,64,1024]{2,1,0:T(8,128)(2,1)S(1)}, u32[]{:S(2)}, u32[]{:S(2)}) %collective-permute-start.25) | collective-permute-done | bytes 131104 | tf_op jit(solution)/shard_map/ppermute | solution.py:29
  159.5 4.9 %collective-permute-done.24 = bf16[1,128,1024]{2,1,0:T(8,128)(2,1)S(1)} collective-permute-done((bf16[1,128,1024]{2,1,0:T(8,128)(2,1)S(1)}, bf16[1,128,1024]{2,1,0:T(8,128)(2,1)S(1)}, u32[]{:S(2)}, u32[]{:S(2)}) %collective-permute-start.24) | collective-permute-done | bytes 262176 | tf_op jit(solution)/shard_map/ppermute | solution.py:29
  167.0 1.7 copy-done.1
  168.7 2.4 %fusion.1 = bf16[2048,1024]{1,0:T(8,128)(2,1)S(1)} fusion(bf16[2048,1024]{1,0:T(8,128)(2,1)S(1)} %broadcast_in_dim.18, s32[]{:T(128)S(6)} %select_n.264, bf16[2048,1024]{1,0:T(8,128)(2,1)S(1)} %copy-done.2, bf16[512,1024]{1,0:T(8,128)(2,1)S(1)} %bitcast.57, bf16[2048,1024]{1,0:T(8,128)(2,1)S(1)} %copy-done.1), kind=kOutput, calls=%fused_computation.8 | convolution fusion | flops 2150629376 | bytes 9437188 | tf_op jit(solution)/shard_map/dot_general | solution.py:295
  171.1 2.4 %fusion.2 = bf16[2048,1024]{1,0:T(8,128)(2,1)S(1)} fusion(bf16[2048,1024]{1,0:T(8,128)(2,1)S(1)} %fusion.1, s32[]{:T(128)S(6)} %select_n.283, bf16[2048,1024]{1,0:T(8,128)(2,1)S(1)} %copy-done.2, bf16[512,1024]{1,0:T(8,128)(2,1)S(1)} %collective-permute-done.27, bf16[2048,1024]{1,0:T(8,128)(2,1)S(1)} %copy-done.1), kind=kOutput, calls=%fused_computation.9 | convolution fusion | flops 2150629376 | bytes 9437188 | tf_op jit(solution)/shard_map/dot_general | solution.py:295
  173.6 2.0 %copy-done.3 = bf16[2048,1024]{1,0:T(8,128)(2,1)} copy-done((bf16[2048,1024]{1,0:T(8,128)(2,1)}, bf16[2048,1024]{1,0:T(8,128)(2,1)S(1)}, u32[]{:S(2)}) %copy-start.3) | copy-done | bytes 4194328
  (118 shorter events, 22.0 us)
Async XLA Ops:
  2.8 15.7 %all-to-all-start = ((f32[32,2,512]{2,1,0:T(2,128)}), f32[32,2,512]{2,1,0:T(2,128)S(1)}, u32[]{:S(2)}, u32[]{:S(2)}) async-start(f32[32,2,512]{2,1,0:T(2,128)} %broadcast_in_dim.19), calls=%async_computation | async-start | bytes 262144 | tf_op jit(solution)/shard_map/all_to_all | solution.py:232
  10.3 2.9 %copy-start.4 = (bf16[512,1024]{1,0:T(8,128)(2,1)S(1)}, bf16[512,1024]{1,0:T(8,128)(2,1)}, u32[]{:S(2)}) copy-start(bf16[512,1024]{1,0:T(8,128)(2,1)} %param.6) | copy-start | bytes 3145732
  18.5 51.0 %all-to-all-start.1 = ((bf16[32,32,1024]{2,1,0:T(8,128)(2,1)}), bf16[32,32,1024]{2,1,0:T(8,128)(2,1)S(1)}, u32[]{:S(2)}, u32[]{:S(2)}) async-start(bf16[32,32,1024]{2,1,0:T(8,128)(2,1)} %bitcast.4), calls=%async_computation.1 | async-start | bytes 4194304 | tf_op jit(solution)/shard_map/all_to_all | solution.py:229
  24.8 2.2 %copy-start = (bf16[2048,1024]{1,0:T(8,128)(2,1)S(1)}, bf16[2048,1024]{1,0:T(8,128)(2,1)}, u32[]{:S(2)}) copy-start(bf16[2048,1024]{1,0:T(8,128)(2,1)} %param.11) | copy-start | bytes 12582916
  25.0 0.8 copy-start.5
  25.1 4.8 %collective-permute-start = (f32[2,640,256]{2,1,0:T(8,128)S(1)}, f32[2,640,256]{2,1,0:T(8,128)S(1)}, u32[]{:S(2)}, u32[]{:S(2)}) collective-permute-start(f32[2,640,256]{2,1,0:T(8,128)S(1)} %constant_dynamic-slice_fusion.11), channel_id=1, source_target_pairs={{0,4},{4,0},{8,12},{12,8},{16,20},{20,16},{24,28},{28,24},{1,5},{5... | collective-permute-start | bytes 3932168 | tf_op jit(solution)/shard_map/ppermute | solution.py:29
  30.1 18.9 %collective-permute-start.3 = (f32[1,320,256]{2,1,0:T(8,128)S(1)}, f32[1,320,256]{2,1,0:T(8,128)S(1)}, u32[]{:S(2)}, u32[]{:S(2)}) collective-permute-start(f32[1,320,256]{2,1,0:T(8,128)S(1)} %constant_dynamic-slice_fusion.8), channel_id=1, source_target_pairs={{0,16},{4,20},{8,24},{12,28},{16,0},{20,4},{24,8},{28,12},{1,17},{... | collective-permute-start | bytes 983048 | tf_op jit(solution)/shard_map/ppermute | solution.py:29
  32.9 16.3 %collective-permute-start.1 = (f32[1,320,256]{2,1,0:T(8,128)S(1)}, f32[1,320,256]{2,1,0:T(8,128)S(1)}, u32[]{:S(2)}, u32[]{:S(2)}) collective-permute-start(f32[1,320,256]{2,1,0:T(8,128)S(1)} %constant_dynamic-slice_fusion.10), channel_id=1, source_target_pairs={{0,8},{4,12},{8,0},{12,4},{16,24},{20,28},{24,16},{28,20},{1,9},{5... | collective-permute-start | bytes 983048 | tf_op jit(solution)/shard_map/ppermute | solution.py:29
  49.1 20.4 %copy-start.6 = (f32[512]{0:T(512)S(1)}, f32[512]{0:T(512)}, u32[]{:S(2)}) copy-start(f32[512]{0:T(512)} %param.8) | copy-start | bytes 6148
  49.1 7.3 %collective-permute-start.4 = (f32[1,160,256]{2,1,0:T(8,128)S(1)}, f32[1,160,256]{2,1,0:T(8,128)S(1)}, u32[]{:S(2)}, u32[]{:S(2)}) collective-permute-start(f32[1,160,256]{2,1,0:T(8,128)S(1)} %constant_dynamic-slice_fusion.7), channel_id=1, source_target_pairs={{0,8},{4,12},{8,0},{12,4},{16,24},{20,28},{24,16},{28,20},{1,9},{5... | collective-permute-start | bytes 491528 | tf_op jit(solution)/shard_map/ppermute | solution.py:29
  49.3 9.0 %collective-permute-start.2 = (f32[1,160,256]{2,1,0:T(8,128)S(1)}, f32[1,160,256]{2,1,0:T(8,128)S(1)}, u32[]{:S(2)}, u32[]{:S(2)}) collective-permute-start(f32[1,160,256]{2,1,0:T(8,128)S(1)} %constant_dynamic-slice_fusion.9), channel_id=1, source_target_pairs={{0,16},{4,20},{8,24},{12,28},{16,0},{20,4},{24,8},{28,12},{1,17},{... | collective-permute-start | bytes 491528 | tf_op jit(solution)/shard_map/ppermute | solution.py:29
  58.4 8.9 %collective-permute-start.5 = (f32[2,80,256]{2,1,0:T(8,128)S(1)}, f32[2,80,256]{2,1,0:T(8,128)S(1)}, u32[]{:S(2)}, u32[]{:S(2)}) collective-permute-start(f32[2,80,256]{2,1,0:T(8,128)S(1)} %fusion.30), channel_id=1, source_target_pairs={{0,1},{1,0},{2,3},{3,2},{4,5},{5,4},{6,7},{7,6},{8,9},{9,8},{10,11... | collective-permute-start | bytes 491528 | tf_op jit(solution)/shard_map/ppermute | solution.py:29
  72.3 2.3 %copy-start.7 = (bf16[512,1024]{1,0:T(8,128)(2,1)}, bf16[512,1024]{1,0:T(8,128)(2,1)S(1)}, u32[]{:S(2)}) copy-start(bf16[512,1024]{1,0:T(8,128)(2,1)S(1)} %get-tuple-element.38) | copy-start | bytes 3145732
  72.3 2.3 %copy-start.8 = (bf16[512,1024]{1,0:T(8,128)(2,1)}, bf16[512,1024]{1,0:T(8,128)(2,1)S(1)}, u32[]{:S(2)}) copy-start(bf16[512,1024]{1,0:T(8,128)(2,1)S(1)} %get-tuple-element.78) | copy-start | bytes 3145732
  74.6 6.3 %collective-permute-start.7 = (f32[2,256,1024]{2,1,0:T(8,128)}, f32[2,256,1024]{2,1,0:T(8,128)S(1)}, u32[]{:S(2)}, u32[]{:S(2)}) collective-permute-start(f32[2,256,1024]{2,1,0:T(8,128)} %bitcast.6), channel_id=1, source_target_pairs={{0,4},{4,0},{8,12},{12,8},{16,20},{20,16},{24,28},{28,24},{1,5},{5... | collective-permute-start | bytes 6291464 | tf_op jit(solution)/shard_map/ppermute | solution.py:29
  75.6 5.3 %collective-permute-start.6 = (f32[2,40,256]{2,1,0:T(8,128)S(1)}, f32[2,40,256]{2,1,0:T(8,128)S(1)}, u32[]{:S(2)}, u32[]{:S(2)}) collective-permute-start(f32[2,40,256]{2,1,0:T(8,128)S(1)} %constant_dynamic-slice_fusion.6), channel_id=1, source_target_pairs={{0,2},{1,3},{2,0},{3,1},{4,6},{5,7},{6,4},{7,5},{8,10},{9,11},{10,... | collective-permute-start | bytes 245768 | tf_op jit(solution)/shard_map/ppermute | solution.py:29
  81.6 12.9 %collective-permute-start.10 = (f32[1,128,1024]{2,1,0:T(8,128)S(1)}, f32[1,128,1024]{2,1,0:T(8,128)S(1)}, u32[]{:S(2)}, u32[]{:S(2)}) collective-permute-start(f32[1,128,1024]{2,1,0:T(8,128)S(1)} %constant_dynamic-slice_fusion.4), channel_id=1, source_target_pairs={{0,16},{4,20},{8,24},{12,28},{16,0},{20,4},{24,8},{28,12},{1,17},{... | collective-permute-start | bytes 1572872 | tf_op jit(solution)/shard_map/ppermute | solution.py:29
  84.9 5.6 %collective-permute-start.8 = (f32[2,40,256]{2,1,0:T(8,128)S(1)}, f32[2,40,256]{2,1,0:T(8,128)S(1)}, u32[]{:S(2)}, u32[]{:S(2)}) collective-permute-start(f32[2,40,256]{2,1,0:T(8,128)S(1)} %dynamic-slice_add_fusion.11), channel_id=1, source_target_pairs={{0,2},{1,3},{2,0},{3,1},{4,6},{5,7},{6,4},{7,5},{8,10},{9,11},{10,... | collective-permute-start | bytes 245768 | tf_op jit(solution)/shard_map/ppermute | solution.py:29
  85.0 12.9 %collective-permute-start.9 = (f32[1,128,1024]{2,1,0:T(8,128)S(1)}, f32[1,128,1024]{2,1,0:T(8,128)S(1)}, u32[]{:S(2)}, u32[]{:S(2)}) collective-permute-start(f32[1,128,1024]{2,1,0:T(8,128)S(1)} %constant_dynamic-slice_fusion.5), channel_id=1, source_target_pairs={{0,8},{4,12},{8,0},{12,4},{16,24},{20,28},{24,16},{28,20},{1,9},{5... | collective-permute-start | bytes 1572872 | tf_op jit(solution)/shard_map/ppermute | solution.py:29
  98.0 6.1 %collective-permute-start.11 = (f32[2,80,256]{2,1,0:T(8,128)S(1)}, f32[2,80,256]{2,1,0:T(8,128)S(1)}, u32[]{:S(2)}, u32[]{:S(2)}) collective-permute-start(f32[2,80,256]{2,1,0:T(8,128)S(1)} %pad_maximum_fusion.6), channel_id=1, source_target_pairs={{0,1},{1,0},{2,3},{3,2},{4,5},{5,4},{6,7},{7,6},{8,9},{9,8},{10,11... | collective-permute-start | bytes 491528 | tf_op jit(solution)/shard_map/ppermute | solution.py:29
  100.8 6.4 %collective-permute-start.13 = (f32[1,64,1024]{2,1,0:T(8,128)S(1)}, f32[1,64,1024]{2,1,0:T(8,128)S(1)}, u32[]{:S(2)}, u32[]{:S(2)}) collective-permute-start(f32[1,64,1024]{2,1,0:T(8,128)S(1)} %constant_dynamic-slice_fusion.2), channel_id=1, source_target_pairs={{0,8},{4,12},{8,0},{12,4},{16,24},{20,28},{24,16},{28,20},{1,9},{5... | collective-permute-start | bytes 786440 | tf_op jit(solution)/shard_map/ppermute | solution.py:29
  101.4 6.9 %collective-permute-start.12 = (f32[1,64,1024]{2,1,0:T(8,128)S(1)}, f32[1,64,1024]{2,1,0:T(8,128)S(1)}, u32[]{:S(2)}, u32[]{:S(2)}) collective-permute-start(f32[1,64,1024]{2,1,0:T(8,128)S(1)} %constant_dynamic-slice_fusion.3), channel_id=1, source_target_pairs={{0,16},{4,20},{8,24},{12,28},{16,0},{20,4},{24,8},{28,12},{1,17},{... | collective-permute-start | bytes 786440 | tf_op jit(solution)/shard_map/ppermute | solution.py:29
  108.3 5.4 %collective-permute-start.14 = (f32[1,160,256]{2,1,0:T(8,128)S(1)}, f32[1,160,256]{2,1,0:T(8,128)S(1)}, u32[]{:S(2)}, u32[]{:S(2)}) collective-permute-start(f32[1,160,256]{2,1,0:T(8,128)S(1)} %get-tuple-element.58), channel_id=1, source_target_pairs={{0,16},{4,20},{8,24},{12,28},{16,0},{20,4},{24,8},{28,12},{1,17},{... | collective-permute-start | bytes 491528 | tf_op jit(solution)/shard_map/ppermute | solution.py:29
  109.9 5.3 %collective-permute-start.15 = (f32[1,160,256]{2,1,0:T(8,128)S(1)}, f32[1,160,256]{2,1,0:T(8,128)S(1)}, u32[]{:S(2)}, u32[]{:S(2)}) collective-permute-start(f32[1,160,256]{2,1,0:T(8,128)S(1)} %get-tuple-element.57), channel_id=1, source_target_pairs={{0,8},{4,12},{8,0},{12,4},{16,24},{20,28},{24,16},{28,20},{1,9},{5... | collective-permute-start | bytes 491528 | tf_op jit(solution)/shard_map/ppermute | solution.py:29
  110.7 7.7 %collective-permute-start.16 = (f32[2,32,1024]{2,1,0:T(8,128)S(1)}, f32[2,32,1024]{2,1,0:T(8,128)S(1)}, u32[]{:S(2)}, u32[]{:S(2)}) collective-permute-start(f32[2,32,1024]{2,1,0:T(8,128)S(1)} %constant_dynamic-slice_fusion.1), channel_id=1, source_target_pairs={{0,1},{1,0},{2,3},{3,2},{4,5},{5,4},{6,7},{7,6},{8,9},{9,8},{10,11... | collective-permute-start | bytes 786440 | tf_op jit(solution)/shard_map/ppermute | solution.py:29
  118.4 6.5 %collective-permute-start.19 = (f32[2,16,1024]{2,1,0:T(8,128)S(1)}, f32[2,16,1024]{2,1,0:T(8,128)S(1)}, u32[]{:S(2)}, u32[]{:S(2)}) collective-permute-start(f32[2,16,1024]{2,1,0:T(8,128)S(1)} %constant_dynamic-slice_fusion), channel_id=1, source_target_pairs={{0,2},{1,3},{2,0},{3,1},{4,6},{5,7},{6,4},{7,5},{8,10},{9,11},{10,... | collective-permute-start | bytes 393224 | tf_op jit(solution)/shard_map/ppermute | solution.py:29
  118.8 7.1 %collective-permute-start.17 = (f32[1,320,256]{2,1,0:T(8,128)S(1)}, f32[1,320,256]{2,1,0:T(8,128)S(1)}, u32[]{:S(2)}, u32[]{:S(2)}) collective-permute-start(f32[1,320,256]{2,1,0:T(8,128)S(1)} %pad_maximum_fusion.2), channel_id=1, source_target_pairs={{0,8},{4,12},{8,0},{12,4},{16,24},{20,28},{24,16},{28,20},{1,9},{5... | collective-permute-start | bytes 983048 | tf_op jit(solution)/shard_map/ppermute | solution.py:29
  120.9 7.1 %collective-permute-start.18 = (f32[1,320,256]{2,1,0:T(8,128)S(1)}, f32[1,320,256]{2,1,0:T(8,128)S(1)}, u32[]{:S(2)}, u32[]{:S(2)}) collective-permute-start(f32[1,320,256]{2,1,0:T(8,128)S(1)} %pad_maximum_fusion.3), channel_id=1, source_target_pairs={{0,16},{4,20},{8,24},{12,28},{16,0},{20,4},{24,8},{28,12},{1,17},{... | collective-permute-start | bytes 983048 | tf_op jit(solution)/shard_map/ppermute | solution.py:29
  128.1 3.1 %collective-permute-start.20 = (f32[2,640,256]{2,1,0:T(8,128)S(1)}, f32[2,640,256]{2,1,0:T(8,128)S(1)}, u32[]{:S(2)}, u32[]{:S(2)}) collective-permute-start(f32[2,640,256]{2,1,0:T(8,128)S(1)} %maximum_maximum_fusion.near_ref), channel_id=1, source_target_pairs={{0,4},{4,0},{8,12},{12,8},{16,20},{20,16},{24,28},{28,24},{1,5},{5... | collective-permute-start | bytes 3932168 | tf_op jit(solution)/shard_map/ppermute | solution.py:29
  139.6 5.4 %collective-permute-start.21 = (bf16[2,16,1024]{2,1,0:T(8,128)(2,1)S(1)}, bf16[2,16,1024]{2,1,0:T(8,128)(2,1)S(1)}, u32[]{:S(2)}, u32[]{:S(2)}) collective-permute-start(bf16[2,16,1024]{2,1,0:T(8,128)(2,1)S(1)} %bitcast.50), channel_id=1, source_target_pairs={{0,2},{1,3},{2,0},{3,1},{4,6},{5,7},{6,4},{7,5},{8,10},{9,11},{10,... | collective-permute-start | bytes 196616 | tf_op jit(solution)/shard_map/ppermute | solution.py:29
  145.0 5.6 %collective-permute-start.22 = (bf16[2,32,1024]{2,1,0:T(8,128)(2,1)S(1)}, bf16[2,32,1024]{2,1,0:T(8,128)(2,1)S(1)}, u32[]{:S(2)}, u32[]{:S(2)}) collective-permute-start(bf16[2,32,1024]{2,1,0:T(8,128)(2,1)S(1)} %pad_maximum_fusion.8), channel_id=1, source_target_pairs={{0,1},{1,0},{2,3},{3,2},{4,5},{5,4},{6,7},{7,6},{8,9},{9,8},{10,11... | collective-permute-start | bytes 393224 | tf_op jit(solution)/shard_map/ppermute | solution.py:29
  150.8 6.1 %collective-permute-start.23 = (bf16[1,64,1024]{2,1,0:T(8,128)(2,1)S(1)}, bf16[1,64,1024]{2,1,0:T(8,128)(2,1)S(1)}, u32[]{:S(2)}, u32[]{:S(2)}) collective-permute-start(bf16[1,64,1024]{2,1,0:T(8,128)(2,1)S(1)} %get-tuple-element.63), channel_id=1, source_target_pairs={{0,16},{4,20},{8,24},{12,28},{16,0},{20,4},{24,8},{28,12},{1,17},{... | collective-permute-start | bytes 393224 | tf_op jit(solution)/shard_map/ppermute | solution.py:29
  153.8 5.4 %collective-permute-start.25 = (bf16[1,64,1024]{2,1,0:T(8,128)(2,1)S(1)}, bf16[1,64,1024]{2,1,0:T(8,128)(2,1)S(1)}, u32[]{:S(2)}, u32[]{:S(2)}) collective-permute-start(bf16[1,64,1024]{2,1,0:T(8,128)(2,1)S(1)} %get-tuple-element.64), channel_id=1, source_target_pairs={{0,8},{4,12},{8,0},{12,4},{16,24},{20,28},{24,16},{28,20},{1,9},{5... | collective-permute-start | bytes 393224 | tf_op jit(solution)/shard_map/ppermute | solution.py:29
  156.9 7.5 %collective-permute-start.24 = (bf16[1,128,1024]{2,1,0:T(8,128)(2,1)S(1)}, bf16[1,128,1024]{2,1,0:T(8,128)(2,1)S(1)}, u32[]{:S(2)}, u32[]{:S(2)}) collective-permute-start(bf16[1,128,1024]{2,1,0:T(8,128)(2,1)S(1)} %pad_maximum_fusion.4), channel_id=1, source_target_pairs={{0,8},{4,12},{8,0},{12,4},{16,24},{20,28},{24,16},{28,20},{1,9},{5... | collective-permute-start | bytes 786440 | tf_op jit(solution)/shard_map/ppermute | solution.py:29
  159.2 6.4 %collective-permute-start.26 = (bf16[1,128,1024]{2,1,0:T(8,128)(2,1)S(1)}, bf16[1,128,1024]{2,1,0:T(8,128)(2,1)S(1)}, u32[]{:S(2)}, u32[]{:S(2)}) collective-permute-start(bf16[1,128,1024]{2,1,0:T(8,128)(2,1)S(1)} %pad_maximum_fusion.5), channel_id=1, source_target_pairs={{0,16},{4,20},{8,24},{12,28},{16,0},{20,4},{24,8},{28,12},{1,17},{... | collective-permute-start | bytes 786440 | tf_op jit(solution)/shard_map/ppermute | solution.py:29
  164.4 2.7 %copy-start.2 = (bf16[2048,1024]{1,0:T(8,128)(2,1)S(1)}, bf16[2048,1024]{1,0:T(8,128)(2,1)}, u32[]{:S(2)}) copy-start(bf16[2048,1024]{1,0:T(8,128)(2,1)} %fusion) | copy-start | bytes 12582916
  165.8 5.3 %collective-permute-start.27 = (bf16[512,1024]{1,0:T(8,128)(2,1)S(1)}, bf16[512,1024]{1,0:T(8,128)(2,1)S(1)}, u32[]{:S(2)}, u32[]{:S(2)}) collective-permute-start(bf16[512,1024]{1,0:T(8,128)(2,1)S(1)} %bitcast.56), channel_id=1, source_target_pairs={{0,4},{4,0},{8,12},{12,8},{16,20},{20,16},{24,28},{28,24},{1,5},{5... | collective-permute-start | bytes 3145736 | tf_op jit(solution)/shard_map/ppermute | solution.py:29
  166.5 2.2 %copy-start.1 = (bf16[2048,1024]{1,0:T(8,128)(2,1)S(1)}, bf16[2048,1024]{1,0:T(8,128)(2,1)}, u32[]{:S(2)}) copy-start(bf16[2048,1024]{1,0:T(8,128)(2,1)} %param.11) | copy-start | bytes 12582916
  173.5 2.0 %copy-start.3 = (bf16[2048,1024]{1,0:T(8,128)(2,1)}, bf16[2048,1024]{1,0:T(8,128)(2,1)S(1)}, u32[]{:S(2)}) copy-start(bf16[2048,1024]{1,0:T(8,128)(2,1)S(1)} %fusion.2) | copy-start | bytes 12582916

commit v4 on v3

--- a/solution.py
+++ b/solution.py
@@ -12,6 +12,7 @@
 MAX_STEPS = 4096
 REFRESH = 32
 FIRST_STEPS = 3
+HINT = 20000000000
 HOLD = 4
 
 
@@ -43,6 +44,15 @@
     other = swap(vals, dim)
     low = my_bit(dim) == 0
     return jnp.concatenate([jnp.where(low, vals, other), jnp.where(low, other, vals)], axis=1)
+
+
+def gather(vals, axis):
+    count, mine = lax.axis_size(axis), lax.axis_index(axis)
+    pairs = lambda flip: [(i, i ^ flip) for i in range(count)]
+    got = [vals] + [lax.ppermute(vals, axis, pairs(flip)) for flip in range(1, count)]
+    bits = count.bit_length() - 1
+    in_order = [sum((i >> b & 1) << (bits - 1 - b) for b in range(bits)) for i in range(count)]
+    return jnp.concatenate([lax.select_n(mine ^ i, *got) for i in in_order], axis=1)
 
 
 def stages():
@@ -198,10 +208,27 @@
             square,
             pltpu.VMEM((1, members), jnp.float32),
         ],
-        compiler_params=pltpu.CompilerParams(vmem_limit_bytes=40 * 1024 * 1024),
+        compiler_params=pltpu.CompilerParams(vmem_limit_bytes=20 * 1024 * 1024),
         cost_estimate=pl.CostEstimate(flops=24 * 2 * rhs.shape[0] * members * members, bytes_accessed=6 * members * members, transcendentals=0),
         name="member_solve",
     )(bit, near, far, rhs)
+
+
+def places_kernel(slot_ref, out_ref):
+    ids = lax.broadcasted_iota(jnp.int32, out_ref.shape, 0)
+    out_ref[...] = jnp.where(ids == slot_ref[...], 1.0, 0.0).astype(jnp.bfloat16)
+
+
+def places(slots, rows):
+    vmem = pl.BlockSpec(memory_space=pltpu.VMEM)
+    return pl.pallas_call(
+        places_kernel,
+        out_shape=jax.ShapeDtypeStruct((rows, slots.shape[1]), jnp.bfloat16),
+        in_specs=[vmem],
+        out_specs=vmem,
+        cost_estimate=pl.CostEstimate(flops=HINT, bytes_accessed=2 * rows * slots.shape[1], transcendentals=0),
+        name="places",
+    )(slots)
 
 
 def weighted(vals, root_weight):
@@ -242,16 +269,19 @@
             for j in range(0, members, TILE)
         ]
     )
-    ahead_steps = steps_of(halve) + steps_of(double)[:0:-1]
-    gram = (tiles.reshape(2, -1, TILE),)
-    for step in ahead_steps[:HOLD]:
-        gram = step(gram)
-
     mine = index_table // rows == me
     mine_ahead = jnp.dot(mine.astype(bf16), earlier, preferred_element_type=f32).astype(jnp.int32)
     chosen = mine[:, None, :] & (mine_ahead[:, None, :] == jnp.arange(capacity, dtype=jnp.int32)[None, :, None])
     slot_of = jnp.sum(jnp.where(chosen, index_table[:, None, :] % rows + 1, 0), axis=2).reshape(1, -1) - 1
-    unpack = (ids[:, None] == slot_of).astype(bf16)
+    unpack = places(slot_of, rows)
+    last = stages()[2][-1]
+    ahead_steps = steps_of(halve)[:-1] + [lambda parts: (merged(parts) + swap(merged(parts), last),)] + steps_of(double)[-2:0:-1]
+    gram = (tiles.reshape(2, -1, TILE),)
+    for i, step in enumerate(ahead_steps[:HOLD]):
+        gram = step(gram)
+        if i == 0:
+            gram = after(gram, unpack)
+
     arranged = jnp.dot(unpack, got.reshape(-1, members), preferred_element_type=f32).astype(bf16)
 
     pred_vals = arranged.astype(f32)
@@ -269,31 +299,34 @@
         cols = lax.dynamic_slice_in_dim(innovation, side * wide, wide, 1)
         return jnp.dot(cols.T, anomalies, preferred_element_type=f32).reshape(2, -1, members)
 
-    block_vals = unknowns.astype(f32)
-    spread = (block_vals - jnp.mean(block_vals, axis=1, keepdims=True)).astype(bf16)
 
     later = iter(ahead_steps[HOLD:])
-    gram, send, spread = lax.optimization_barrier((gram, cross_part(1 - bit), spread))
+    gram, send = lax.optimization_barrier((gram, cross_part(1 - bit)))
     cross = (cross_part(bit) + swap(send, head),)
     gram = next(later)(gram)
-    for step in steps_of(halve)[1:]:
-        gram, cross = lax.optimization_barrier((gram, cross))
-        gram, cross = next(later, lambda parts: parts)(gram), step(cross)
+    for i, step in enumerate(steps_of(halve)[1:]):
+        cross = step(cross)
+        if i == 0:
+            gram = after(gram, cross[0])
+        gram = next(later, lambda parts: parts)(gram)
     for step in later:
         gram = step(gram)
     near, cross = lax.optimization_barrier((merged(gram), merged(cross)))
     side = jnp.reshape(bit, (1,)).astype(jnp.int32)
     gain = solve(side, near, swap(near, head), cross.reshape(-1, members)).reshape(2, -1, members)
 
-    gain = (gain,)
-    for step in steps_of(double)[:0:-1]:
+    gain = (gather(gain, "obs"),)
+    block = after(unknowns, gain)
+    block_vals = block.astype(f32)
+    spread = (block_vals - jnp.mean(block_vals, axis=1, keepdims=True)).astype(bf16)
+    for step in steps_of(double)[len(stages()[1][0]) : 0 : -1]:
         gain = step(gain)
     gain = merged(gain).reshape(wide, members)
     other = swap(gain, head)
 
     def side_of(gain, at):
         moved = lax.dot_general(spread, gain, (((1,), (1,)), ((), ())), preferred_element_type=f32)
-        return (lax.dynamic_slice_in_dim(unknowns, at, wide, 1).astype(f32) + moved).astype(bf16)
+        return (lax.dynamic_slice_in_dim(block, at, wide, 1).astype(f32) + moved).astype(bf16)
 
     updated = lax.dynamic_update_slice_in_dim(jnp.zeros_like(unknowns), side_of(gain, bit * wide), bit * wide, 1)
     updated = lax.dynamic_update_slice_in_dim(updated, side_of(other, (1 - bit) * wide), (1 - bit) * wide, 1)

time: 176 us -> 169 us (0.960)
  waiting for transfers between devices: 87.5 us -> 78.2 us
  Pallas kernels: 8.44 us -> 11.7 us
  other arithmetic: 11.1 us -> 8.52 us
  matrix products: 17.4 us -> 19.5 us
    ppermute x28 -> x25, waiting for transfers between devices: 82.9 us -> 69.6 us  [swap(): lax.ppermute(vals, axis, [(i, i ^ 1 << b) for i in range(lax.axis_size(ax...]
    ppermute x28 -> x25, starting transfers between devices: 31.7 us -> 27 us  [swap(): lax.ppermute(vals, axis, [(i, i ^ 1 << b) for i in range(lax.axis_size(ax...]
    ppermute x0 -> x3, starting transfers between devices: none -> 4.45 us  [gather(): lax.ppermute(vals, axis, pairs(flip))]
    ppermute x0 -> x3, waiting for transfers between devices: none -> 4.23 us  [gather(): lax.ppermute(vals, axis, pairs(flip))]
    unnamed x19 -> x14, local copies, waits for them, and re-layouts: 5.31 us -> 2.04 us
    convert_element_type x1 -> x0, other arithmetic: 2.76 us -> none  [on_device(): (block_vals - jnp.mean(block_vals, axis=1, keepdims=True)).astype(bf16)]
    dynamic_slice x12 -> x10, local copies, waits for them, and re-layouts: 0.38 us -> 2.98 us  [halves(): lax.dynamic_slice_in_dim(vals, b * half, half, 1)]
    reduce_sum x1, other arithmetic: 2.89 us -> 0.62 us  [on_device(): jnp.mean(block_vals, axis=1, keepdims=True)]
  transfers between devices with their start and end apart: 30 -> 30, of which waited for: 26 -> 25; matrix products, arithmetic and copies ran while one was open for 11% -> 12% of each run, Pallas kernels for 0% -> 1%
where the time goes in v4:
time: 169 us
  waiting for transfers between devices  78.2 us (46%)
  starting transfers between devices  42.4 us (25%)
  matrix products  19.5 us (12%)
  Pallas kernels  11.7 us (7%)
  other arithmetic  8.52 us (5%)
  local copies, waits for them, and re-layouts  7.13 us (4%)
    ppermute x25, waiting for transfers between devices, swap(): lax.ppermute(vals, axis, [(i, i ^ 1 << b) for i in range(lax.axis_size(ax...  69.6 us
    ppermute x25, starting transfers between devices, swap(): lax.ppermute(vals, axis, [(i, i ^ 1 << b) for i in range(lax.axis_size(ax...  27 us
    pallas_call x1, Pallas kernels, solve(): pl.pallas_call(solve_kernel, out_shape=jax.ShapeDtypeStruct(rhs.shape, jn...  9.84 us
    all_to_all x1, starting transfers between devices, on_device(): lax.all_to_all(jnp.broadcast_to(own, (shards, 2, rows)), AXES, split_axis...  7.3 us
    dot_general x2, matrix products, side_of(): lax.dot_general(spread, gain, (((1,), (1,)), ((), ())), preferred_element...  5.29 us
    ppermute x3, starting transfers between devices, gather(): lax.ppermute(vals, axis, pairs(flip))  4.45 us
    dot_general x2, matrix products, cross_part(): jnp.dot(cols.T, anomalies, preferred_element_type=f32)  4.34 us
    ppermute x3, waiting for transfers between devices, gather(): lax.ppermute(vals, axis, pairs(flip))  4.23 us
  transfers between devices with their start and end apart: 30, of which 25 were waited for; matrix products, arithmetic and copies ran while one was open for 12% of the time, Pallas kernels for 1%

profile of v4, /device:TPU:0, one launch (start us, length us, event | category | flops | bytes accessed | tf_op | source)
XLA Modules:
  0.0 168.7 jit_solution(11313146800028169693)
XLA Ops:
  2.8 7.3 %all-to-all-start = ((f32[32,2,512]{2,1,0:T(2,128)}), f32[32,2,512]{2,1,0:T(2,128)S(1)}, u32[]{:S(2)}, u32[]{:S(2)}) async-start(f32[32,2,512]{2,1,0:T(2,128)} %broadcast_in_dim.19), calls=%async_computation | async-start | bytes 262144 | tf_op jit(solution)/shard_map/all_to_all | solution.py:259
  10.3 1.4 convert_reduce_fusion.2
  11.7 3.8 %fusion.9 = bf16[1024,1024]{1,0:T(8,128)(2,1)} fusion(bf16[512,1024]{1,0:T(8,128)(2,1)} %param.6, s32[512]{0:T(512)S(1)} %convert_add_fusion), kind=kOutput, calls=%fused_computation.24 | convolution fusion | flops 1075314688 | bytes 3147776 | tf_op jit(solution)/shard_map/dot_general | solution.py:255
  15.5 2.9 %all-to-all-done = f32[32,2,512]{2,1,0:T(2,128)S(1)} async-done(((f32[32,2,512]{2,1,0:T(2,128)}), f32[32,2,512]{2,1,0:T(2,128)S(1)}, u32[]{:S(2)}, u32[]{:S(2)}) %all-to-all-start) | async-done | bytes 131104 | tf_op jit(solution)/shard_map/all_to_all | solution.py:259
  18.5 3.6 %all-to-all-start.1 = ((bf16[32,32,1024]{2,1,0:T(8,128)(2,1)}), bf16[32,32,1024]{2,1,0:T(8,128)(2,1)}, u32[]{:S(2)}, u32[]{:S(2)}) async-start(bf16[32,32,1024]{2,1,0:T(8,128)(2,1)} %bitcast.5), calls=%async_computation.1 | async-start | bytes 4194304 | tf_op jit(solution)/shard_map/all_to_all | solution.py:256
  24.9 1.2 constant_dynamic-slice_fusion.9
  27.7 1.9 %places.1 = bf16[512,1024]{1,0:T(8,128)(2,1)} custom-call(s32[1,1024]{1,0:T(1,128)} %sub.76.slot_ref), custom_call_target="tpu_custom_call" | custom-call | flops 20000000000 | bytes 1048576 | tf_op jit(solution)/shard_map/places/pallas_call | solution.py:224
  29.6 1.5 dynamic-slice_add_fusion
  31.2 1.8 %collective-permute-start.3 = (f32[1,320,256]{2,1,0:T(8,128)S(1)}, f32[1,320,256]{2,1,0:T(8,128)S(1)}, u32[]{:S(2)}, u32[]{:S(2)}) collective-permute-start(f32[1,320,256]{2,1,0:T(8,128)S(1)} %constant_dynamic-slice_fusion.6), channel_id=1, source_target_pairs={{0,16},{4,20},{8,24},{12,28},{16,0},{20,4},{24,8},{28,12},{1,17},{... | collective-permute-start | bytes 983048 | tf_op jit(solution)/shard_map/ppermute | solution.py:30
  33.0 1.5 collective-permute-start.1
  34.6 14.7 %collective-permute-done.3 = f32[1,320,256]{2,1,0:T(8,128)S(1)} collective-permute-done((f32[1,320,256]{2,1,0:T(8,128)S(1)}, f32[1,320,256]{2,1,0:T(8,128)S(1)}, u32[]{:S(2)}, u32[]{:S(2)}) %collective-permute-start.3) | collective-permute-done | bytes 327712 | tf_op jit(solution)/shard_map/ppermute | solution.py:30
  49.4 1.2 collective-permute-start.4
  50.7 1.8 %collective-permute-start.2 = (f32[1,160,256]{2,1,0:T(8,128)S(1)}, f32[1,160,256]{2,1,0:T(8,128)S(1)}, u32[]{:S(2)}, u32[]{:S(2)}) collective-permute-start(f32[1,160,256]{2,1,0:T(8,128)S(1)} %constant_dynamic-slice_fusion.7), channel_id=1, source_target_pairs={{0,16},{4,20},{8,24},{12,28},{16,0},{20,4},{24,8},{28,12},{1,17},{... | collective-permute-start | bytes 491528 | tf_op jit(solution)/shard_map/ppermute | solution.py:30
  52.5 4.2 %collective-permute-done.4 = f32[1,160,256]{2,1,0:T(8,128)S(1)} collective-permute-done((f32[1,160,256]{2,1,0:T(8,128)S(1)}, f32[1,160,256]{2,1,0:T(8,128)S(1)}, u32[]{:S(2)}, u32[]{:S(2)}) %collective-permute-start.4) | collective-permute-done | bytes 163872 | tf_op jit(solution)/shard_map/ppermute | solution.py:30
  56.7 2.3 %collective-permute-done.2 = f32[1,160,256]{2,1,0:T(8,128)S(1)} collective-permute-done((f32[1,160,256]{2,1,0:T(8,128)S(1)}, f32[1,160,256]{2,1,0:T(8,128)S(1)}, u32[]{:S(2)}, u32[]{:S(2)}) %collective-permute-start.2) | collective-permute-done | bytes 163872 | tf_op jit(solution)/shard_map/ppermute | solution.py:30
  59.1 1.3 collective-permute-start.5
  60.4 7.6 %collective-permute-done.5 = f32[2,80,256]{2,1,0:T(8,128)S(1)} collective-permute-done((f32[2,80,256]{2,1,0:T(8,128)S(1)}, f32[2,80,256]{2,1,0:T(8,128)S(1)}, u32[]{:S(2)}, u32[]{:S(2)}) %collective-permute-start.5) | collective-permute-done | bytes 163872 | tf_op jit(solution)/shard_map/ppermute | solution.py:30
  68.1 1.5 all-to-all-done.1
  69.6 3.5 %multiply_reduce_fusion = (f32[512]{0:T(512)S(1)}, f32[512]{0:T(512)S(1)}, bf16[512,1024]{1,0:T(8,128)(2,1)S(1)}, bf16[512,1024]{1,0:T(8,128)(2,1)S(1)}) fusion(bf16[512,1024]{1,0:T(8,128)(2,1)S(1)} %copy-done.4, f32[512]{0:T(512)S(1)} %copy-done.5, f32[512]{0:T(512)S(1)} %divide_sqrt_fusion, bf16[512,1024]{1,0:T(8,128)(2,1)} %places.1, ...), kind=kOutput, calls=%fused_computation.17 | convolution fusion | flops 1078983680 | bytes 6299648 | tf_op jit(solution)/shard_map/dot_general | solution.py:285
  73.1 2.2 %fusion.21 = f32[512,1024]{1,0:T(8,128)} fusion(bf16[512,1024]{1,0:T(8,128)(2,1)S(1)} %get-tuple-element.20, s32[]{:T(128)S(6)} %select_n.355, bf16[512,1024]{1,0:T(8,128)(2,1)S(1)} %get-tuple-element.58, f32[512]{0:T(512)S(1)} %broadcast_multiply_fusion.2, f32[512]{0:T(512)S(1)} %divide_sqrt_fusion), kind=kOutput, calls=%fused_computation.49 | convolution fusion | flops 538968064 | bytes 3674116 | tf_op jit(solution)/shard_map/dot_general | solution.py:300
  75.4 1.0 collective-permute-start.7
  76.4 2.1 %fusion.19 = f32[512,1024]{1,0:T(8,128)S(1)} fusion(bf16[512,1024]{1,0:T(8,128)(2,1)S(1)} %get-tuple-element.20, s32[]{:T(128)S(6)} %select_n.356, bf16[512,1024]{1,0:T(8,128)(2,1)} %copy-done.6, f32[512]{0:T(512)S(1)} %broadcast_multiply_fusion.2, f32[512]{0:T(512)S(1)} %divide_sqrt_fusion), kind=kOutput, calls=%fused_computation.47 | convolution fusion | flops 538968064 | bytes 3674116 | tf_op jit(solution)/shard_map/dot_general | solution.py:300
  78.5 1.9 %collective-permute-done.7 = f32[2,256,1024]{2,1,0:T(8,128)S(1)} collective-permute-done((f32[2,256,1024]{2,1,0:T(8,128)}, f32[2,256,1024]{2,1,0:T(8,128)S(1)}, u32[]{:S(2)}, u32[]{:S(2)}) %collective-permute-start.7) | collective-permute-done | bytes 2097184 | tf_op jit(solution)/shard_map/ppermute | solution.py:30
  81.8 2.1 %collective-permute-start.8 = (f32[1,128,1024]{2,1,0:T(8,128)}, f32[1,128,1024]{2,1,0:T(8,128)S(1)}, u32[]{:S(2)}, u32[]{:S(2)}) collective-permute-start(f32[1,128,1024]{2,1,0:T(8,128)} %constant_dynamic-slice_fusion.4), channel_id=1, source_target_pairs={{0,8},{4,12},{8,0},{12,4},{16,24},{20,28},{24,16},{28,20},{1,9},{5... | collective-permute-start | bytes 1572872 | tf_op jit(solution)/shard_map/ppermute | solution.py:30
  86.1 9.5 %collective-permute-done.6 = f32[2,80,256]{2,1,0:T(8,128)S(1)} collective-permute-done((f32[2,80,256]{2,1,0:T(8,128)S(1)}, f32[2,80,256]{2,1,0:T(8,128)S(1)}, u32[]{:S(2)}, u32[]{:S(2)}) %collective-permute-start.6) | collective-permute-done | bytes 163872 | tf_op jit(solution)/shard_map/ppermute | solution.py:30
  96.6 2.0 %collective-permute-start.9 = (f32[2,80,256]{2,1,0:T(8,128)S(1)}, f32[2,80,256]{2,1,0:T(8,128)S(1)}, u32[]{:S(2)}, u32[]{:S(2)}) collective-permute-start(f32[2,80,256]{2,1,0:T(8,128)S(1)} %add.212), channel_id=1, source_target_pairs={{0,1},{1,0},{2,3},{3,2},{4,5},{5,4},{6,7},{7,6},{8,9},{9,8},{10,11... | collective-permute-start | bytes 491528 | tf_op jit(solution)/shard_map/ppermute | solution.py:30
  99.3 1.3 collective-permute-start.14
  100.6 2.0 %collective-permute-done.9 = f32[2,80,256]{2,1,0:T(8,128)S(1)} collective-permute-done((f32[2,80,256]{2,1,0:T(8,128)S(1)}, f32[2,80,256]{2,1,0:T(8,128)S(1)}, u32[]{:S(2)}, u32[]{:S(2)}) %collective-permute-start.9) | collective-permute-done | bytes 163872 | tf_op jit(solution)/shard_map/ppermute | solution.py:30
  103.6 1.2 collective-permute-start.12
  104.8 3.4 %collective-permute-done.16 = f32[1,64,1024]{2,1,0:T(8,128)S(1)} collective-permute-done((f32[1,64,1024]{2,1,0:T(8,128)S(1)}, f32[1,64,1024]{2,1,0:T(8,128)S(1)}, u32[]{:S(2)}, u32[]{:S(2)}) %collective-permute-start.16) | collective-permute-done | bytes 262176 | tf_op jit(solution)/shard_map/ppermute | solution.py:30
  108.7 1.4 collective-permute-start.17
  110.4 1.5 collective-permute-start.11
  112.6 3.7 %collective-permute-done.17 = f32[2,32,1024]{2,1,0:T(8,128)S(1)} collective-permute-done((f32[2,32,1024]{2,1,0:T(8,128)S(1)}, f32[2,32,1024]{2,1,0:T(8,128)S(1)}, u32[]{:S(2)}, u32[]{:S(2)}) %collective-permute-start.17) | collective-permute-done | bytes 262176 | tf_op jit(solution)/shard_map/ppermute | solution.py:30
  116.5 1.9 %collective-permute-done.11 = f32[1,320,256]{2,1,0:T(8,128)S(1)} collective-permute-done((f32[1,320,256]{2,1,0:T(8,128)S(1)}, f32[1,320,256]{2,1,0:T(8,128)S(1)}, u32[]{:S(2)}, u32[]{:S(2)}) %collective-permute-start.11) | collective-permute-done | bytes 327712 | tf_op jit(solution)/shard_map/ppermute | solution.py:30
  119.5 4.2 %collective-permute-done.18 = f32[2,16,1024]{2,1,0:T(8,128)S(1)} collective-permute-done((f32[2,16,1024]{2,1,0:T(8,128)S(1)}, f32[2,16,1024]{2,1,0:T(8,128)S(1)}, u32[]{:S(2)}, u32[]{:S(2)}) %collective-permute-start.18) | collective-permute-done | bytes 131104 | tf_op jit(solution)/shard_map/ppermute | solution.py:30
  123.8 3.0 %collective-permute-done.19.far_ref = f32[2,640,256]{2,1,0:T(8,128)S(1)} collective-permute-done((f32[2,640,256]{2,1,0:T(8,128)S(1)}, f32[2,640,256]{2,1,0:T(8,128)S(1)}, u32[]{:S(2)}, u32[]{:S(2)}) %collective-permute-start.19) | collective-permute-done | bytes 1310752 | tf_op jit(solution)/shard_map/ppermute | solution.py:30
  126.8 9.8 %member_solve.1 = bf16[32,1024]{1,0:T(8,128)(2,1)S(1)} custom-call(s32[1]{0:T(128)} %bitcast.bit_ref, f32[2,640,256]{2,1,0:T(8,128)S(1)} %maximum_maximum_fusion.near_ref, f32[2,640,256]{2,1,0:T(8,128)S(1)} %collective-permute-done.19.far_ref, f32[32,1024]{1,0:T(8,128)S(1)} %bitcast.48), custom_call_target="tpu_custom_call" | custom-call | flops 1610612736 | bytes 6291456 | tf_op jit(solution)/shard_map/member_solve/pallas_call | solution.py:199
  137.0 1.3 collective-permute-start.21
  138.3 2.8 %collective-permute-start.22 = (bf16[2,16,1024]{2,1,0:T(8,128)(2,1)S(1)}, bf16[2,16,1024]{2,1,0:T(8,128)(2,1)S(1)}, u32[]{:S(2)}, u32[]{:S(2)}) collective-permute-start(bf16[2,16,1024]{2,1,0:T(8,128)(2,1)S(1)} %bitcast.51), channel_id=1, source_target_pairs={{0,3},{1,2},{2,1},{3,0},{4,7},{5,6},{6,5},{7,4},{8,11},{9,10},{10,... | collective-permute-start | bytes 196616 | tf_op jit(solution)/shard_map/ppermute | solution.py:52
  141.8 3.5 %collective-permute-done.21 = bf16[2,16,1024]{2,1,0:T(8,128)(2,1)S(1)} collective-permute-done((bf16[2,16,1024]{2,1,0:T(8,128)(2,1)S(1)}, bf16[2,16,1024]{2,1,0:T(8,128)(2,1)S(1)}, u32[]{:S(2)}, u32[]{:S(2)}) %collective-permute-start.21) | collective-permute-done | bytes 65568 | tf_op jit(solution)/shard_map/ppermute | solution.py:52
  146.1 1.5 collective-permute-start.25
  147.6 2.9 %collective-permute-done.23 = bf16[1,64,1024]{2,1,0:T(8,128)(2,1)S(1)} collective-permute-done((bf16[1,64,1024]{2,1,0:T(8,128)(2,1)S(1)}, bf16[1,64,1024]{2,1,0:T(8,128)(2,1)S(1)}, u32[]{:S(2)}, u32[]{:S(2)}) %collective-permute-start.23) | collective-permute-done | bytes 131104 | tf_op jit(solution)/shard_map/ppermute | solution.py:30
  151.1 2.3 %collective-permute-start.24 = (bf16[1,128,1024]{2,1,0:T(8,128)(2,1)S(1)}, bf16[1,128,1024]{2,1,0:T(8,128)(2,1)S(1)}, u32[]{:S(2)}, u32[]{:S(2)}) collective-permute-start(bf16[1,128,1024]{2,1,0:T(8,128)(2,1)S(1)} %pad_maximum_fusion.4), channel_id=1, source_target_pairs={{0,8},{4,12},{8,0},{12,4},{16,24},{20,28},{24,16},{28,20},{1,9},{5... | collective-permute-start | bytes 786440 | tf_op jit(solution)/shard_map/ppermute | solution.py:30
  154.8 3.0 %collective-permute-done.24 = bf16[1,128,1024]{2,1,0:T(8,128)(2,1)S(1)} collective-permute-done((bf16[1,128,1024]{2,1,0:T(8,128)(2,1)S(1)}, bf16[1,128,1024]{2,1,0:T(8,128)(2,1)S(1)}, u32[]{:S(2)}, u32[]{:S(2)}) %collective-permute-start.24) | collective-permute-done | bytes 262176 | tf_op jit(solution)/shard_map/ppermute | solution.py:30
  157.9 2.0 %collective-permute-done.26 = bf16[1,128,1024]{2,1,0:T(8,128)(2,1)S(1)} collective-permute-done((bf16[1,128,1024]{2,1,0:T(8,128)(2,1)S(1)}, bf16[1,128,1024]{2,1,0:T(8,128)(2,1)S(1)}, u32[]{:S(2)}, u32[]{:S(2)}) %collective-permute-start.26) | collective-permute-done | bytes 262176 | tf_op jit(solution)/shard_map/ppermute | solution.py:30
  161.4 2.6 %fusion.1 = bf16[2048,1024]{1,0:T(8,128)(2,1)S(1)} fusion(bf16[2048,1024]{1,0:T(8,128)(2,1)S(1)} %broadcast_in_dim.18, s32[]{:T(128)S(6)} %select_n.356, bf16[512,1024]{1,0:T(8,128)(2,1)S(1)} %bitcast.57, bf16[2048,1024]{1,0:T(8,128)(2,1)S(1)} %copy-done, f32[2048]{0:T(1024)S(1)} %broadcast_multiply_fusion), kind=kOutput, calls=%fused_computation.8 | convolution fusion | flops 2156920832 | bytes 9445380 | tf_op jit(solution)/shard_map/dot_general | solution.py:328
  164.0 2.6 %fusion.2 = bf16[2048,1024]{1,0:T(8,128)(2,1)S(1)} fusion(bf16[2048,1024]{1,0:T(8,128)(2,1)S(1)} %fusion.1, s32[]{:T(128)S(6)} %select_n.355, bf16[512,1024]{1,0:T(8,128)(2,1)S(1)} %collective-permute-done.27, bf16[2048,1024]{1,0:T(8,128)(2,1)S(1)} %copy-done, f32[2048]{0:T(1024)S(1)} %broadcast_multiply_fusion), kind=kOutput, calls=%fused_computation.9 | convolution fusion | flops 2156920832 | bytes 9445380 | tf_op jit(solution)/shard_map/dot_general | solution.py:328
  166.7 2.0 %copy-done.1 = bf16[2048,1024]{1,0:T(8,128)(2,1)} copy-done((bf16[2048,1024]{1,0:T(8,128)(2,1)}, bf16[2048,1024]{1,0:T(8,128)(2,1)S(1)}, u32[]{:S(2)}) %copy-start.1) | copy-done | bytes 4194328
  (107 shorter events, 21.5 us)
Async XLA Ops:
  2.8 15.7 %all-to-all-start = ((f32[32,2,512]{2,1,0:T(2,128)}), f32[32,2,512]{2,1,0:T(2,128)S(1)}, u32[]{:S(2)}, u32[]{:S(2)}) async-start(f32[32,2,512]{2,1,0:T(2,128)} %broadcast_in_dim.19), calls=%async_computation | async-start | bytes 262144 | tf_op jit(solution)/shard_map/all_to_all | solution.py:259
  18.5 4.4 %copy-start.2 = (bf16[512,1024]{1,0:T(8,128)(2,1)S(1)}, bf16[512,1024]{1,0:T(8,128)(2,1)}, u32[]{:S(2)}) copy-start(bf16[512,1024]{1,0:T(8,128)(2,1)} %param.6) | copy-start | bytes 3145732
  18.5 51.1 %all-to-all-start.1 = ((bf16[32,32,1024]{2,1,0:T(8,128)(2,1)}), bf16[32,32,1024]{2,1,0:T(8,128)(2,1)}, u32[]{:S(2)}, u32[]{:S(2)}) async-start(bf16[32,32,1024]{2,1,0:T(8,128)(2,1)} %bitcast.5), calls=%async_computation.1 | async-start | bytes 4194304 | tf_op jit(solution)/shard_map/all_to_all | solution.py:256
  26.1 3.5 %collective-permute-start = (f32[2,640,256]{2,1,0:T(8,128)}, f32[2,640,256]{2,1,0:T(8,128)}, u32[]{:S(2)}, u32[]{:S(2)}) collective-permute-start(f32[2,640,256]{2,1,0:T(8,128)} %constant_dynamic-slice_fusion.9), channel_id=1, source_target_pairs={{0,4},{4,0},{8,12},{12,8},{16,20},{20,16},{24,28},{28,24},{1,5},{5... | collective-permute-start | bytes 3932168 | tf_op jit(solution)/shard_map/ppermute | solution.py:30
  31.2 18.1 %collective-permute-start.3 = (f32[1,320,256]{2,1,0:T(8,128)S(1)}, f32[1,320,256]{2,1,0:T(8,128)S(1)}, u32[]{:S(2)}, u32[]{:S(2)}) collective-permute-start(f32[1,320,256]{2,1,0:T(8,128)S(1)} %constant_dynamic-slice_fusion.6), channel_id=1, source_target_pairs={{0,16},{4,20},{8,24},{12,28},{16,0},{20,4},{24,8},{28,12},{1,17},{... | collective-permute-start | bytes 983048 | tf_op jit(solution)/shard_map/ppermute | solution.py:30
  33.0 27.4 %copy-start.3 = (f32[512]{0:T(512)S(1)}, f32[512]{0:T(512)}, u32[]{:S(2)}) copy-start(f32[512]{0:T(512)} %param.9) | copy-start | bytes 6148
  33.0 17.6 %collective-permute-start.1 = (f32[1,320,256]{2,1,0:T(8,128)S(1)}, f32[1,320,256]{2,1,0:T(8,128)S(1)}, u32[]{:S(2)}, u32[]{:S(2)}) collective-permute-start(f32[1,320,256]{2,1,0:T(8,128)S(1)} %constant_dynamic-slice_fusion.8), channel_id=1, source_target_pairs={{0,8},{4,12},{8,0},{12,4},{16,24},{20,28},{24,16},{28,20},{1,9},{5... | collective-permute-start | bytes 983048 | tf_op jit(solution)/shard_map/ppermute | solution.py:30
  49.3 20.2 %copy-start.4 = (bf16[512,1024]{1,0:T(8,128)(2,1)S(1)}, bf16[512,1024]{1,0:T(8,128)(2,1)}, u32[]{:S(2)}) copy-start(bf16[512,1024]{1,0:T(8,128)(2,1)} %param.10) | copy-start | bytes 3145732
  49.3 20.2 %copy-start.5 = (f32[512]{0:T(512)S(1)}, f32[512]{0:T(512)}, u32[]{:S(2)}) copy-start(f32[512]{0:T(512)} %param.8) | copy-start | bytes 6148
  49.4 7.3 %collective-permute-start.4 = (f32[1,160,256]{2,1,0:T(8,128)S(1)}, f32[1,160,256]{2,1,0:T(8,128)S(1)}, u32[]{:S(2)}, u32[]{:S(2)}) collective-permute-start(f32[1,160,256]{2,1,0:T(8,128)S(1)} %constant_dynamic-slice_fusion.5), channel_id=1, source_target_pairs={{0,8},{4,12},{8,0},{12,4},{16,24},{20,28},{24,16},{28,20},{1,9},{5... | collective-permute-start | bytes 491528 | tf_op jit(solution)/shard_map/ppermute | solution.py:30
  50.7 8.3 %collective-permute-start.2 = (f32[1,160,256]{2,1,0:T(8,128)S(1)}, f32[1,160,256]{2,1,0:T(8,128)S(1)}, u32[]{:S(2)}, u32[]{:S(2)}) collective-permute-start(f32[1,160,256]{2,1,0:T(8,128)S(1)} %constant_dynamic-slice_fusion.7), channel_id=1, source_target_pairs={{0,16},{4,20},{8,24},{12,28},{16,0},{20,4},{24,8},{28,12},{1,17},{... | collective-permute-start | bytes 491528 | tf_op jit(solution)/shard_map/ppermute | solution.py:30
  59.1 9.0 %collective-permute-start.5 = (f32[2,80,256]{2,1,0:T(8,128)S(1)}, f32[2,80,256]{2,1,0:T(8,128)S(1)}, u32[]{:S(2)}, u32[]{:S(2)}) collective-permute-start(f32[2,80,256]{2,1,0:T(8,128)S(1)} %fusion.33), channel_id=1, source_target_pairs={{0,1},{1,0},{2,3},{3,2},{4,5},{5,4},{6,7},{7,6},{8,9},{9,8},{10,11... | collective-permute-start | bytes 491528 | tf_op jit(solution)/shard_map/ppermute | solution.py:30
  73.1 2.3 %copy-start.6 = (bf16[512,1024]{1,0:T(8,128)(2,1)}, bf16[512,1024]{1,0:T(8,128)(2,1)S(1)}, u32[]{:S(2)}) copy-start(bf16[512,1024]{1,0:T(8,128)(2,1)S(1)} %get-tuple-element.58) | copy-start | bytes 3145732
  75.4 5.0 %collective-permute-start.7 = (f32[2,256,1024]{2,1,0:T(8,128)}, f32[2,256,1024]{2,1,0:T(8,128)S(1)}, u32[]{:S(2)}, u32[]{:S(2)}) collective-permute-start(f32[2,256,1024]{2,1,0:T(8,128)} %bitcast.7), channel_id=1, source_target_pairs={{0,4},{4,0},{8,12},{12,8},{16,20},{20,16},{24,28},{28,24},{1,5},{5... | collective-permute-start | bytes 6291464 | tf_op jit(solution)/shard_map/ppermute | solution.py:30
  81.8 14.8 %collective-permute-start.8 = (f32[1,128,1024]{2,1,0:T(8,128)}, f32[1,128,1024]{2,1,0:T(8,128)S(1)}, u32[]{:S(2)}, u32[]{:S(2)}) collective-permute-start(f32[1,128,1024]{2,1,0:T(8,128)} %constant_dynamic-slice_fusion.4), channel_id=1, source_target_pairs={{0,8},{4,12},{8,0},{12,4},{16,24},{20,28},{24,16},{28,20},{1,9},{5... | collective-permute-start | bytes 1572872 | tf_op jit(solution)/shard_map/ppermute | solution.py:30
  84.7 14.1 %collective-permute-start.15 = (f32[1,128,1024]{2,1,0:T(8,128)}, f32[1,128,1024]{2,1,0:T(8,128)S(1)}, u32[]{:S(2)}, u32[]{:S(2)}) collective-permute-start(f32[1,128,1024]{2,1,0:T(8,128)} %constant_dynamic-slice_fusion.2), channel_id=1, source_target_pairs={{0,16},{4,20},{8,24},{12,28},{16,0},{20,4},{24,8},{28,12},{1,17},{... | collective-permute-start | bytes 1572872 | tf_op jit(solution)/shard_map/ppermute | solution.py:30
  85.3 10.3 %collective-permute-start.6 = (f32[2,80,256]{2,1,0:T(8,128)S(1)}, f32[2,80,256]{2,1,0:T(8,128)S(1)}, u32[]{:S(2)}, u32[]{:S(2)}) collective-permute-start(f32[2,80,256]{2,1,0:T(8,128)S(1)} %fusion.35), channel_id=1, source_target_pairs={{0,2},{1,3},{2,0},{3,1},{4,6},{5,7},{6,4},{7,5},{8,10},{9,11},{10,... | collective-permute-start | bytes 491528 | tf_op jit(solution)/shard_map/ppermute | solution.py:30
  96.6 6.0 %collective-permute-start.9 = (f32[2,80,256]{2,1,0:T(8,128)S(1)}, f32[2,80,256]{2,1,0:T(8,128)S(1)}, u32[]{:S(2)}, u32[]{:S(2)}) collective-permute-start(f32[2,80,256]{2,1,0:T(8,128)S(1)} %add.212), channel_id=1, source_target_pairs={{0,1},{1,0},{2,3},{3,2},{4,5},{5,4},{6,7},{7,6},{8,9},{9,8},{10,11... | collective-permute-start | bytes 491528 | tf_op jit(solution)/shard_map/ppermute | solution.py:30
  98.9 9.3 %collective-permute-start.16 = (f32[1,64,1024]{2,1,0:T(8,128)S(1)}, f32[1,64,1024]{2,1,0:T(8,128)S(1)}, u32[]{:S(2)}, u32[]{:S(2)}) collective-permute-start(f32[1,64,1024]{2,1,0:T(8,128)S(1)} %constant_dynamic-slice_fusion.1), channel_id=1, source_target_pairs={{0,8},{4,12},{8,0},{12,4},{16,24},{20,28},{24,16},{28,20},{1,9},{5... | collective-permute-start | bytes 786440 | tf_op jit(solution)/shard_map/ppermute | solution.py:30
  99.3 9.3 %collective-permute-start.14 = (f32[1,64,1024]{2,1,0:T(8,128)S(1)}, f32[1,64,1024]{2,1,0:T(8,128)S(1)}, u32[]{:S(2)}, u32[]{:S(2)}) collective-permute-start(f32[1,64,1024]{2,1,0:T(8,128)S(1)} %constant_dynamic-slice_fusion.3), channel_id=1, source_target_pairs={{0,16},{4,20},{8,24},{12,28},{16,0},{20,4},{24,8},{28,12},{1,17},{... | collective-permute-start | bytes 786440 | tf_op jit(solution)/shard_map/ppermute | solution.py:30
  102.6 7.7 %collective-permute-start.10 = (f32[1,160,256]{2,1,0:T(8,128)S(1)}, f32[1,160,256]{2,1,0:T(8,128)S(1)}, u32[]{:S(2)}, u32[]{:S(2)}) collective-permute-start(f32[1,160,256]{2,1,0:T(8,128)S(1)} %get-tuple-element.39), channel_id=1, source_target_pairs={{0,16},{4,20},{8,24},{12,28},{16,0},{20,4},{24,8},{28,12},{1,17},{... | collective-permute-start | bytes 491528 | tf_op jit(solution)/shard_map/ppermute | solution.py:30
  103.6 8.3 %collective-permute-start.12 = (f32[1,160,256]{2,1,0:T(8,128)S(1)}, f32[1,160,256]{2,1,0:T(8,128)S(1)}, u32[]{:S(2)}, u32[]{:S(2)}) collective-permute-start(f32[1,160,256]{2,1,0:T(8,128)S(1)} %get-tuple-element.40), channel_id=1, source_target_pairs={{0,8},{4,12},{8,0},{12,4},{16,24},{20,28},{24,16},{28,20},{1,9},{5... | collective-permute-start | bytes 491528 | tf_op jit(solution)/shard_map/ppermute | solution.py:30
  108.7 7.6 %collective-permute-start.17 = (f32[2,32,1024]{2,1,0:T(8,128)S(1)}, f32[2,32,1024]{2,1,0:T(8,128)S(1)}, u32[]{:S(2)}, u32[]{:S(2)}) collective-permute-start(f32[2,32,1024]{2,1,0:T(8,128)S(1)} %fusion.23), channel_id=1, source_target_pairs={{0,1},{1,0},{2,3},{3,2},{4,5},{5,4},{6,7},{7,6},{8,9},{9,8},{10,11... | collective-permute-start | bytes 786440 | tf_op jit(solution)/shard_map/ppermute | solution.py:30
  110.4 8.0 %collective-permute-start.11 = (f32[1,320,256]{2,1,0:T(8,128)S(1)}, f32[1,320,256]{2,1,0:T(8,128)S(1)}, u32[]{:S(2)}, u32[]{:S(2)}) collective-permute-start(f32[1,320,256]{2,1,0:T(8,128)S(1)} %pad_maximum_fusion.1), channel_id=1, source_target_pairs={{0,8},{4,12},{8,0},{12,4},{16,24},{20,28},{24,16},{28,20},{1,9},{5... | collective-permute-start | bytes 983048 | tf_op jit(solution)/shard_map/ppermute | solution.py:30
  112.0 7.4 %collective-permute-start.13 = (f32[1,320,256]{2,1,0:T(8,128)S(1)}, f32[1,320,256]{2,1,0:T(8,128)S(1)}, u32[]{:S(2)}, u32[]{:S(2)}) collective-permute-start(f32[1,320,256]{2,1,0:T(8,128)S(1)} %pad_maximum_fusion.2), channel_id=1, source_target_pairs={{0,16},{4,20},{8,24},{12,28},{16,0},{20,4},{24,8},{28,12},{1,17},{... | collective-permute-start | bytes 983048 | tf_op jit(solution)/shard_map/ppermute | solution.py:30
  116.4 7.3 %collective-permute-start.18 = (f32[2,16,1024]{2,1,0:T(8,128)S(1)}, f32[2,16,1024]{2,1,0:T(8,128)S(1)}, u32[]{:S(2)}, u32[]{:S(2)}) collective-permute-start(f32[2,16,1024]{2,1,0:T(8,128)S(1)} %constant_dynamic-slice_fusion), channel_id=1, source_target_pairs={{0,2},{1,3},{2,0},{3,1},{4,6},{5,7},{6,4},{7,5},{8,10},{9,11},{10,... | collective-permute-start | bytes 393224 | tf_op jit(solution)/shard_map/ppermute | solution.py:30
  123.7 3.1 %collective-permute-start.19 = (f32[2,640,256]{2,1,0:T(8,128)S(1)}, f32[2,640,256]{2,1,0:T(8,128)S(1)}, u32[]{:S(2)}, u32[]{:S(2)}) collective-permute-start(f32[2,640,256]{2,1,0:T(8,128)S(1)} %maximum_maximum_fusion.near_ref), channel_id=1, source_target_pairs={{0,4},{4,0},{8,12},{12,8},{16,20},{20,16},{24,28},{28,24},{1,5},{5... | collective-permute-start | bytes 3932168 | tf_op jit(solution)/shard_map/ppermute | solution.py:30
  136.7 5.1 %collective-permute-start.20 = (bf16[2,16,1024]{2,1,0:T(8,128)(2,1)S(1)}, bf16[2,16,1024]{2,1,0:T(8,128)(2,1)S(1)}, u32[]{:S(2)}, u32[]{:S(2)}) collective-permute-start(bf16[2,16,1024]{2,1,0:T(8,128)(2,1)S(1)} %bitcast.49), channel_id=1, source_target_pairs={{0,1},{1,0},{2,3},{3,2},{4,5},{5,4},{6,7},{7,6},{8,9},{9,8},{10,11... | collective-permute-start | bytes 196616 | tf_op jit(solution)/shard_map/ppermute | solution.py:52
  137.0 8.4 %collective-permute-start.21 = (bf16[2,16,1024]{2,1,0:T(8,128)(2,1)S(1)}, bf16[2,16,1024]{2,1,0:T(8,128)(2,1)S(1)}, u32[]{:S(2)}, u32[]{:S(2)}) collective-permute-start(bf16[2,16,1024]{2,1,0:T(8,128)(2,1)S(1)} %bitcast.50), channel_id=1, source_target_pairs={{0,2},{1,3},{2,0},{3,1},{4,6},{5,7},{6,4},{7,5},{8,10},{9,11},{10,... | collective-permute-start | bytes 196616 | tf_op jit(solution)/shard_map/ppermute | solution.py:52
  138.3 7.1 %collective-permute-start.22 = (bf16[2,16,1024]{2,1,0:T(8,128)(2,1)S(1)}, bf16[2,16,1024]{2,1,0:T(8,128)(2,1)S(1)}, u32[]{:S(2)}, u32[]{:S(2)}) collective-permute-start(bf16[2,16,1024]{2,1,0:T(8,128)(2,1)S(1)} %bitcast.51), channel_id=1, source_target_pairs={{0,3},{1,2},{2,1},{3,0},{4,7},{5,6},{6,5},{7,4},{8,11},{9,10},{10,... | collective-permute-start | bytes 196616 | tf_op jit(solution)/shard_map/ppermute | solution.py:52
  145.5 5.0 %collective-permute-start.23 = (bf16[1,64,1024]{2,1,0:T(8,128)(2,1)S(1)}, bf16[1,64,1024]{2,1,0:T(8,128)(2,1)S(1)}, u32[]{:S(2)}, u32[]{:S(2)}) collective-permute-start(bf16[1,64,1024]{2,1,0:T(8,128)(2,1)S(1)} %get-tuple-element.47), channel_id=1, source_target_pairs={{0,16},{4,20},{8,24},{12,28},{16,0},{20,4},{24,8},{28,12},{1,17},{... | collective-permute-start | bytes 393224 | tf_op jit(solution)/shard_map/ppermute | solution.py:30
  146.1 5.0 %collective-permute-start.25 = (bf16[1,64,1024]{2,1,0:T(8,128)(2,1)S(1)}, bf16[1,64,1024]{2,1,0:T(8,128)(2,1)S(1)}, u32[]{:S(2)}, u32[]{:S(2)}) collective-permute-start(bf16[1,64,1024]{2,1,0:T(8,128)(2,1)S(1)} %get-tuple-element.48), channel_id=1, source_target_pairs={{0,8},{4,12},{8,0},{12,4},{16,24},{20,28},{24,16},{28,20},{1,9},{5... | collective-permute-start | bytes 393224 | tf_op jit(solution)/shard_map/ppermute | solution.py:30
  151.1 6.7 %collective-permute-start.24 = (bf16[1,128,1024]{2,1,0:T(8,128)(2,1)S(1)}, bf16[1,128,1024]{2,1,0:T(8,128)(2,1)S(1)}, u32[]{:S(2)}, u32[]{:S(2)}) collective-permute-start(bf16[1,128,1024]{2,1,0:T(8,128)(2,1)S(1)} %pad_maximum_fusion.4), channel_id=1, source_target_pairs={{0,8},{4,12},{8,0},{12,4},{16,24},{20,28},{24,16},{28,20},{1,9},{5... | collective-permute-start | bytes 786440 | tf_op jit(solution)/shard_map/ppermute | solution.py:30
  153.5 6.4 %collective-permute-start.26 = (bf16[1,128,1024]{2,1,0:T(8,128)(2,1)S(1)}, bf16[1,128,1024]{2,1,0:T(8,128)(2,1)S(1)}, u32[]{:S(2)}, u32[]{:S(2)}) collective-permute-start(bf16[1,128,1024]{2,1,0:T(8,128)(2,1)S(1)} %pad_maximum_fusion.5), channel_id=1, source_target_pairs={{0,16},{4,20},{8,24},{12,28},{16,0},{20,4},{24,8},{28,12},{1,17},{... | collective-permute-start | bytes 786440 | tf_op jit(solution)/shard_map/ppermute | solution.py:30
  154.8 5.4 %copy-start = (bf16[2048,1024]{1,0:T(8,128)(2,1)S(1)}, bf16[2048,1024]{1,0:T(8,128)(2,1)}, u32[]{:S(2)}) copy-start(bf16[2048,1024]{1,0:T(8,128)(2,1)} %param.11) | copy-start | bytes 12582916
  160.1 3.9 %collective-permute-start.27 = (bf16[512,1024]{1,0:T(8,128)(2,1)S(1)}, bf16[512,1024]{1,0:T(8,128)(2,1)S(1)}, u32[]{:S(2)}, u32[]{:S(2)}) collective-permute-start(bf16[512,1024]{1,0:T(8,128)(2,1)S(1)} %bitcast.56), channel_id=1, source_target_pairs={{0,4},{4,0},{8,12},{12,8},{16,20},{20,16},{24,28},{28,24},{1,5},{5... | collective-permute-start | bytes 3145736 | tf_op jit(solution)/shard_map/ppermute | solution.py:30
  166.7 2.0 %copy-start.1 = (bf16[2048,1024]{1,0:T(8,128)(2,1)}, bf16[2048,1024]{1,0:T(8,128)(2,1)S(1)}, u32[]{:S(2)}) copy-start(bf16[2048,1024]{1,0:T(8,128)(2,1)S(1)} %fusion.2) | copy-start | bytes 12582916

commit v5 on v4

--- a/solution.py
+++ b/solution.py
@@ -9,9 +9,9 @@
 AXES = ("state", "obs")
 TILE = 256
 TOLERANCE = 5e-4
-MAX_STEPS = 4096
-REFRESH = 32
-FIRST_STEPS = 3
+STEPS = 512
+ROUNDS = 32
+FIRST_STEPS = 4
 HINT = 20000000000
 HOLD = 4
 
@@ -175,20 +175,38 @@
         if i < FIRST_STEPS - 1:
             p, rz = turn(r, p, rz)
 
+    def norm(r):
+        return jnp.sum(r * r, axis=1, keepdims=True)
+
+    def keep_better(x, r, new_x):
+        new_r = rhs - times(new_x)
+        better = norm(new_r) < norm(r)
+        progress = jnp.max(jnp.where(norm(new_r) < 0.5 * norm(r), 1, 0))
+        return jnp.where(better, new_x, x), jnp.where(better, new_r, r), progress
+
     r = rhs - times(x)
-    p, rz = turn(r, r, jnp.zeros((count, 1), jnp.float32))
 
     def more(carry):
-        return jnp.logical_and(carry[0] < MAX_STEPS, carry[1] > 0.0)
+        return jnp.logical_and(carry[0] < STEPS, carry[1] > 0.0)
 
     def advance(carry):
         step, _, x, r, p, rz = carry
         x, r = step_of(times, x, r, p, rz)
-        r = lax.cond(step % REFRESH == REFRESH - 1, lambda x, r: rhs - times(x), lambda x, r: r, x, r)
         p, rz = turn(r, p, rz)
         return step + 1, unsolved(x, r), x, r, p, rz
 
-    x = lax.while_loop(more, advance, (jnp.int32(0), unsolved(x, r), x, r, p, rz))[2]
+    def more_rounds(carry):
+        count, gap, progress = carry[:3]
+        return jnp.logical_and(jnp.logical_and(count < ROUNDS, gap > 0.0), progress > 0)
+
+    def another(carry):
+        count, gap, _, x, r = carry
+        p, rz = turn(r, r, jnp.zeros((rhs.shape[0], 1), jnp.float32))
+        new_x = lax.while_loop(more, advance, (jnp.int32(0), gap, x, r, p, rz))[2]
+        x, r, progress = keep_better(x, r, new_x)
+        return count + 1, unsolved(x, r), progress, x, r
+
+    x = lax.while_loop(more_rounds, another, (jnp.int32(0), unsolved(x, r), jnp.int32(1), x, r))[3]
     out_ref[...] = x.astype(jnp.bfloat16)
 
 

time: 169 us -> 170 us (level)
  no operation moved by 1% of the time
where the time goes in v5:
time: 170 us; the launch traced here: 169 us
  waiting for transfers between devices  78.6 us (46%)
  starting transfers between devices  42.1 us (25%)
  matrix products  19.6 us (12%)
  Pallas kernels  12.4 us (7%)
  other arithmetic  8.52 us (5%)
  local copies, waits for them, and re-layouts  7.13 us (4%)
    ppermute x25, waiting for transfers between devices, swap(): lax.ppermute(vals, axis, [(i, i ^ 1 << b) for i in range(lax.axis_size(ax...  69.9 us
    ppermute x25, starting transfers between devices, swap(): lax.ppermute(vals, axis, [(i, i ^ 1 << b) for i in range(lax.axis_size(ax...  26.8 us
    pallas_call x1, Pallas kernels, solve(): pl.pallas_call(solve_kernel, out_shape=jax.ShapeDtypeStruct(rhs.shape, jn...  10.6 us
    all_to_all x1, starting transfers between devices, on_device(): lax.all_to_all(jnp.broadcast_to(own, (shards, 2, rows)), AXES, split_axis...  7.3 us
    dot_general x2, matrix products, side_of(): lax.dot_general(spread, gain, (((1,), (1,)), ((), ())), preferred_element...  5.3 us
    ppermute x3, starting transfers between devices, gather(): lax.ppermute(vals, axis, pairs(flip))  4.45 us
    dot_general x2, matrix products, cross_part(): jnp.dot(cols.T, anomalies, preferred_element_type=f32)  4.34 us
    ppermute x3, waiting for transfers between devices, gather(): lax.ppermute(vals, axis, pairs(flip))  4.25 us
  transfers between devices with their start and end apart: 30, of which 25 were waited for; matrix products, arithmetic and copies ran while one was open for 12% of the time, Pallas kernels for 1%

profile of v5, /device:TPU:0, one launch (start us, length us, event | category | flops | bytes accessed | tf_op | source)
XLA Modules:
  0.0 169.5 jit_solution(6439292162951399109)
XLA Ops:
  2.8 7.3 %all-to-all-start = ((f32[32,2,512]{2,1,0:T(2,128)}), f32[32,2,512]{2,1,0:T(2,128)S(1)}, u32[]{:S(2)}, u32[]{:S(2)}) async-start(f32[32,2,512]{2,1,0:T(2,128)} %broadcast_in_dim.19), calls=%async_computation | async-start | bytes 262144 | tf_op jit(solution)/shard_map/all_to_all | solution.py:277
  10.3 1.4 convert_reduce_fusion.2
  11.7 3.8 %fusion.9 = bf16[1024,1024]{1,0:T(8,128)(2,1)} fusion(bf16[512,1024]{1,0:T(8,128)(2,1)} %param.6, s32[512]{0:T(512)S(1)} %convert_add_fusion), kind=kOutput, calls=%fused_computation.24 | convolution fusion | flops 1075314688 | bytes 3147776 | tf_op jit(solution)/shard_map/dot_general | solution.py:273
  15.5 2.9 %all-to-all-done = f32[32,2,512]{2,1,0:T(2,128)S(1)} async-done(((f32[32,2,512]{2,1,0:T(2,128)}), f32[32,2,512]{2,1,0:T(2,128)S(1)}, u32[]{:S(2)}, u32[]{:S(2)}) %all-to-all-start) | async-done | bytes 131104 | tf_op jit(solution)/shard_map/all_to_all | solution.py:277
  18.5 3.6 %all-to-all-start.1 = ((bf16[32,32,1024]{2,1,0:T(8,128)(2,1)}), bf16[32,32,1024]{2,1,0:T(8,128)(2,1)}, u32[]{:S(2)}, u32[]{:S(2)}) async-start(bf16[32,32,1024]{2,1,0:T(8,128)(2,1)} %bitcast.5), calls=%async_computation.1 | async-start | bytes 4194304 | tf_op jit(solution)/shard_map/all_to_all | solution.py:274
  24.9 1.2 constant_dynamic-slice_fusion.9
  27.7 1.9 %places.1 = bf16[512,1024]{1,0:T(8,128)(2,1)} custom-call(s32[1,1024]{1,0:T(1,128)} %sub.76.slot_ref), custom_call_target="tpu_custom_call" | custom-call | flops 20000000000 | bytes 1048576 | tf_op jit(solution)/shard_map/places/pallas_call | solution.py:242
  29.6 1.5 dynamic-slice_add_fusion
  31.2 1.8 %collective-permute-start.3 = (f32[1,320,256]{2,1,0:T(8,128)S(1)}, f32[1,320,256]{2,1,0:T(8,128)S(1)}, u32[]{:S(2)}, u32[]{:S(2)}) collective-permute-start(f32[1,320,256]{2,1,0:T(8,128)S(1)} %constant_dynamic-slice_fusion.6), channel_id=1, source_target_pairs={{0,16},{4,20},{8,24},{12,28},{16,0},{20,4},{24,8},{28,12},{1,17},{... | collective-permute-start | bytes 983048 | tf_op jit(solution)/shard_map/ppermute | solution.py:30
  33.0 1.5 collective-permute-start.1
  34.6 14.7 %collective-permute-done.3 = f32[1,320,256]{2,1,0:T(8,128)S(1)} collective-permute-done((f32[1,320,256]{2,1,0:T(8,128)S(1)}, f32[1,320,256]{2,1,0:T(8,128)S(1)}, u32[]{:S(2)}, u32[]{:S(2)}) %collective-permute-start.3) | collective-permute-done | bytes 327712 | tf_op jit(solution)/shard_map/ppermute | solution.py:30
  49.4 1.2 collective-permute-start.4
  50.7 1.8 %collective-permute-start.2 = (f32[1,160,256]{2,1,0:T(8,128)S(1)}, f32[1,160,256]{2,1,0:T(8,128)S(1)}, u32[]{:S(2)}, u32[]{:S(2)}) collective-permute-start(f32[1,160,256]{2,1,0:T(8,128)S(1)} %constant_dynamic-slice_fusion.7), channel_id=1, source_target_pairs={{0,16},{4,20},{8,24},{12,28},{16,0},{20,4},{24,8},{28,12},{1,17},{... | collective-permute-start | bytes 491528 | tf_op jit(solution)/shard_map/ppermute | solution.py:30
  52.5 4.2 %collective-permute-done.4 = f32[1,160,256]{2,1,0:T(8,128)S(1)} collective-permute-done((f32[1,160,256]{2,1,0:T(8,128)S(1)}, f32[1,160,256]{2,1,0:T(8,128)S(1)}, u32[]{:S(2)}, u32[]{:S(2)}) %collective-permute-start.4) | collective-permute-done | bytes 163872 | tf_op jit(solution)/shard_map/ppermute | solution.py:30
  56.7 2.3 %collective-permute-done.2 = f32[1,160,256]{2,1,0:T(8,128)S(1)} collective-permute-done((f32[1,160,256]{2,1,0:T(8,128)S(1)}, f32[1,160,256]{2,1,0:T(8,128)S(1)}, u32[]{:S(2)}, u32[]{:S(2)}) %collective-permute-start.2) | collective-permute-done | bytes 163872 | tf_op jit(solution)/shard_map/ppermute | solution.py:30
  59.1 1.3 collective-permute-start.5
  60.4 7.6 %collective-permute-done.5 = f32[2,80,256]{2,1,0:T(8,128)S(1)} collective-permute-done((f32[2,80,256]{2,1,0:T(8,128)S(1)}, f32[2,80,256]{2,1,0:T(8,128)S(1)}, u32[]{:S(2)}, u32[]{:S(2)}) %collective-permute-start.5) | collective-permute-done | bytes 163872 | tf_op jit(solution)/shard_map/ppermute | solution.py:30
  68.1 1.5 all-to-all-done.1
  69.6 3.5 %multiply_reduce_fusion = (f32[512]{0:T(512)S(1)}, f32[512]{0:T(512)S(1)}, bf16[512,1024]{1,0:T(8,128)(2,1)S(1)}, bf16[512,1024]{1,0:T(8,128)(2,1)S(1)}) fusion(bf16[512,1024]{1,0:T(8,128)(2,1)S(1)} %copy-done.4, f32[512]{0:T(512)S(1)} %copy-done.5, f32[512]{0:T(512)S(1)} %divide_sqrt_fusion, bf16[512,1024]{1,0:T(8,128)(2,1)} %places.1, ...), kind=kOutput, calls=%fused_computation.17 | convolution fusion | flops 1078983680 | bytes 6299648 | tf_op jit(solution)/shard_map/dot_general | solution.py:303
  73.1 2.2 %fusion.21 = f32[512,1024]{1,0:T(8,128)} fusion(bf16[512,1024]{1,0:T(8,128)(2,1)S(1)} %get-tuple-element.20, s32[]{:T(128)S(6)} %select_n.355, bf16[512,1024]{1,0:T(8,128)(2,1)S(1)} %get-tuple-element.58, f32[512]{0:T(512)S(1)} %broadcast_multiply_fusion.2, f32[512]{0:T(512)S(1)} %divide_sqrt_fusion), kind=kOutput, calls=%fused_computation.49 | convolution fusion | flops 538968064 | bytes 3674116 | tf_op jit(solution)/shard_map/dot_general | solution.py:318
  75.4 1.0 collective-permute-start.7
  76.4 2.1 %fusion.19 = f32[512,1024]{1,0:T(8,128)S(1)} fusion(bf16[512,1024]{1,0:T(8,128)(2,1)S(1)} %get-tuple-element.20, s32[]{:T(128)S(6)} %select_n.356, bf16[512,1024]{1,0:T(8,128)(2,1)} %copy-done.6, f32[512]{0:T(512)S(1)} %broadcast_multiply_fusion.2, f32[512]{0:T(512)S(1)} %divide_sqrt_fusion), kind=kOutput, calls=%fused_computation.47 | convolution fusion | flops 538968064 | bytes 3674116 | tf_op jit(solution)/shard_map/dot_general | solution.py:318
  78.5 1.9 %collective-permute-done.7 = f32[2,256,1024]{2,1,0:T(8,128)S(1)} collective-permute-done((f32[2,256,1024]{2,1,0:T(8,128)}, f32[2,256,1024]{2,1,0:T(8,128)S(1)}, u32[]{:S(2)}, u32[]{:S(2)}) %collective-permute-start.7) | collective-permute-done | bytes 2097184 | tf_op jit(solution)/shard_map/ppermute | solution.py:30
  81.8 2.1 %collective-permute-start.8 = (f32[1,128,1024]{2,1,0:T(8,128)}, f32[1,128,1024]{2,1,0:T(8,128)S(1)}, u32[]{:S(2)}, u32[]{:S(2)}) collective-permute-start(f32[1,128,1024]{2,1,0:T(8,128)} %constant_dynamic-slice_fusion.4), channel_id=1, source_target_pairs={{0,8},{4,12},{8,0},{12,4},{16,24},{20,28},{24,16},{28,20},{1,9},{5... | collective-permute-start | bytes 1572872 | tf_op jit(solution)/shard_map/ppermute | solution.py:30
  86.1 9.5 %collective-permute-done.6 = f32[2,80,256]{2,1,0:T(8,128)S(1)} collective-permute-done((f32[2,80,256]{2,1,0:T(8,128)S(1)}, f32[2,80,256]{2,1,0:T(8,128)S(1)}, u32[]{:S(2)}, u32[]{:S(2)}) %collective-permute-start.6) | collective-permute-done | bytes 163872 | tf_op jit(solution)/shard_map/ppermute | solution.py:30
  96.6 2.0 %collective-permute-start.9 = (f32[2,80,256]{2,1,0:T(8,128)S(1)}, f32[2,80,256]{2,1,0:T(8,128)S(1)}, u32[]{:S(2)}, u32[]{:S(2)}) collective-permute-start(f32[2,80,256]{2,1,0:T(8,128)S(1)} %add.212), channel_id=1, source_target_pairs={{0,1},{1,0},{2,3},{3,2},{4,5},{5,4},{6,7},{7,6},{8,9},{9,8},{10,11... | collective-permute-start | bytes 491528 | tf_op jit(solution)/shard_map/ppermute | solution.py:30
  99.3 1.3 collective-permute-start.14
  100.6 2.0 %collective-permute-done.9 = f32[2,80,256]{2,1,0:T(8,128)S(1)} collective-permute-done((f32[2,80,256]{2,1,0:T(8,128)S(1)}, f32[2,80,256]{2,1,0:T(8,128)S(1)}, u32[]{:S(2)}, u32[]{:S(2)}) %collective-permute-start.9) | collective-permute-done | bytes 163872 | tf_op jit(solution)/shard_map/ppermute | solution.py:30
  103.6 1.2 collective-permute-start.12
  104.8 3.4 %collective-permute-done.16 = f32[1,64,1024]{2,1,0:T(8,128)S(1)} collective-permute-done((f32[1,64,1024]{2,1,0:T(8,128)S(1)}, f32[1,64,1024]{2,1,0:T(8,128)S(1)}, u32[]{:S(2)}, u32[]{:S(2)}) %collective-permute-start.16) | collective-permute-done | bytes 262176 | tf_op jit(solution)/shard_map/ppermute | solution.py:30
  108.7 1.4 collective-permute-start.17
  110.4 1.5 collective-permute-start.11
  112.6 3.7 %collective-permute-done.17 = f32[2,32,1024]{2,1,0:T(8,128)S(1)} collective-permute-done((f32[2,32,1024]{2,1,0:T(8,128)S(1)}, f32[2,32,1024]{2,1,0:T(8,128)S(1)}, u32[]{:S(2)}, u32[]{:S(2)}) %collective-permute-start.17) | collective-permute-done | bytes 262176 | tf_op jit(solution)/shard_map/ppermute | solution.py:30
  116.5 1.9 %collective-permute-done.11 = f32[1,320,256]{2,1,0:T(8,128)S(1)} collective-permute-done((f32[1,320,256]{2,1,0:T(8,128)S(1)}, f32[1,320,256]{2,1,0:T(8,128)S(1)}, u32[]{:S(2)}, u32[]{:S(2)}) %collective-permute-start.11) | collective-permute-done | bytes 327712 | tf_op jit(solution)/shard_map/ppermute | solution.py:30
  119.5 4.2 %collective-permute-done.18 = f32[2,16,1024]{2,1,0:T(8,128)S(1)} collective-permute-done((f32[2,16,1024]{2,1,0:T(8,128)S(1)}, f32[2,16,1024]{2,1,0:T(8,128)S(1)}, u32[]{:S(2)}, u32[]{:S(2)}) %collective-permute-start.18) | collective-permute-done | bytes 131104 | tf_op jit(solution)/shard_map/ppermute | solution.py:30
  123.8 3.0 %collective-permute-done.19.far_ref = f32[2,640,256]{2,1,0:T(8,128)S(1)} collective-permute-done((f32[2,640,256]{2,1,0:T(8,128)S(1)}, f32[2,640,256]{2,1,0:T(8,128)S(1)}, u32[]{:S(2)}, u32[]{:S(2)}) %collective-permute-start.19) | collective-permute-done | bytes 1310752 | tf_op jit(solution)/shard_map/ppermute | solution.py:30
  126.8 10.6 %member_solve.1 = bf16[32,1024]{1,0:T(8,128)(2,1)S(1)} custom-call(s32[1]{0:T(128)} %bitcast.bit_ref, f32[2,640,256]{2,1,0:T(8,128)S(1)} %maximum_maximum_fusion.near_ref, f32[2,640,256]{2,1,0:T(8,128)S(1)} %collective-permute-done.19.far_ref, f32[32,1024]{1,0:T(8,128)S(1)} %bitcast.48), custom_call_target="tpu_custom_call" | custom-call | flops 1610612736 | bytes 6291456 | tf_op jit(solution)/shard_map/member_solve/pallas_call | solution.py:217
  137.7 1.3 collective-permute-start.21
  139.0 2.8 %collective-permute-start.22 = (bf16[2,16,1024]{2,1,0:T(8,128)(2,1)S(1)}, bf16[2,16,1024]{2,1,0:T(8,128)(2,1)S(1)}, u32[]{:S(2)}, u32[]{:S(2)}) collective-permute-start(bf16[2,16,1024]{2,1,0:T(8,128)(2,1)S(1)} %bitcast.51), channel_id=1, source_target_pairs={{0,3},{1,2},{2,1},{3,0},{4,7},{5,6},{6,5},{7,4},{8,11},{9,10},{10,... | collective-permute-start | bytes 196616 | tf_op jit(solution)/shard_map/ppermute | solution.py:52
  142.6 3.5 %collective-permute-done.21 = bf16[2,16,1024]{2,1,0:T(8,128)(2,1)S(1)} collective-permute-done((bf16[2,16,1024]{2,1,0:T(8,128)(2,1)S(1)}, bf16[2,16,1024]{2,1,0:T(8,128)(2,1)S(1)}, u32[]{:S(2)}, u32[]{:S(2)}) %collective-permute-start.21) | collective-permute-done | bytes 65568 | tf_op jit(solution)/shard_map/ppermute | solution.py:52
  146.8 1.5 collective-permute-start.25
  148.3 2.9 %collective-permute-done.23 = bf16[1,64,1024]{2,1,0:T(8,128)(2,1)S(1)} collective-permute-done((bf16[1,64,1024]{2,1,0:T(8,128)(2,1)S(1)}, bf16[1,64,1024]{2,1,0:T(8,128)(2,1)S(1)}, u32[]{:S(2)}, u32[]{:S(2)}) %collective-permute-start.23) | collective-permute-done | bytes 131104 | tf_op jit(solution)/shard_map/ppermute | solution.py:30
  152.1 2.1 %collective-permute-start.24 = (bf16[1,128,1024]{2,1,0:T(8,128)(2,1)S(1)}, bf16[1,128,1024]{2,1,0:T(8,128)(2,1)S(1)}, u32[]{:S(2)}, u32[]{:S(2)}) collective-permute-start(bf16[1,128,1024]{2,1,0:T(8,128)(2,1)S(1)} %pad_maximum_fusion.4), channel_id=1, source_target_pairs={{0,8},{4,12},{8,0},{12,4},{16,24},{20,28},{24,16},{28,20},{1,9},{5... | collective-permute-start | bytes 786440 | tf_op jit(solution)/shard_map/ppermute | solution.py:30
  155.5 3.1 %collective-permute-done.24 = bf16[1,128,1024]{2,1,0:T(8,128)(2,1)S(1)} collective-permute-done((bf16[1,128,1024]{2,1,0:T(8,128)(2,1)S(1)}, bf16[1,128,1024]{2,1,0:T(8,128)(2,1)S(1)}, u32[]{:S(2)}, u32[]{:S(2)}) %collective-permute-start.24) | collective-permute-done | bytes 262176 | tf_op jit(solution)/shard_map/ppermute | solution.py:30
  158.7 2.0 %collective-permute-done.26 = bf16[1,128,1024]{2,1,0:T(8,128)(2,1)S(1)} collective-permute-done((bf16[1,128,1024]{2,1,0:T(8,128)(2,1)S(1)}, bf16[1,128,1024]{2,1,0:T(8,128)(2,1)S(1)}, u32[]{:S(2)}, u32[]{:S(2)}) %collective-permute-start.26) | collective-permute-done | bytes 262176 | tf_op jit(solution)/shard_map/ppermute | solution.py:30
  162.1 2.6 %fusion.1 = bf16[2048,1024]{1,0:T(8,128)(2,1)S(1)} fusion(bf16[2048,1024]{1,0:T(8,128)(2,1)S(1)} %broadcast_in_dim.18, s32[]{:T(128)S(6)} %select_n.356, bf16[512,1024]{1,0:T(8,128)(2,1)S(1)} %bitcast.57, bf16[2048,1024]{1,0:T(8,128)(2,1)S(1)} %copy-done, f32[2048]{0:T(1024)S(1)} %broadcast_multiply_fusion), kind=kOutput, calls=%fused_computation.8 | convolution fusion | flops 2156920832 | bytes 9445380 | tf_op jit(solution)/shard_map/dot_general | solution.py:346
  164.8 2.7 %fusion.2 = bf16[2048,1024]{1,0:T(8,128)(2,1)S(1)} fusion(bf16[2048,1024]{1,0:T(8,128)(2,1)S(1)} %fusion.1, s32[]{:T(128)S(6)} %select_n.355, bf16[512,1024]{1,0:T(8,128)(2,1)S(1)} %collective-permute-done.27, bf16[2048,1024]{1,0:T(8,128)(2,1)S(1)} %copy-done, f32[2048]{0:T(1024)S(1)} %broadcast_multiply_fusion), kind=kOutput, calls=%fused_computation.9 | convolution fusion | flops 2156920832 | bytes 9445380 | tf_op jit(solution)/shard_map/dot_general | solution.py:346
  167.5 2.0 %copy-done.1 = bf16[2048,1024]{1,0:T(8,128)(2,1)} copy-done((bf16[2048,1024]{1,0:T(8,128)(2,1)}, bf16[2048,1024]{1,0:T(8,128)(2,1)S(1)}, u32[]{:S(2)}) %copy-start.1) | copy-done | bytes 4194328
  (107 shorter events, 21.7 us)
Async XLA Ops:
  2.8 15.7 %all-to-all-start = ((f32[32,2,512]{2,1,0:T(2,128)}), f32[32,2,512]{2,1,0:T(2,128)S(1)}, u32[]{:S(2)}, u32[]{:S(2)}) async-start(f32[32,2,512]{2,1,0:T(2,128)} %broadcast_in_dim.19), calls=%async_computation | async-start | bytes 262144 | tf_op jit(solution)/shard_map/all_to_all | solution.py:277
  18.5 4.4 %copy-start.2 = (bf16[512,1024]{1,0:T(8,128)(2,1)S(1)}, bf16[512,1024]{1,0:T(8,128)(2,1)}, u32[]{:S(2)}) copy-start(bf16[512,1024]{1,0:T(8,128)(2,1)} %param.6) | copy-start | bytes 3145732
  18.5 51.1 %all-to-all-start.1 = ((bf16[32,32,1024]{2,1,0:T(8,128)(2,1)}), bf16[32,32,1024]{2,1,0:T(8,128)(2,1)}, u32[]{:S(2)}, u32[]{:S(2)}) async-start(bf16[32,32,1024]{2,1,0:T(8,128)(2,1)} %bitcast.5), calls=%async_computation.1 | async-start | bytes 4194304 | tf_op jit(solution)/shard_map/all_to_all | solution.py:274
  26.1 3.5 %collective-permute-start = (f32[2,640,256]{2,1,0:T(8,128)}, f32[2,640,256]{2,1,0:T(8,128)}, u32[]{:S(2)}, u32[]{:S(2)}) collective-permute-start(f32[2,640,256]{2,1,0:T(8,128)} %constant_dynamic-slice_fusion.9), channel_id=1, source_target_pairs={{0,4},{4,0},{8,12},{12,8},{16,20},{20,16},{24,28},{28,24},{1,5},{5... | collective-permute-start | bytes 3932168 | tf_op jit(solution)/shard_map/ppermute | solution.py:30
  31.2 18.1 %collective-permute-start.3 = (f32[1,320,256]{2,1,0:T(8,128)S(1)}, f32[1,320,256]{2,1,0:T(8,128)S(1)}, u32[]{:S(2)}, u32[]{:S(2)}) collective-permute-start(f32[1,320,256]{2,1,0:T(8,128)S(1)} %constant_dynamic-slice_fusion.6), channel_id=1, source_target_pairs={{0,16},{4,20},{8,24},{12,28},{16,0},{20,4},{24,8},{28,12},{1,17},{... | collective-permute-start | bytes 983048 | tf_op jit(solution)/shard_map/ppermute | solution.py:30
  33.0 27.4 %copy-start.3 = (f32[512]{0:T(512)S(1)}, f32[512]{0:T(512)}, u32[]{:S(2)}) copy-start(f32[512]{0:T(512)} %param.9) | copy-start | bytes 6148
  33.0 17.6 %collective-permute-start.1 = (f32[1,320,256]{2,1,0:T(8,128)S(1)}, f32[1,320,256]{2,1,0:T(8,128)S(1)}, u32[]{:S(2)}, u32[]{:S(2)}) collective-permute-start(f32[1,320,256]{2,1,0:T(8,128)S(1)} %constant_dynamic-slice_fusion.8), channel_id=1, source_target_pairs={{0,8},{4,12},{8,0},{12,4},{16,24},{20,28},{24,16},{28,20},{1,9},{5... | collective-permute-start | bytes 983048 | tf_op jit(solution)/shard_map/ppermute | solution.py:30
  49.3 20.2 %copy-start.4 = (bf16[512,1024]{1,0:T(8,128)(2,1)S(1)}, bf16[512,1024]{1,0:T(8,128)(2,1)}, u32[]{:S(2)}) copy-start(bf16[512,1024]{1,0:T(8,128)(2,1)} %param.10) | copy-start | bytes 3145732
  49.3 20.2 %copy-start.5 = (f32[512]{0:T(512)S(1)}, f32[512]{0:T(512)}, u32[]{:S(2)}) copy-start(f32[512]{0:T(512)} %param.8) | copy-start | bytes 6148
  49.4 7.3 %collective-permute-start.4 = (f32[1,160,256]{2,1,0:T(8,128)S(1)}, f32[1,160,256]{2,1,0:T(8,128)S(1)}, u32[]{:S(2)}, u32[]{:S(2)}) collective-permute-start(f32[1,160,256]{2,1,0:T(8,128)S(1)} %constant_dynamic-slice_fusion.5), channel_id=1, source_target_pairs={{0,8},{4,12},{8,0},{12,4},{16,24},{20,28},{24,16},{28,20},{1,9},{5... | collective-permute-start | bytes 491528 | tf_op jit(solution)/shard_map/ppermute | solution.py:30
  50.7 8.3 %collective-permute-start.2 = (f32[1,160,256]{2,1,0:T(8,128)S(1)}, f32[1,160,256]{2,1,0:T(8,128)S(1)}, u32[]{:S(2)}, u32[]{:S(2)}) collective-permute-start(f32[1,160,256]{2,1,0:T(8,128)S(1)} %constant_dynamic-slice_fusion.7), channel_id=1, source_target_pairs={{0,16},{4,20},{8,24},{12,28},{16,0},{20,4},{24,8},{28,12},{1,17},{... | collective-permute-start | bytes 491528 | tf_op jit(solution)/shard_map/ppermute | solution.py:30
  59.1 9.0 %collective-permute-start.5 = (f32[2,80,256]{2,1,0:T(8,128)S(1)}, f32[2,80,256]{2,1,0:T(8,128)S(1)}, u32[]{:S(2)}, u32[]{:S(2)}) collective-permute-start(f32[2,80,256]{2,1,0:T(8,128)S(1)} %fusion.33), channel_id=1, source_target_pairs={{0,1},{1,0},{2,3},{3,2},{4,5},{5,4},{6,7},{7,6},{8,9},{9,8},{10,11... | collective-permute-start | bytes 491528 | tf_op jit(solution)/shard_map/ppermute | solution.py:30
  73.1 2.3 %copy-start.6 = (bf16[512,1024]{1,0:T(8,128)(2,1)}, bf16[512,1024]{1,0:T(8,128)(2,1)S(1)}, u32[]{:S(2)}) copy-start(bf16[512,1024]{1,0:T(8,128)(2,1)S(1)} %get-tuple-element.58) | copy-start | bytes 3145732
  75.4 5.0 %collective-permute-start.7 = (f32[2,256,1024]{2,1,0:T(8,128)}, f32[2,256,1024]{2,1,0:T(8,128)S(1)}, u32[]{:S(2)}, u32[]{:S(2)}) collective-permute-start(f32[2,256,1024]{2,1,0:T(8,128)} %bitcast.7), channel_id=1, source_target_pairs={{0,4},{4,0},{8,12},{12,8},{16,20},{20,16},{24,28},{28,24},{1,5},{5... | collective-permute-start | bytes 6291464 | tf_op jit(solution)/shard_map/ppermute | solution.py:30
  81.8 14.8 %collective-permute-start.8 = (f32[1,128,1024]{2,1,0:T(8,128)}, f32[1,128,1024]{2,1,0:T(8,128)S(1)}, u32[]{:S(2)}, u32[]{:S(2)}) collective-permute-start(f32[1,128,1024]{2,1,0:T(8,128)} %constant_dynamic-slice_fusion.4), channel_id=1, source_target_pairs={{0,8},{4,12},{8,0},{12,4},{16,24},{20,28},{24,16},{28,20},{1,9},{5... | collective-permute-start | bytes 1572872 | tf_op jit(solution)/shard_map/ppermute | solution.py:30
  84.7 14.1 %collective-permute-start.15 = (f32[1,128,1024]{2,1,0:T(8,128)}, f32[1,128,1024]{2,1,0:T(8,128)S(1)}, u32[]{:S(2)}, u32[]{:S(2)}) collective-permute-start(f32[1,128,1024]{2,1,0:T(8,128)} %constant_dynamic-slice_fusion.2), channel_id=1, source_target_pairs={{0,16},{4,20},{8,24},{12,28},{16,0},{20,4},{24,8},{28,12},{1,17},{... | collective-permute-start | bytes 1572872 | tf_op jit(solution)/shard_map/ppermute | solution.py:30
  85.3 10.3 %collective-permute-start.6 = (f32[2,80,256]{2,1,0:T(8,128)S(1)}, f32[2,80,256]{2,1,0:T(8,128)S(1)}, u32[]{:S(2)}, u32[]{:S(2)}) collective-permute-start(f32[2,80,256]{2,1,0:T(8,128)S(1)} %fusion.35), channel_id=1, source_target_pairs={{0,2},{1,3},{2,0},{3,1},{4,6},{5,7},{6,4},{7,5},{8,10},{9,11},{10,... | collective-permute-start | bytes 491528 | tf_op jit(solution)/shard_map/ppermute | solution.py:30
  96.6 6.0 %collective-permute-start.9 = (f32[2,80,256]{2,1,0:T(8,128)S(1)}, f32[2,80,256]{2,1,0:T(8,128)S(1)}, u32[]{:S(2)}, u32[]{:S(2)}) collective-permute-start(f32[2,80,256]{2,1,0:T(8,128)S(1)} %add.212), channel_id=1, source_target_pairs={{0,1},{1,0},{2,3},{3,2},{4,5},{5,4},{6,7},{7,6},{8,9},{9,8},{10,11... | collective-permute-start | bytes 491528 | tf_op jit(solution)/shard_map/ppermute | solution.py:30
  98.9 9.3 %collective-permute-start.16 = (f32[1,64,1024]{2,1,0:T(8,128)S(1)}, f32[1,64,1024]{2,1,0:T(8,128)S(1)}, u32[]{:S(2)}, u32[]{:S(2)}) collective-permute-start(f32[1,64,1024]{2,1,0:T(8,128)S(1)} %constant_dynamic-slice_fusion.1), channel_id=1, source_target_pairs={{0,8},{4,12},{8,0},{12,4},{16,24},{20,28},{24,16},{28,20},{1,9},{5... | collective-permute-start | bytes 786440 | tf_op jit(solution)/shard_map/ppermute | solution.py:30
  99.3 9.3 %collective-permute-start.14 = (f32[1,64,1024]{2,1,0:T(8,128)S(1)}, f32[1,64,1024]{2,1,0:T(8,128)S(1)}, u32[]{:S(2)}, u32[]{:S(2)}) collective-permute-start(f32[1,64,1024]{2,1,0:T(8,128)S(1)} %constant_dynamic-slice_fusion.3), channel_id=1, source_target_pairs={{0,16},{4,20},{8,24},{12,28},{16,0},{20,4},{24,8},{28,12},{1,17},{... | collective-permute-start | bytes 786440 | tf_op jit(solution)/shard_map/ppermute | solution.py:30
  102.6 7.7 %collective-permute-start.10 = (f32[1,160,256]{2,1,0:T(8,128)S(1)}, f32[1,160,256]{2,1,0:T(8,128)S(1)}, u32[]{:S(2)}, u32[]{:S(2)}) collective-permute-start(f32[1,160,256]{2,1,0:T(8,128)S(1)} %get-tuple-element.39), channel_id=1, source_target_pairs={{0,16},{4,20},{8,24},{12,28},{16,0},{20,4},{24,8},{28,12},{1,17},{... | collective-permute-start | bytes 491528 | tf_op jit(solution)/shard_map/ppermute | solution.py:30
  103.6 8.3 %collective-permute-start.12 = (f32[1,160,256]{2,1,0:T(8,128)S(1)}, f32[1,160,256]{2,1,0:T(8,128)S(1)}, u32[]{:S(2)}, u32[]{:S(2)}) collective-permute-start(f32[1,160,256]{2,1,0:T(8,128)S(1)} %get-tuple-element.40), channel_id=1, source_target_pairs={{0,8},{4,12},{8,0},{12,4},{16,24},{20,28},{24,16},{28,20},{1,9},{5... | collective-permute-start | bytes 491528 | tf_op jit(solution)/shard_map/ppermute | solution.py:30
  108.7 7.6 %collective-permute-start.17 = (f32[2,32,1024]{2,1,0:T(8,128)S(1)}, f32[2,32,1024]{2,1,0:T(8,128)S(1)}, u32[]{:S(2)}, u32[]{:S(2)}) collective-permute-start(f32[2,32,1024]{2,1,0:T(8,128)S(1)} %fusion.23), channel_id=1, source_target_pairs={{0,1},{1,0},{2,3},{3,2},{4,5},{5,4},{6,7},{7,6},{8,9},{9,8},{10,11... | collective-permute-start | bytes 786440 | tf_op jit(solution)/shard_map/ppermute | solution.py:30
  110.4 8.0 %collective-permute-start.11 = (f32[1,320,256]{2,1,0:T(8,128)S(1)}, f32[1,320,256]{2,1,0:T(8,128)S(1)}, u32[]{:S(2)}, u32[]{:S(2)}) collective-permute-start(f32[1,320,256]{2,1,0:T(8,128)S(1)} %pad_maximum_fusion.1), channel_id=1, source_target_pairs={{0,8},{4,12},{8,0},{12,4},{16,24},{20,28},{24,16},{28,20},{1,9},{5... | collective-permute-start | bytes 983048 | tf_op jit(solution)/shard_map/ppermute | solution.py:30
  112.0 7.4 %collective-permute-start.13 = (f32[1,320,256]{2,1,0:T(8,128)S(1)}, f32[1,320,256]{2,1,0:T(8,128)S(1)}, u32[]{:S(2)}, u32[]{:S(2)}) collective-permute-start(f32[1,320,256]{2,1,0:T(8,128)S(1)} %pad_maximum_fusion.2), channel_id=1, source_target_pairs={{0,16},{4,20},{8,24},{12,28},{16,0},{20,4},{24,8},{28,12},{1,17},{... | collective-permute-start | bytes 983048 | tf_op jit(solution)/shard_map/ppermute | solution.py:30
  116.4 7.3 %collective-permute-start.18 = (f32[2,16,1024]{2,1,0:T(8,128)S(1)}, f32[2,16,1024]{2,1,0:T(8,128)S(1)}, u32[]{:S(2)}, u32[]{:S(2)}) collective-permute-start(f32[2,16,1024]{2,1,0:T(8,128)S(1)} %constant_dynamic-slice_fusion), channel_id=1, source_target_pairs={{0,2},{1,3},{2,0},{3,1},{4,6},{5,7},{6,4},{7,5},{8,10},{9,11},{10,... | collective-permute-start | bytes 393224 | tf_op jit(solution)/shard_map/ppermute | solution.py:30
  123.7 3.1 %collective-permute-start.19 = (f32[2,640,256]{2,1,0:T(8,128)S(1)}, f32[2,640,256]{2,1,0:T(8,128)S(1)}, u32[]{:S(2)}, u32[]{:S(2)}) collective-permute-start(f32[2,640,256]{2,1,0:T(8,128)S(1)} %maximum_maximum_fusion.near_ref), channel_id=1, source_target_pairs={{0,4},{4,0},{8,12},{12,8},{16,20},{20,16},{24,28},{28,24},{1,5},{5... | collective-permute-start | bytes 3932168 | tf_op jit(solution)/shard_map/ppermute | solution.py:30
  137.4 5.2 %collective-permute-start.20 = (bf16[2,16,1024]{2,1,0:T(8,128)(2,1)S(1)}, bf16[2,16,1024]{2,1,0:T(8,128)(2,1)S(1)}, u32[]{:S(2)}, u32[]{:S(2)}) collective-permute-start(bf16[2,16,1024]{2,1,0:T(8,128)(2,1)S(1)} %bitcast.49), channel_id=1, source_target_pairs={{0,1},{1,0},{2,3},{3,2},{4,5},{5,4},{6,7},{7,6},{8,9},{9,8},{10,11... | collective-permute-start | bytes 196616 | tf_op jit(solution)/shard_map/ppermute | solution.py:52
  137.7 8.4 %collective-permute-start.21 = (bf16[2,16,1024]{2,1,0:T(8,128)(2,1)S(1)}, bf16[2,16,1024]{2,1,0:T(8,128)(2,1)S(1)}, u32[]{:S(2)}, u32[]{:S(2)}) collective-permute-start(bf16[2,16,1024]{2,1,0:T(8,128)(2,1)S(1)} %bitcast.50), channel_id=1, source_target_pairs={{0,2},{1,3},{2,0},{3,1},{4,6},{5,7},{6,4},{7,5},{8,10},{9,11},{10,... | collective-permute-start | bytes 196616 | tf_op jit(solution)/shard_map/ppermute | solution.py:52
  139.0 7.1 %collective-permute-start.22 = (bf16[2,16,1024]{2,1,0:T(8,128)(2,1)S(1)}, bf16[2,16,1024]{2,1,0:T(8,128)(2,1)S(1)}, u32[]{:S(2)}, u32[]{:S(2)}) collective-permute-start(bf16[2,16,1024]{2,1,0:T(8,128)(2,1)S(1)} %bitcast.51), channel_id=1, source_target_pairs={{0,3},{1,2},{2,1},{3,0},{4,7},{5,6},{6,5},{7,4},{8,11},{9,10},{10,... | collective-permute-start | bytes 196616 | tf_op jit(solution)/shard_map/ppermute | solution.py:52
  146.2 5.0 %collective-permute-start.23 = (bf16[1,64,1024]{2,1,0:T(8,128)(2,1)S(1)}, bf16[1,64,1024]{2,1,0:T(8,128)(2,1)S(1)}, u32[]{:S(2)}, u32[]{:S(2)}) collective-permute-start(bf16[1,64,1024]{2,1,0:T(8,128)(2,1)S(1)} %get-tuple-element.47), channel_id=1, source_target_pairs={{0,16},{4,20},{8,24},{12,28},{16,0},{20,4},{24,8},{28,12},{1,17},{... | collective-permute-start | bytes 393224 | tf_op jit(solution)/shard_map/ppermute | solution.py:30
  146.8 5.2 %collective-permute-start.25 = (bf16[1,64,1024]{2,1,0:T(8,128)(2,1)S(1)}, bf16[1,64,1024]{2,1,0:T(8,128)(2,1)S(1)}, u32[]{:S(2)}, u32[]{:S(2)}) collective-permute-start(bf16[1,64,1024]{2,1,0:T(8,128)(2,1)S(1)} %get-tuple-element.48), channel_id=1, source_target_pairs={{0,8},{4,12},{8,0},{12,4},{16,24},{20,28},{24,16},{28,20},{1,9},{5... | collective-permute-start | bytes 393224 | tf_op jit(solution)/shard_map/ppermute | solution.py:30
  152.1 6.5 %collective-permute-start.24 = (bf16[1,128,1024]{2,1,0:T(8,128)(2,1)S(1)}, bf16[1,128,1024]{2,1,0:T(8,128)(2,1)S(1)}, u32[]{:S(2)}, u32[]{:S(2)}) collective-permute-start(bf16[1,128,1024]{2,1,0:T(8,128)(2,1)S(1)} %pad_maximum_fusion.4), channel_id=1, source_target_pairs={{0,8},{4,12},{8,0},{12,4},{16,24},{20,28},{24,16},{28,20},{1,9},{5... | collective-permute-start | bytes 786440 | tf_op jit(solution)/shard_map/ppermute | solution.py:30
  154.3 6.4 %collective-permute-start.26 = (bf16[1,128,1024]{2,1,0:T(8,128)(2,1)S(1)}, bf16[1,128,1024]{2,1,0:T(8,128)(2,1)S(1)}, u32[]{:S(2)}, u32[]{:S(2)}) collective-permute-start(bf16[1,128,1024]{2,1,0:T(8,128)(2,1)S(1)} %pad_maximum_fusion.5), channel_id=1, source_target_pairs={{0,16},{4,20},{8,24},{12,28},{16,0},{20,4},{24,8},{28,12},{1,17},{... | collective-permute-start | bytes 786440 | tf_op jit(solution)/shard_map/ppermute | solution.py:30
  155.5 5.5 %copy-start = (bf16[2048,1024]{1,0:T(8,128)(2,1)S(1)}, bf16[2048,1024]{1,0:T(8,128)(2,1)}, u32[]{:S(2)}) copy-start(bf16[2048,1024]{1,0:T(8,128)(2,1)} %param.11) | copy-start | bytes 12582916
  160.9 3.9 %collective-permute-start.27 = (bf16[512,1024]{1,0:T(8,128)(2,1)S(1)}, bf16[512,1024]{1,0:T(8,128)(2,1)S(1)}, u32[]{:S(2)}, u32[]{:S(2)}) collective-permute-start(bf16[512,1024]{1,0:T(8,128)(2,1)S(1)} %bitcast.56), channel_id=1, source_target_pairs={{0,4},{4,0},{8,12},{12,8},{16,20},{20,16},{24,28},{28,24},{1,5},{5... | collective-permute-start | bytes 3145736 | tf_op jit(solution)/shard_map/ppermute | solution.py:30
  167.5 2.0 %copy-start.1 = (bf16[2048,1024]{1,0:T(8,128)(2,1)}, bf16[2048,1024]{1,0:T(8,128)(2,1)S(1)}, u32[]{:S(2)}) copy-start(bf16[2048,1024]{1,0:T(8,128)(2,1)S(1)} %fusion.2) | copy-start | bytes 12582916

commit v6 on v5

--- a/solution.py
+++ b/solution.py
@@ -38,6 +38,12 @@
 def halve(vals, dim):
     keep, send = halves(vals, my_bit(dim))
     return keep + swap(send, dim)
+
+
+def halve_sum(one, other, dim):
+    bit = my_bit(dim)
+    (keep, send), (keep_other, send_other) = halves(one, bit), halves(other, bit)
+    return keep + keep_other + swap(send + send_other, dim)
 
 
 def double(vals, dim):
@@ -320,10 +326,15 @@
 
     later = iter(ahead_steps[HOLD:])
     gram, send = lax.optimization_barrier((gram, cross_part(1 - bit)))
-    cross = (cross_part(bit) + swap(send, head),)
+    kept, came = cross_part(bit), swap(send, head)
+    cross = None
     gram = next(later)(gram)
     for i, step in enumerate(steps_of(halve)[1:]):
-        cross = step(cross)
+        if i == 0:
+            dims = next(zip(*stages()[1], strict=True))
+            cross = tuple(halve_sum(kept[n : n + 1], came[n : n + 1], dim) for n, dim in enumerate(dims))
+        else:
+            cross = step(cross)
         if i == 0:
             gram = after(gram, cross[0])
         gram = next(later, lambda parts: parts)(gram)

time: 170 us -> 175 us (1.029)
  other arithmetic: 8.52 us -> 12.2 us
  local copies, waits for them, and re-layouts: 7.13 us -> 9.09 us
    add x1 -> x4, other arithmetic: 0.39 us -> 4.18 us  [halve_sum(): return keep + keep_other + swap(send + send_other, dim)]
    unnamed x14 -> x16, local copies, waits for them, and re-layouts: 2.04 us -> 3.98 us
    slice x0 -> x2, local copies, waits for them, and re-layouts: none -> 1.82 us  [the longest x1 1.68 us: on_device(): came[n:n + 1]]
  transfers between devices with their start and end apart: 30 -> 30, of which waited for: 25 -> 23; matrix products, arithmetic and copies ran while one was open for 12% -> 13% of each run, Pallas kernels for 1% -> 1%
where the time goes in v6:
time: 175 us
  waiting for transfers between devices  78.3 us (45%)
  starting transfers between devices  42 us (24%)
  matrix products  19.6 us (11%)
  Pallas kernels  12.4 us (7%)
  other arithmetic  12.2 us (7%)
  local copies, waits for them, and re-layouts  9.09 us (5%)
    ppermute x25, waiting for transfers between devices, swap(): lax.ppermute(vals, axis, [(i, i ^ 1 << b) for i in range(lax.axis_size(ax...  69.6 us
    ppermute x25, starting transfers between devices, swap(): lax.ppermute(vals, axis, [(i, i ^ 1 << b) for i in range(lax.axis_size(ax...  26.6 us
    pallas_call x1, Pallas kernels, solve(): pl.pallas_call(solve_kernel, out_shape=jax.ShapeDtypeStruct(rhs.shape, jn...  10.6 us
    all_to_all x1, starting transfers between devices, on_device(): lax.all_to_all(jnp.broadcast_to(own, (shards, 2, rows)), AXES, split_axis...  7.3 us
    dot_general x2, matrix products, side_of(): lax.dot_general(spread, gain, (((1,), (1,)), ((), ())), preferred_element...  5.32 us
    ppermute x3, starting transfers between devices, gather(): lax.ppermute(vals, axis, pairs(flip))  4.45 us
    dot_general x2, matrix products, cross_part(): jnp.dot(cols.T, anomalies, preferred_element_type=f32)  4.37 us
    ppermute x3, waiting for transfers between devices, gather(): lax.ppermute(vals, axis, pairs(flip))  4.3 us
  transfers between devices with their start and end apart: 30, of which 23 were waited for; matrix products, arithmetic and copies ran while one was open for 13% of the time, Pallas kernels for 1%

profile of v6, /device:TPU:0, one launch (start us, length us, event | category | flops | bytes accessed | tf_op | source)
XLA Modules:
  0.0 174.8 jit_solution(15352329938971600831)
XLA Ops:
  2.8 7.3 %all-to-all-start = ((f32[32,2,512]{2,1,0:T(2,128)}), f32[32,2,512]{2,1,0:T(2,128)S(1)}, u32[]{:S(2)}, u32[]{:S(2)}) async-start(f32[32,2,512]{2,1,0:T(2,128)} %broadcast_in_dim.19), calls=%async_computation | async-start | bytes 262144 | tf_op jit(solution)/shard_map/all_to_all | solution.py:283
  10.3 1.4 convert_reduce_fusion.2
  11.8 3.8 %fusion.9 = bf16[1024,1024]{1,0:T(8,128)(2,1)} fusion(bf16[512,1024]{1,0:T(8,128)(2,1)} %param.6, s32[512]{0:T(512)S(1)} %convert_add_fusion), kind=kOutput, calls=%fused_computation.24 | convolution fusion | flops 1075314688 | bytes 3147776 | tf_op jit(solution)/shard_map/dot_general | solution.py:279
  15.5 2.9 %all-to-all-done = f32[32,2,512]{2,1,0:T(2,128)S(1)} async-done(((f32[32,2,512]{2,1,0:T(2,128)}), f32[32,2,512]{2,1,0:T(2,128)S(1)}, u32[]{:S(2)}, u32[]{:S(2)}) %all-to-all-start) | async-done | bytes 131104 | tf_op jit(solution)/shard_map/all_to_all | solution.py:283
  18.5 3.6 %all-to-all-start.1 = ((bf16[32,32,1024]{2,1,0:T(8,128)(2,1)}), bf16[32,32,1024]{2,1,0:T(8,128)(2,1)}, u32[]{:S(2)}, u32[]{:S(2)}) async-start(bf16[32,32,1024]{2,1,0:T(8,128)(2,1)} %bitcast.5), calls=%async_computation.1 | async-start | bytes 4194304 | tf_op jit(solution)/shard_map/all_to_all | solution.py:280
  24.9 1.1 constant_dynamic-slice_fusion.7
  27.7 1.9 %places.1 = bf16[512,1024]{1,0:T(8,128)(2,1)} custom-call(s32[1,1024]{1,0:T(1,128)} %sub.78.slot_ref), custom_call_target="tpu_custom_call" | custom-call | flops 20000000000 | bytes 1048576 | tf_op jit(solution)/shard_map/places/pallas_call | solution.py:248
  29.6 1.5 dynamic-slice_add_fusion
  31.2 1.8 %collective-permute-start.3 = (f32[1,320,256]{2,1,0:T(8,128)S(1)}, f32[1,320,256]{2,1,0:T(8,128)S(1)}, u32[]{:S(2)}, u32[]{:S(2)}) collective-permute-start(f32[1,320,256]{2,1,0:T(8,128)S(1)} %constant_dynamic-slice_fusion.4), channel_id=1, source_target_pairs={{0,16},{4,20},{8,24},{12,28},{16,0},{20,4},{24,8},{28,12},{1,17},{... | collective-permute-start | bytes 983048 | tf_op jit(solution)/shard_map/ppermute | solution.py:30
  33.0 1.5 collective-permute-start.1
  34.6 14.7 %collective-permute-done.3 = f32[1,320,256]{2,1,0:T(8,128)S(1)} collective-permute-done((f32[1,320,256]{2,1,0:T(8,128)S(1)}, f32[1,320,256]{2,1,0:T(8,128)S(1)}, u32[]{:S(2)}, u32[]{:S(2)}) %collective-permute-start.3) | collective-permute-done | bytes 327712 | tf_op jit(solution)/shard_map/ppermute | solution.py:30
  49.4 1.2 collective-permute-start.4
  50.7 1.9 %collective-permute-start.2 = (f32[1,160,256]{2,1,0:T(8,128)S(1)}, f32[1,160,256]{2,1,0:T(8,128)S(1)}, u32[]{:S(2)}, u32[]{:S(2)}) collective-permute-start(f32[1,160,256]{2,1,0:T(8,128)S(1)} %constant_dynamic-slice_fusion.5), channel_id=1, source_target_pairs={{0,16},{4,20},{8,24},{12,28},{16,0},{20,4},{24,8},{28,12},{1,17},{... | collective-permute-start | bytes 491528 | tf_op jit(solution)/shard_map/ppermute | solution.py:30
  52.5 4.2 %collective-permute-done.4 = f32[1,160,256]{2,1,0:T(8,128)S(1)} collective-permute-done((f32[1,160,256]{2,1,0:T(8,128)S(1)}, f32[1,160,256]{2,1,0:T(8,128)S(1)}, u32[]{:S(2)}, u32[]{:S(2)}) %collective-permute-start.4) | collective-permute-done | bytes 163872 | tf_op jit(solution)/shard_map/ppermute | solution.py:30
  56.7 2.3 %collective-permute-done.2 = f32[1,160,256]{2,1,0:T(8,128)S(1)} collective-permute-done((f32[1,160,256]{2,1,0:T(8,128)S(1)}, f32[1,160,256]{2,1,0:T(8,128)S(1)}, u32[]{:S(2)}, u32[]{:S(2)}) %collective-permute-start.2) | collective-permute-done | bytes 163872 | tf_op jit(solution)/shard_map/ppermute | solution.py:30
  59.1 1.4 collective-permute-start.5
  60.4 7.6 %collective-permute-done.5 = f32[2,80,256]{2,1,0:T(8,128)S(1)} collective-permute-done((f32[2,80,256]{2,1,0:T(8,128)S(1)}, f32[2,80,256]{2,1,0:T(8,128)S(1)}, u32[]{:S(2)}, u32[]{:S(2)}) %collective-permute-start.5) | collective-permute-done | bytes 163872 | tf_op jit(solution)/shard_map/ppermute | solution.py:30
  68.1 1.5 all-to-all-done.1
  69.6 3.5 %multiply_reduce_fusion = (f32[512]{0:T(512)S(1)}, f32[512]{0:T(512)S(1)}, bf16[512,1024]{1,0:T(8,128)(2,1)S(1)}, bf16[512,1024]{1,0:T(8,128)(2,1)S(1)}) fusion(bf16[512,1024]{1,0:T(8,128)(2,1)S(1)} %copy-done.5, f32[512]{0:T(512)S(1)} %copy-done.6, f32[512]{0:T(512)S(1)} %divide_sqrt_fusion, bf16[512,1024]{1,0:T(8,128)(2,1)} %places.1, ...), kind=kOutput, calls=%fused_computation.17 | convolution fusion | flops 1078983680 | bytes 6299648 | tf_op jit(solution)/shard_map/dot_general | solution.py:309
  74.1 2.2 %fusion.23 = f32[512,1024]{1,0:T(8,128)} fusion(bf16[512,1024]{1,0:T(8,128)(2,1)S(1)} %get-tuple-element.20, s32[]{:T(128)S(6)} %select_n.359, bf16[512,1024]{1,0:T(8,128)(2,1)S(1)} %get-tuple-element.60, f32[512]{0:T(512)S(1)} %broadcast_multiply_fusion.2, f32[512]{0:T(512)S(1)} %divide_sqrt_fusion), kind=kOutput, calls=%fused_computation.53 | convolution fusion | flops 538968064 | bytes 3674116 | tf_op jit(solution)/shard_map/dot_general | solution.py:324
  77.3 2.1 %fusion.21 = f32[512,1024]{1,0:T(8,128)S(1)} fusion(bf16[512,1024]{1,0:T(8,128)(2,1)S(1)} %get-tuple-element.20, s32[]{:T(128)S(6)} %select_n.360, bf16[512,1024]{1,0:T(8,128)(2,1)} %copy-done.7, f32[512]{0:T(512)S(1)} %broadcast_multiply_fusion.2, f32[512]{0:T(512)S(1)} %divide_sqrt_fusion), kind=kOutput, calls=%fused_computation.51 | convolution fusion | flops 538968064 | bytes 3674116 | tf_op jit(solution)/shard_map/dot_general | solution.py:324
  79.6 1.8 %collective-permute-done.7 = f32[2,256,1024]{2,1,0:T(8,128)} collective-permute-done((f32[2,256,1024]{2,1,0:T(8,128)}, f32[2,256,1024]{2,1,0:T(8,128)}, u32[]{:S(2)}, u32[]{:S(2)}) %collective-permute-start.7) | collective-permute-done | bytes 2097184 | tf_op jit(solution)/shard_map/ppermute | solution.py:30
  81.5 1.7 fusion.54
  85.0 2.1 %collective-permute-start.8 = (f32[1,128,1024]{2,1,0:T(8,128)}, f32[1,128,1024]{2,1,0:T(8,128)}, u32[]{:S(2)}, u32[]{:S(2)}) collective-permute-start(f32[1,128,1024]{2,1,0:T(8,128)} %bitcast_add_fusion.2), channel_id=1, source_target_pairs={{0,8},{4,12},{8,0},{12,4},{16,24},{20,28},{24,16},{28,20},{1,9},{5... | collective-permute-start | bytes 1572872 | tf_op jit(solution)/shard_map/ppermute | solution.py:30
  89.4 9.5 %collective-permute-done.6 = f32[2,80,256]{2,1,0:T(8,128)S(1)} collective-permute-done((f32[2,80,256]{2,1,0:T(8,128)S(1)}, f32[2,80,256]{2,1,0:T(8,128)S(1)}, u32[]{:S(2)}, u32[]{:S(2)}) %collective-permute-start.6) | collective-permute-done | bytes 163872 | tf_op jit(solution)/shard_map/ppermute | solution.py:30
  99.9 1.3 fusion.20
  101.2 2.0 %collective-permute-start.9 = (f32[2,80,256]{2,1,0:T(8,128)S(1)}, f32[2,80,256]{2,1,0:T(8,128)S(1)}, u32[]{:S(2)}, u32[]{:S(2)}) collective-permute-start(f32[2,80,256]{2,1,0:T(8,128)S(1)} %add.225), channel_id=1, source_target_pairs={{0,1},{1,0},{2,3},{3,2},{4,5},{5,4},{6,7},{7,6},{8,9},{9,8},{10,11... | collective-permute-start | bytes 491528 | tf_op jit(solution)/shard_map/ppermute | solution.py:30
  103.2 1.2 fusion.19
  104.8 1.5 collective-permute-start.14
  108.2 1.2 collective-permute-start.12
  109.4 4.1 %collective-permute-done.16 = f32[1,64,1024]{2,1,0:T(8,128)S(1)} collective-permute-done((f32[1,64,1024]{2,1,0:T(8,128)S(1)}, f32[1,64,1024]{2,1,0:T(8,128)S(1)}, u32[]{:S(2)}, u32[]{:S(2)}) %collective-permute-start.16) | collective-permute-done | bytes 262176 | tf_op jit(solution)/shard_map/ppermute | solution.py:30
  113.7 1.8 %collective-permute-start.17 = (f32[2,32,1024]{2,1,0:T(8,128)S(1)}, f32[2,32,1024]{2,1,0:T(8,128)S(1)}, u32[]{:S(2)}, u32[]{:S(2)}) collective-permute-start(f32[2,32,1024]{2,1,0:T(8,128)S(1)} %fusion.25), channel_id=1, source_target_pairs={{0,1},{1,0},{2,3},{3,2},{4,5},{5,4},{6,7},{7,6},{8,9},{9,8},{10,11... | collective-permute-start | bytes 786440 | tf_op jit(solution)/shard_map/ppermute | solution.py:30
  115.5 1.6 collective-permute-start.11
  117.8 3.7 %collective-permute-done.17 = f32[2,32,1024]{2,1,0:T(8,128)S(1)} collective-permute-done((f32[2,32,1024]{2,1,0:T(8,128)S(1)}, f32[2,32,1024]{2,1,0:T(8,128)S(1)}, u32[]{:S(2)}, u32[]{:S(2)}) %collective-permute-start.17) | collective-permute-done | bytes 262176 | tf_op jit(solution)/shard_map/ppermute | solution.py:30
  121.7 1.3 collective-permute-done.11
  123.1 1.4 collective-permute-done.13
  124.6 4.3 %collective-permute-done.18 = f32[2,16,1024]{2,1,0:T(8,128)S(1)} collective-permute-done((f32[2,16,1024]{2,1,0:T(8,128)S(1)}, f32[2,16,1024]{2,1,0:T(8,128)S(1)}, u32[]{:S(2)}, u32[]{:S(2)}) %collective-permute-start.18) | collective-permute-done | bytes 131104 | tf_op jit(solution)/shard_map/ppermute | solution.py:30
  129.0 3.0 %collective-permute-done.19.far_ref = f32[2,640,256]{2,1,0:T(8,128)S(1)} collective-permute-done((f32[2,640,256]{2,1,0:T(8,128)S(1)}, f32[2,640,256]{2,1,0:T(8,128)S(1)}, u32[]{:S(2)}, u32[]{:S(2)}) %collective-permute-start.19) | collective-permute-done | bytes 1310752 | tf_op jit(solution)/shard_map/ppermute | solution.py:30
  132.0 10.6 %member_solve.1 = bf16[32,1024]{1,0:T(8,128)(2,1)S(1)} custom-call(s32[1]{0:T(128)} %bitcast.bit_ref, f32[2,640,256]{2,1,0:T(8,128)S(1)} %maximum_maximum_fusion.near_ref, f32[2,640,256]{2,1,0:T(8,128)S(1)} %collective-permute-done.19.far_ref, f32[32,1024]{1,0:T(8,128)S(1)} %bitcast.59), custom_call_target="tpu_custom_call" | custom-call | flops 1610612736 | bytes 6291456 | tf_op jit(solution)/shard_map/member_solve/pallas_call | solution.py:223
  144.2 2.9 %collective-permute-start.22 = (bf16[2,16,1024]{2,1,0:T(8,128)(2,1)S(1)}, bf16[2,16,1024]{2,1,0:T(8,128)(2,1)S(1)}, u32[]{:S(2)}, u32[]{:S(2)}) collective-permute-start(bf16[2,16,1024]{2,1,0:T(8,128)(2,1)S(1)} %bitcast.62), channel_id=1, source_target_pairs={{0,3},{1,2},{2,1},{3,0},{4,7},{5,6},{6,5},{7,4},{8,11},{9,10},{10,... | collective-permute-start | bytes 196616 | tf_op jit(solution)/shard_map/ppermute | solution.py:58
  147.7 3.7 %collective-permute-done.21 = bf16[2,16,1024]{2,1,0:T(8,128)(2,1)S(1)} collective-permute-done((bf16[2,16,1024]{2,1,0:T(8,128)(2,1)S(1)}, bf16[2,16,1024]{2,1,0:T(8,128)(2,1)S(1)}, u32[]{:S(2)}, u32[]{:S(2)}) %collective-permute-start.21) | collective-permute-done | bytes 65568 | tf_op jit(solution)/shard_map/ppermute | solution.py:58
  151.5 1.2 collective-permute-start.23
  153.7 2.8 %collective-permute-done.23 = bf16[1,64,1024]{2,1,0:T(8,128)(2,1)S(1)} collective-permute-done((bf16[1,64,1024]{2,1,0:T(8,128)(2,1)S(1)}, bf16[1,64,1024]{2,1,0:T(8,128)(2,1)S(1)}, u32[]{:S(2)}, u32[]{:S(2)}) %collective-permute-start.23) | collective-permute-done | bytes 131104 | tf_op jit(solution)/shard_map/ppermute | solution.py:30
  156.5 2.0 %collective-permute-done.25 = bf16[1,64,1024]{2,1,0:T(8,128)(2,1)S(1)} collective-permute-done((bf16[1,64,1024]{2,1,0:T(8,128)(2,1)S(1)}, bf16[1,64,1024]{2,1,0:T(8,128)(2,1)S(1)}, u32[]{:S(2)}, u32[]{:S(2)}) %collective-permute-start.25) | collective-permute-done | bytes 131104 | tf_op jit(solution)/shard_map/ppermute | solution.py:30
  161.2 3.9 %collective-permute-done.24 = bf16[1,128,1024]{2,1,0:T(8,128)(2,1)S(1)} collective-permute-done((bf16[1,128,1024]{2,1,0:T(8,128)(2,1)S(1)}, bf16[1,128,1024]{2,1,0:T(8,128)(2,1)S(1)}, u32[]{:S(2)}, u32[]{:S(2)}) %collective-permute-start.24) | collective-permute-done | bytes 262176 | tf_op jit(solution)/shard_map/ppermute | solution.py:30
  167.4 2.7 %fusion.1 = bf16[2048,1024]{1,0:T(8,128)(2,1)S(1)} fusion(bf16[2048,1024]{1,0:T(8,128)(2,1)S(1)} %broadcast_in_dim.18, s32[]{:T(128)S(6)} %select_n.360, bf16[512,1024]{1,0:T(8,128)(2,1)S(1)} %bitcast.67, bf16[2048,1024]{1,0:T(8,128)(2,1)S(1)} %copy-done, f32[2048]{0:T(1024)S(1)} %broadcast_multiply_fusion), kind=kOutput, calls=%fused_computation.8 | convolution fusion | flops 2156920832 | bytes 9445380 | tf_op jit(solution)/shard_map/dot_general | solution.py:357
  170.1 2.7 %fusion.2 = bf16[2048,1024]{1,0:T(8,128)(2,1)S(1)} fusion(bf16[2048,1024]{1,0:T(8,128)(2,1)S(1)} %fusion.1, s32[]{:T(128)S(6)} %select_n.359, bf16[512,1024]{1,0:T(8,128)(2,1)S(1)} %collective-permute-done.27, bf16[2048,1024]{1,0:T(8,128)(2,1)S(1)} %copy-done, f32[2048]{0:T(1024)S(1)} %broadcast_multiply_fusion), kind=kOutput, calls=%fused_computation.9 | convolution fusion | flops 2156920832 | bytes 9445380 | tf_op jit(solution)/shard_map/dot_general | solution.py:357
  172.8 2.0 %copy-done.1 = bf16[2048,1024]{1,0:T(8,128)(2,1)} copy-done((bf16[2048,1024]{1,0:T(8,128)(2,1)}, bf16[2048,1024]{1,0:T(8,128)(2,1)S(1)}, u32[]{:S(2)}) %copy-start.1) | copy-done | bytes 4194328
  (109 shorter events, 26.2 us)
Async XLA Ops:
  2.8 15.7 %all-to-all-start = ((f32[32,2,512]{2,1,0:T(2,128)}), f32[32,2,512]{2,1,0:T(2,128)S(1)}, u32[]{:S(2)}, u32[]{:S(2)}) async-start(f32[32,2,512]{2,1,0:T(2,128)} %broadcast_in_dim.19), calls=%async_computation | async-start | bytes 262144 | tf_op jit(solution)/shard_map/all_to_all | solution.py:283
  18.5 4.4 %copy-start.2 = (bf16[512,1024]{1,0:T(8,128)(2,1)S(1)}, bf16[512,1024]{1,0:T(8,128)(2,1)}, u32[]{:S(2)}) copy-start(bf16[512,1024]{1,0:T(8,128)(2,1)} %param.6) | copy-start | bytes 3145732
  18.5 51.1 %all-to-all-start.1 = ((bf16[32,32,1024]{2,1,0:T(8,128)(2,1)}), bf16[32,32,1024]{2,1,0:T(8,128)(2,1)}, u32[]{:S(2)}, u32[]{:S(2)}) async-start(bf16[32,32,1024]{2,1,0:T(8,128)(2,1)} %bitcast.5), calls=%async_computation.1 | async-start | bytes 4194304 | tf_op jit(solution)/shard_map/all_to_all | solution.py:280
  26.1 3.5 %collective-permute-start = (f32[2,640,256]{2,1,0:T(8,128)}, f32[2,640,256]{2,1,0:T(8,128)}, u32[]{:S(2)}, u32[]{:S(2)}) collective-permute-start(f32[2,640,256]{2,1,0:T(8,128)} %constant_dynamic-slice_fusion.7), channel_id=1, source_target_pairs={{0,4},{4,0},{8,12},{12,8},{16,20},{20,16},{24,28},{28,24},{1,5},{5... | collective-permute-start | bytes 3932168 | tf_op jit(solution)/shard_map/ppermute | solution.py:30
  31.2 18.1 %collective-permute-start.3 = (f32[1,320,256]{2,1,0:T(8,128)S(1)}, f32[1,320,256]{2,1,0:T(8,128)S(1)}, u32[]{:S(2)}, u32[]{:S(2)}) collective-permute-start(f32[1,320,256]{2,1,0:T(8,128)S(1)} %constant_dynamic-slice_fusion.4), channel_id=1, source_target_pairs={{0,16},{4,20},{8,24},{12,28},{16,0},{20,4},{24,8},{28,12},{1,17},{... | collective-permute-start | bytes 983048 | tf_op jit(solution)/shard_map/ppermute | solution.py:30
  33.0 27.4 %copy-start.4 = (f32[512]{0:T(512)S(1)}, f32[512]{0:T(512)}, u32[]{:S(2)}) copy-start(f32[512]{0:T(512)} %param.9) | copy-start | bytes 6148
  33.0 17.6 %collective-permute-start.1 = (f32[1,320,256]{2,1,0:T(8,128)S(1)}, f32[1,320,256]{2,1,0:T(8,128)S(1)}, u32[]{:S(2)}, u32[]{:S(2)}) collective-permute-start(f32[1,320,256]{2,1,0:T(8,128)S(1)} %constant_dynamic-slice_fusion.6), channel_id=1, source_target_pairs={{0,8},{4,12},{8,0},{12,4},{16,24},{20,28},{24,16},{28,20},{1,9},{5... | collective-permute-start | bytes 983048 | tf_op jit(solution)/shard_map/ppermute | solution.py:30
  49.3 20.2 %copy-start.5 = (bf16[512,1024]{1,0:T(8,128)(2,1)S(1)}, bf16[512,1024]{1,0:T(8,128)(2,1)}, u32[]{:S(2)}) copy-start(bf16[512,1024]{1,0:T(8,128)(2,1)} %param.10) | copy-start | bytes 3145732
  49.3 20.2 %copy-start.6 = (f32[512]{0:T(512)S(1)}, f32[512]{0:T(512)}, u32[]{:S(2)}) copy-start(f32[512]{0:T(512)} %param.8) | copy-start | bytes 6148
  49.4 7.3 %collective-permute-start.4 = (f32[1,160,256]{2,1,0:T(8,128)S(1)}, f32[1,160,256]{2,1,0:T(8,128)S(1)}, u32[]{:S(2)}, u32[]{:S(2)}) collective-permute-start(f32[1,160,256]{2,1,0:T(8,128)S(1)} %constant_dynamic-slice_fusion.3), channel_id=1, source_target_pairs={{0,8},{4,12},{8,0},{12,4},{16,24},{20,28},{24,16},{28,20},{1,9},{5... | collective-permute-start | bytes 491528 | tf_op jit(solution)/shard_map/ppermute | solution.py:30
  50.7 8.3 %collective-permute-start.2 = (f32[1,160,256]{2,1,0:T(8,128)S(1)}, f32[1,160,256]{2,1,0:T(8,128)S(1)}, u32[]{:S(2)}, u32[]{:S(2)}) collective-permute-start(f32[1,160,256]{2,1,0:T(8,128)S(1)} %constant_dynamic-slice_fusion.5), channel_id=1, source_target_pairs={{0,16},{4,20},{8,24},{12,28},{16,0},{20,4},{24,8},{28,12},{1,17},{... | collective-permute-start | bytes 491528 | tf_op jit(solution)/shard_map/ppermute | solution.py:30
  59.1 9.0 %collective-permute-start.5 = (f32[2,80,256]{2,1,0:T(8,128)S(1)}, f32[2,80,256]{2,1,0:T(8,128)S(1)}, u32[]{:S(2)}, u32[]{:S(2)}) collective-permute-start(f32[2,80,256]{2,1,0:T(8,128)S(1)} %fusion.35), channel_id=1, source_target_pairs={{0,1},{1,0},{2,3},{3,2},{4,5},{5,4},{6,7},{7,6},{8,9},{9,8},{10,11... | collective-permute-start | bytes 491528 | tf_op jit(solution)/shard_map/ppermute | solution.py:30
  73.1 1.0 copy-start.7
  76.4 5.1 %collective-permute-start.7 = (f32[2,256,1024]{2,1,0:T(8,128)}, f32[2,256,1024]{2,1,0:T(8,128)}, u32[]{:S(2)}, u32[]{:S(2)}) collective-permute-start(f32[2,256,1024]{2,1,0:T(8,128)} %bitcast.7), channel_id=1, source_target_pairs={{0,4},{4,0},{8,12},{12,8},{16,20},{20,16},{24,28},{28,24},{1,5},{5... | collective-permute-start | bytes 6291464 | tf_op jit(solution)/shard_map/ppermute | solution.py:30
  83.1 1.0 copy-start.3
  85.0 14.9 %collective-permute-start.8 = (f32[1,128,1024]{2,1,0:T(8,128)}, f32[1,128,1024]{2,1,0:T(8,128)}, u32[]{:S(2)}, u32[]{:S(2)}) collective-permute-start(f32[1,128,1024]{2,1,0:T(8,128)} %bitcast_add_fusion.2), channel_id=1, source_target_pairs={{0,8},{4,12},{8,0},{12,4},{16,24},{20,28},{24,16},{28,20},{1,9},{5... | collective-permute-start | bytes 1572872 | tf_op jit(solution)/shard_map/ppermute | solution.py:30
  88.0 15.2 %collective-permute-start.15 = (f32[1,128,1024]{2,1,0:T(8,128)}, f32[1,128,1024]{2,1,0:T(8,128)}, u32[]{:S(2)}, u32[]{:S(2)}) collective-permute-start(f32[1,128,1024]{2,1,0:T(8,128)} %bitcast_add_fusion), channel_id=1, source_target_pairs={{0,16},{4,20},{8,24},{12,28},{16,0},{20,4},{24,8},{28,12},{1,17},{... | collective-permute-start | bytes 1572872 | tf_op jit(solution)/shard_map/ppermute | solution.py:30
  88.5 10.3 %collective-permute-start.6 = (f32[2,80,256]{2,1,0:T(8,128)S(1)}, f32[2,80,256]{2,1,0:T(8,128)S(1)}, u32[]{:S(2)}, u32[]{:S(2)}) collective-permute-start(f32[2,80,256]{2,1,0:T(8,128)S(1)} %fusion.37), channel_id=1, source_target_pairs={{0,2},{1,3},{2,0},{3,1},{4,6},{5,7},{6,4},{7,5},{8,10},{9,11},{10,... | collective-permute-start | bytes 491528 | tf_op jit(solution)/shard_map/ppermute | solution.py:30
  101.2 6.0 %collective-permute-start.9 = (f32[2,80,256]{2,1,0:T(8,128)S(1)}, f32[2,80,256]{2,1,0:T(8,128)S(1)}, u32[]{:S(2)}, u32[]{:S(2)}) collective-permute-start(f32[2,80,256]{2,1,0:T(8,128)S(1)} %add.225), channel_id=1, source_target_pairs={{0,1},{1,0},{2,3},{3,2},{4,5},{5,4},{6,7},{7,6},{8,9},{9,8},{10,11... | collective-permute-start | bytes 491528 | tf_op jit(solution)/shard_map/ppermute | solution.py:30
  104.4 9.1 %collective-permute-start.16 = (f32[1,64,1024]{2,1,0:T(8,128)S(1)}, f32[1,64,1024]{2,1,0:T(8,128)S(1)}, u32[]{:S(2)}, u32[]{:S(2)}) collective-permute-start(f32[1,64,1024]{2,1,0:T(8,128)S(1)} %constant_dynamic-slice_fusion.1), channel_id=1, source_target_pairs={{0,8},{4,12},{8,0},{12,4},{16,24},{20,28},{24,16},{28,20},{1,9},{5... | collective-permute-start | bytes 786440 | tf_op jit(solution)/shard_map/ppermute | solution.py:30
  104.8 8.9 %collective-permute-start.14 = (f32[1,64,1024]{2,1,0:T(8,128)S(1)}, f32[1,64,1024]{2,1,0:T(8,128)S(1)}, u32[]{:S(2)}, u32[]{:S(2)}) collective-permute-start(f32[1,64,1024]{2,1,0:T(8,128)S(1)} %constant_dynamic-slice_fusion.2), channel_id=1, source_target_pairs={{0,16},{4,20},{8,24},{12,28},{16,0},{20,4},{24,8},{28,12},{1,17},{... | collective-permute-start | bytes 786440 | tf_op jit(solution)/shard_map/ppermute | solution.py:30
  107.2 8.3 %collective-permute-start.10 = (f32[1,160,256]{2,1,0:T(8,128)S(1)}, f32[1,160,256]{2,1,0:T(8,128)S(1)}, u32[]{:S(2)}, u32[]{:S(2)}) collective-permute-start(f32[1,160,256]{2,1,0:T(8,128)S(1)} %get-tuple-element.41), channel_id=1, source_target_pairs={{0,16},{4,20},{8,24},{12,28},{16,0},{20,4},{24,8},{28,12},{1,17},{... | collective-permute-start | bytes 491528 | tf_op jit(solution)/shard_map/ppermute | solution.py:30
  108.2 9.0 %collective-permute-start.12 = (f32[1,160,256]{2,1,0:T(8,128)S(1)}, f32[1,160,256]{2,1,0:T(8,128)S(1)}, u32[]{:S(2)}, u32[]{:S(2)}) collective-permute-start(f32[1,160,256]{2,1,0:T(8,128)S(1)} %get-tuple-element.42), channel_id=1, source_target_pairs={{0,8},{4,12},{8,0},{12,4},{16,24},{20,28},{24,16},{28,20},{1,9},{5... | collective-permute-start | bytes 491528 | tf_op jit(solution)/shard_map/ppermute | solution.py:30
  113.7 7.8 %collective-permute-start.17 = (f32[2,32,1024]{2,1,0:T(8,128)S(1)}, f32[2,32,1024]{2,1,0:T(8,128)S(1)}, u32[]{:S(2)}, u32[]{:S(2)}) collective-permute-start(f32[2,32,1024]{2,1,0:T(8,128)S(1)} %fusion.25), channel_id=1, source_target_pairs={{0,1},{1,0},{2,3},{3,2},{4,5},{5,4},{6,7},{7,6},{8,9},{9,8},{10,11... | collective-permute-start | bytes 786440 | tf_op jit(solution)/shard_map/ppermute | solution.py:30
  115.5 7.5 %collective-permute-start.11 = (f32[1,320,256]{2,1,0:T(8,128)S(1)}, f32[1,320,256]{2,1,0:T(8,128)S(1)}, u32[]{:S(2)}, u32[]{:S(2)}) collective-permute-start(f32[1,320,256]{2,1,0:T(8,128)S(1)} %pad_maximum_fusion.1), channel_id=1, source_target_pairs={{0,8},{4,12},{8,0},{12,4},{16,24},{20,28},{24,16},{28,20},{1,9},{5... | collective-permute-start | bytes 983048 | tf_op jit(solution)/shard_map/ppermute | solution.py:30
  117.2 7.2 %collective-permute-start.13 = (f32[1,320,256]{2,1,0:T(8,128)S(1)}, f32[1,320,256]{2,1,0:T(8,128)S(1)}, u32[]{:S(2)}, u32[]{:S(2)}) collective-permute-start(f32[1,320,256]{2,1,0:T(8,128)S(1)} %pad_maximum_fusion.2), channel_id=1, source_target_pairs={{0,16},{4,20},{8,24},{12,28},{16,0},{20,4},{24,8},{28,12},{1,17},{... | collective-permute-start | bytes 983048 | tf_op jit(solution)/shard_map/ppermute | solution.py:30
  121.6 7.3 %collective-permute-start.18 = (f32[2,16,1024]{2,1,0:T(8,128)S(1)}, f32[2,16,1024]{2,1,0:T(8,128)S(1)}, u32[]{:S(2)}, u32[]{:S(2)}) collective-permute-start(f32[2,16,1024]{2,1,0:T(8,128)S(1)} %constant_dynamic-slice_fusion), channel_id=1, source_target_pairs={{0,2},{1,3},{2,0},{3,1},{4,6},{5,7},{6,4},{7,5},{8,10},{9,11},{10,... | collective-permute-start | bytes 393224 | tf_op jit(solution)/shard_map/ppermute | solution.py:30
  128.9 3.1 %collective-permute-start.19 = (f32[2,640,256]{2,1,0:T(8,128)S(1)}, f32[2,640,256]{2,1,0:T(8,128)S(1)}, u32[]{:S(2)}, u32[]{:S(2)}) collective-permute-start(f32[2,640,256]{2,1,0:T(8,128)S(1)} %maximum_maximum_fusion.near_ref), channel_id=1, source_target_pairs={{0,4},{4,0},{8,12},{12,8},{16,20},{20,16},{24,28},{28,24},{1,5},{5... | collective-permute-start | bytes 3932168 | tf_op jit(solution)/shard_map/ppermute | solution.py:30
  142.6 5.0 %collective-permute-start.20 = (bf16[2,16,1024]{2,1,0:T(8,128)(2,1)S(1)}, bf16[2,16,1024]{2,1,0:T(8,128)(2,1)S(1)}, u32[]{:S(2)}, u32[]{:S(2)}) collective-permute-start(bf16[2,16,1024]{2,1,0:T(8,128)(2,1)S(1)} %bitcast.60), channel_id=1, source_target_pairs={{0,1},{1,0},{2,3},{3,2},{4,5},{5,4},{6,7},{7,6},{8,9},{9,8},{10,11... | collective-permute-start | bytes 196616 | tf_op jit(solution)/shard_map/ppermute | solution.py:58
  143.1 8.3 %collective-permute-start.21 = (bf16[2,16,1024]{2,1,0:T(8,128)(2,1)S(1)}, bf16[2,16,1024]{2,1,0:T(8,128)(2,1)S(1)}, u32[]{:S(2)}, u32[]{:S(2)}) collective-permute-start(bf16[2,16,1024]{2,1,0:T(8,128)(2,1)S(1)} %bitcast.61), channel_id=1, source_target_pairs={{0,2},{1,3},{2,0},{3,1},{4,6},{5,7},{6,4},{7,5},{8,10},{9,11},{10,... | collective-permute-start | bytes 196616 | tf_op jit(solution)/shard_map/ppermute | solution.py:58
  144.2 7.2 %collective-permute-start.22 = (bf16[2,16,1024]{2,1,0:T(8,128)(2,1)S(1)}, bf16[2,16,1024]{2,1,0:T(8,128)(2,1)S(1)}, u32[]{:S(2)}, u32[]{:S(2)}) collective-permute-start(bf16[2,16,1024]{2,1,0:T(8,128)(2,1)S(1)} %bitcast.62), channel_id=1, source_target_pairs={{0,3},{1,2},{2,1},{3,0},{4,7},{5,6},{6,5},{7,4},{8,11},{9,10},{10,... | collective-permute-start | bytes 196616 | tf_op jit(solution)/shard_map/ppermute | solution.py:58
  151.5 5.0 %collective-permute-start.23 = (bf16[1,64,1024]{2,1,0:T(8,128)(2,1)S(1)}, bf16[1,64,1024]{2,1,0:T(8,128)(2,1)S(1)}, u32[]{:S(2)}, u32[]{:S(2)}) collective-permute-start(bf16[1,64,1024]{2,1,0:T(8,128)(2,1)S(1)} %get-tuple-element.49), channel_id=1, source_target_pairs={{0,16},{4,20},{8,24},{12,28},{16,0},{20,4},{24,8},{28,12},{1,17},{... | collective-permute-start | bytes 393224 | tf_op jit(solution)/shard_map/ppermute | solution.py:30
  152.6 5.9 %collective-permute-start.25 = (bf16[1,64,1024]{2,1,0:T(8,128)(2,1)S(1)}, bf16[1,64,1024]{2,1,0:T(8,128)(2,1)S(1)}, u32[]{:S(2)}, u32[]{:S(2)}) collective-permute-start(bf16[1,64,1024]{2,1,0:T(8,128)(2,1)S(1)} %get-tuple-element.50), channel_id=1, source_target_pairs={{0,8},{4,12},{8,0},{12,4},{16,24},{20,28},{24,16},{28,20},{1,9},{5... | collective-permute-start | bytes 393224 | tf_op jit(solution)/shard_map/ppermute | solution.py:30
  158.6 6.4 %collective-permute-start.24 = (bf16[1,128,1024]{2,1,0:T(8,128)(2,1)S(1)}, bf16[1,128,1024]{2,1,0:T(8,128)(2,1)S(1)}, u32[]{:S(2)}, u32[]{:S(2)}) collective-permute-start(bf16[1,128,1024]{2,1,0:T(8,128)(2,1)S(1)} %pad_maximum_fusion.4), channel_id=1, source_target_pairs={{0,8},{4,12},{8,0},{12,4},{16,24},{20,28},{24,16},{28,20},{1,9},{5... | collective-permute-start | bytes 786440 | tf_op jit(solution)/shard_map/ppermute | solution.py:30
  159.5 6.4 %collective-permute-start.26 = (bf16[1,128,1024]{2,1,0:T(8,128)(2,1)S(1)}, bf16[1,128,1024]{2,1,0:T(8,128)(2,1)S(1)}, u32[]{:S(2)}, u32[]{:S(2)}) collective-permute-start(bf16[1,128,1024]{2,1,0:T(8,128)(2,1)S(1)} %pad_maximum_fusion.5), channel_id=1, source_target_pairs={{0,16},{4,20},{8,24},{12,28},{16,0},{20,4},{24,8},{28,12},{1,17},{... | collective-permute-start | bytes 786440 | tf_op jit(solution)/shard_map/ppermute | solution.py:30
  161.2 5.1 %copy-start = (bf16[2048,1024]{1,0:T(8,128)(2,1)S(1)}, bf16[2048,1024]{1,0:T(8,128)(2,1)}, u32[]{:S(2)}) copy-start(bf16[2048,1024]{1,0:T(8,128)(2,1)} %param.11) | copy-start | bytes 12582916
  166.2 3.9 %collective-permute-start.27 = (bf16[512,1024]{1,0:T(8,128)(2,1)S(1)}, bf16[512,1024]{1,0:T(8,128)(2,1)S(1)}, u32[]{:S(2)}, u32[]{:S(2)}) collective-permute-start(bf16[512,1024]{1,0:T(8,128)(2,1)S(1)} %bitcast.66), channel_id=1, source_target_pairs={{0,4},{4,0},{8,12},{12,8},{16,20},{20,16},{24,28},{28,24},{1,5},{5... | collective-permute-start | bytes 3145736 | tf_op jit(solution)/shard_map/ppermute | solution.py:30
  172.7 2.0 %copy-start.1 = (bf16[2048,1024]{1,0:T(8,128)(2,1)}, bf16[2048,1024]{1,0:T(8,128)(2,1)S(1)}, u32[]{:S(2)}) copy-start(bf16[2048,1024]{1,0:T(8,128)(2,1)S(1)} %fusion.2) | copy-start | bytes 12582916
